TPU v7x, 256 devices: a whole 4x4x8 slice. The times are simulated.
256 devices in a mesh: outer: 32 (over y, z), inner: 8 (over x, core).
Axes of the slice: x: 4, y: 4, z: 8, core: 2. Of those that a mesh axis runs over, the one named last changes fastest.
Arguments:
- embeddings: bfloat16 [32768, 1536], P(('outer', 'inner')), may hold values from -6 to 6
- fine_centroids: bfloat16 [8192, 1536], P('inner'), may hold values from -6 to 6
- coarse_centroids: bfloat16 [1024, 1536], replicated, may hold values from -6 to 6
Outputs:
- new_fine: bfloat16 [8192, 1536], P('inner')
- new_coarse: bfloat16 [1024, 1536], P('inner')
All inputs are finite; a program needn't handle non-finite values.
Results may differ from a plain program's by a relative error of at most 0.007.
Values may be sent and summed in bfloat16 or wider, within the bound.
No kernel may reach another device: no remote copies, remote signals or barrier semaphores. Data moves between devices by JAX's collectives and lax.ppermute only.
A program may use at most 128 MiB of HBM per device.

v0:
```python
import math

import jax
import jax.numpy as jnp
from jax import lax
from jax.sharding import PartitionSpec as P


def center_terms(points, centers, score_scale):
    scores = (
        lax.dot_general(
            points, centers, (((1,), (1,)), ((), ())), preferred_element_type=jnp.float32
        )
        * score_scale
    )
    row_top = jnp.max(scores, axis=1, keepdims=True)
    weights = jnp.exp(scores - row_top)
    weights_bf = (weights / jnp.sum(weights, axis=1, keepdims=True)).astype(jnp.bfloat16)
    weighted = lax.dot_general(
        weights_bf, points, (((0,), (0,)), ((), ())), preferred_element_type=jnp.float32
    )
    total_mass = jnp.sum(weights_bf.astype(jnp.float32), axis=0)
    return (weighted, total_mass)


def shards(embeddings, fine_centroids, coarse_centroids):
    score_scale = 4.0 / math.sqrt(embeddings.shape[1])
    gathered = lax.all_gather(embeddings, "inner", axis=0, tiled=True)
    scores = (
        lax.dot_general(
            gathered, fine_centroids, (((1,), (1,)), ((), ())), preferred_element_type=jnp.float32
        )
        * score_scale
    )
    local_top = jnp.max(scores, axis=1)
    row_top = lax.pmax(local_top, "inner")
    weights = jnp.exp(scores - row_top[:, None])
    row_total = lax.psum(jnp.sum(weights, axis=1), "inner")
    weights_bf = (weights / row_total[:, None]).astype(jnp.bfloat16)
    fine_weighted = lax.dot_general(
        weights_bf, gathered, (((0,), (0,)), ((), ())), preferred_element_type=jnp.float32
    )
    fine_mass = jnp.sum(weights_bf.astype(jnp.float32), axis=0)
    weighted, total_mass = lax.psum((fine_weighted, fine_mass), "outer")
    new_fine = (weighted / jnp.maximum(total_mass, 1.0)[:, None]).astype(jnp.bfloat16)
    coarse_weighted, coarse_mass = center_terms(fine_centroids, coarse_centroids, score_scale)
    coarse_weighted, coarse_mass = (
        lax.psum_scatter(coarse_weighted, "inner", scatter_dimension=0, tiled=True),
        lax.psum_scatter(coarse_mass, "inner", scatter_dimension=0, tiled=True),
    )
    new_coarse = (coarse_weighted / jnp.maximum(coarse_mass, 1.0)[:, None]).astype(jnp.bfloat16)
    return (new_fine, new_coarse)


def solution(mesh):
    placed = (P(("outer", "inner"), None), P("inner", None), P())
    return jax.shard_map(
        shards,
        mesh=mesh,
        in_specs=placed,
        out_specs=(P("inner", None), P("inner", None)),
        check_vma=False,
    )
```

profile of v0, /device:TPU:80, one launch (start us, length us, event | category | flops | bytes accessed | tf_op | source)
XLA Modules:
  0.0 326.0 jit_solution(5142157982962381164)
XLA Ops:
  7.2 0.0 copy-start
  7.2 0.0 all-gather.2.cloned.1.call-start
  7.2 0.7 all-gather.2.cloned.1.call-update
  7.9 0.0 all-reduce.4.cloned.1.call-start
  8.0 1.1 copy-done
  9.1 5.3 %multiply_reduce_fusion = (f32[1024]{0:T(1024)S(1)}, f32[1024,1024]{0,1:T(8,128)S(1)}) fusion(bf16[1024,1536]{1,0:T(8,128)(2,1)S(1)} %copy-done, bf16[1024,1536]{1,0:T(8,128)(2,1)} %param.5), kind=kOutput, calls=%fused_computation.7 | convolution fusion | flops 3223321600 | bytes 10489856 | tf_op jit(solution)/shard_map/dot_general | solution.py:11
  14.4 0.7 fusion.1
  15.1 2.2 convert_reduce_fusion
  17.3 24.9 %all-gather.2.cloned.1.call-done = bf16[1024,1536]{1,0:T(8,128)(2,1)} async-done(((bf16[128,1536]{1,0:T(8,128)(2,1)}), bf16[1024,1536]{1,0:T(8,128)(2,1)}) %all-gather.2.cloned.1.call-update) | async-done | bytes 3145744 | tf_op jit(solution)/shard_map/all_gather | solution.py:28
  42.2 6.8 %multiply_reduce_fusion.1 = (f32[1024]{0:T(1024)S(1)}, f32[1024,1024]{0,1:T(8,128)}) fusion(bf16[1024,1536]{1,0:T(8,128)(2,1)} %all-gather.2.cloned.1.call-done, bf16[1024,1536]{1,0:T(8,128)(2,1)S(1)} %copy-done), kind=kOutput, calls=%fused_computation.8 | convolution fusion | flops 3223321600 | bytes 10489856 | tf_op jit(solution)/shard_map/dot_general | solution.py:30
  49.1 13.8 %pmax.7 = f32[1024]{0:T(1024)S(1)} all-reduce(f32[1024]{0:T(1024)S(1)} %get-tuple-element.8), channel_id=1, replica_groups=mesh['outer'=32,'inner'=8] {'inner'}, use_global_device_ids=true, to_apply=%region_1.0 | all-reduce | flops 1024 | bytes 8192 | tf_op jit(solution)/shard_map/pmax | solution.py:36
  62.9 2.9 fusion
  65.8 12.7 %all-reduce.1 = (f32[1024]{0:T(1024)S(1)}, f32[1024]{0:T(1024)S(1)}) all-reduce(f32[1024]{0:T(1024)S(1)} %fusion, f32[1024]{0:T(1024)S(1)} %get-tuple-element.6), channel_id=1, replica_groups=mesh['outer'=32,'inner'=8] {'inner'}, use_global_device_ids=true, to_apply=%region_3.0 | all-reduce | flops 2048 | bytes 16384 | tf_op jit(solution)/shard_map/psum | solution.py:38
  78.5 0.0 copy-start.1
  78.5 3.3 %convert_reduce_fusion.1 = (f32[1024]{0:T(1024)S(1)}, bf16[1024,1024]{0,1:T(8,128)(2,1)S(1)}) fusion(f32[1024]{0:T(1024)S(1)} %get-tuple-element.2, f32[1024]{0:T(1024)S(1)} %pmax.7, f32[1024,1024]{0,1:T(8,128)} %get-tuple-element.9), kind=kLoop, calls=%fused_computation.4 | loop fusion | flops 6290432 | bytes 6303744 | tf_op jit(solution)/shard_map/reduce_sum | solution.py:43
  81.8 0.0 copy-done.1
  81.8 5.4 %fusion.2 = f32[1024,1536]{1,0:T(8,128)} fusion(bf16[1024,1024]{0,1:T(8,128)(2,1)S(1)} %get-tuple-element.5, bf16[1024,1536]{1,0:T(8,128)(2,1)S(1)} %copy-done.1), kind=kOutput, calls=%fused_computation.14 | convolution fusion | flops 3221225472 | bytes 11534336 | tf_op jit(solution)/shard_map/dot_general | solution.py:40
  87.2 0.0 all-reduce.4.cloned.1.call-update
  87.2 0.0 reduce-scatter.2.cloned.1.call-start
  87.3 6.9 %fusion.3 = f32[1024,1536]{1,0:T(8,128)} fusion(bf16[1024,1024]{0,1:T(8,128)(2,1)} %get-tuple-element.7, bf16[1024,1536]{1,0:T(8,128)(2,1)S(1)} %copy-done), kind=kOutput, calls=%fused_computation.15 | convolution fusion | flops 3221225472 | bytes 11534336 | tf_op jit(solution)/shard_map/dot_general | solution.py:19
  94.2 0.0 copy-start.2
  94.2 0.0 reduce-scatter.2.cloned.1.call-update
  94.2 0.6 copy-done.2
  94.9 0.6 dynamic-slice
  96.1 62.1 %psum.23 = f32[1024]{0:T(1024)S(1)} all-reduce(f32[1024]{0:T(1024)S(1)} %get-tuple-element.4), channel_id=1, replica_groups=mesh['outer'=32,'inner'=8] {'outer'}, use_global_device_ids=true, to_apply=%region_6.0 | all-reduce | flops 1024 | bytes 8192 | tf_op jit(solution)/shard_map/psum | solution.py:44
  158.2 0.1 dynamic-slice_maximum_fusion
  158.3 111.1 %all-reduce.4.cloned.1.call-done = f32[1024,1536]{1,0:T(8,128)} async-done(((f32[1024,1536]{1,0:T(8,128)}), f32[1024,1536]{1,0:T(8,128)}) %all-reduce.4.cloned.1.call-update) | async-done | bytes 6291472 | tf_op jit(solution)/shard_map/psum | solution.py:44
  269.4 5.3 %divide_convert_fusion = bf16[1024,1536]{1,0:T(8,128)(2,1)} fusion(f32[1024,1536]{1,0:T(8,128)} %all-reduce.4.cloned.1.call-done, f32[1024]{0:T(1024)S(1)} %broadcast_maximum_fusion), kind=kLoop, calls=%fused_computation | loop fusion | flops 3145728 | bytes 9441280 | tf_op jit(solution)/shard_map/convert_element_type | solution.py:45
  274.6 42.9 %reduce-scatter.2.cloned.1.call-done = f32[128,1536]{1,0:T(8,128)} async-done(((f32[1024,1536]{1,0:T(8,128)}), f32[128,1536]{1,0:T(8,128)}) %reduce-scatter.2.cloned.1.call-update) | async-done | bytes 786448 | tf_op jit(solution)/shard_map/reduce_scatter | solution.py:48
  317.5 2.0 divide_convert_fusion.3
  (1 shorter events, 0.0 us)
Async XLA Ops:
  7.2 1.9 copy-start
  7.2 35.0 %all-gather.2.cloned.1.call-start = ((), (), s32[]{:S(2)}) async-start(), calls=%async_computation.1 | async-start | bytes 3538944 | tf_op jit(solution)/shard_map/all_gather | solution.py:28
  7.9 261.5 %all-reduce.4.cloned.1.call-start = ((), (), s32[]{:S(2)}) async-start(), calls=%async_computation.2 | async-start | bytes 12582912 | tf_op jit(solution)/shard_map/psum | solution.py:44
  78.5 3.3 %copy-start.1 = (bf16[1024,1536]{1,0:T(8,128)(2,1)S(1)}, bf16[1024,1536]{1,0:T(8,128)(2,1)}, u32[]{:S(2)}) copy-start(bf16[1024,1536]{1,0:T(8,128)(2,1)} %all-gather.2.cloned.1.call-done) | copy-start | bytes 9437188
  87.2 230.3 %reduce-scatter.2.cloned.1.call-start = ((), (), s32[]{:S(2)}) async-start(), calls=%async_computation.3 | async-start | bytes 7077888 | tf_op jit(solution)/shard_map/reduce_scatter | solution.py:48
  94.2 0.7 copy-start.2
Sparse Core Ops, SparseCore 0:
  9.8 32.3 all-gather.1
  87.3 181.9 all-reduce.3
  272.1 45.3 reduce-scatter.1
where the time goes:
time: 328 us; the launch traced here: 326 us
  waiting for transfers between devices  180 us (55%)
  blocking collectives  88.6 us (27%)
  matrix products  24.5 us (7%)
  other arithmetic  16.5 us (5%)
  between operations  14.4 us (4%)
    psum x1, waiting for transfers between devices, shards(): weighted, total_mass = lax.psum((fine_weighted, fine_mass), 'outer')  111 us
    psum x1, blocking collectives, shards(): weighted, total_mass = lax.psum((fine_weighted, fine_mass), 'outer')  62.1 us
    reduce_scatter x1, waiting for transfers between devices, shards(): lax.psum_scatter(coarse_weighted, 'inner', scatter_dimension=0, tiled=True)  42.9 us
    all_gather x1, waiting for transfers between devices, shards(): gathered = lax.all_gather(embeddings, 'inner', axis=0, tiled=True)  24.9 us
    pmax x1, blocking collectives, shards(): row_top = lax.pmax(local_top, 'inner')  13.8 us
    psum x1, blocking collectives, shards(): row_total = lax.psum(jnp.sum(weights, axis=1), 'inner')  12.7 us
    dot_general x1, matrix products, center_terms(): lax.dot_general(weights_bf, points, (((0,), (0,)), ((), ())), preferred_e...  6.9 us
    dot_general x1, matrix products, shards(): lax.dot_general(gathered, fine_centroids, (((1,), (1,)), ((), ())), prefe...  6.83 us
  transfers between devices with their start and end apart: 3, of which 3 were waited for; matrix products, arithmetic and copies ran while one was open for 6% of the time, Pallas kernels for 0%

commit v1 on v0

v1 whole, which is shorter than its diff:
```python
import functools
import math

import jax
import jax.numpy as jnp
import numpy as np
from jax import lax
from jax.experimental import pallas as pl
from jax.experimental.pallas import tpu as pltpu
from jax.sharding import Mesh, PartitionSpec as P

D = 1536
ROWS = 128
BLOCK = 32
TILE = 256
EXTRA = 16
NA = 960 // 128 * 128
NB = D - NA
SCALE = 4.0 / math.sqrt(D)
BF16, F32 = jnp.bfloat16, jnp.float32
ROW_DOT = (((1,), (1,)), ((), ()))

Y_BITS = ((0, 0), (1, 0), (1, 1), (0, 1))
Z_BITS = tuple((g & 1, (g >> 1) & 1, (g >> 2) & 1) for g in (z ^ (z >> 1) for z in range(8)))


def label(y, z, c):
    h, g = Y_BITS[(y - c) % 4], Z_BITS[(z - c) % 8]
    return h[0] << 4 | h[1] << 3 | g[0] << 2 | g[1] << 1 | g[2]


def flip_pairs(bit):
    pairs = []
    for c in range(2):
        where = {label(y, z, c): (y * 8 + z) * 2 + c for y in range(4) for z in range(8)}
        pairs += [(where[k], where[k ^ (1 << bit)]) for k in where]
    return sorted(pairs)


FLIPS = {bit: flip_pairs(bit) for bit in range(5)}


def owner_tables():
    owner = np.zeros((4, 8, 2, 32), np.int32)
    place = np.zeros((4, 8, 2, 32), np.int32)
    for c in range(2):
        block = {label(y, z, c): y * 8 + z for y in range(4) for z in range(8)}
        for y in range(4):
            for z in range(8):
                for p in range(32):
                    b = block[p ^ label(y, z, c)]
                    owner[y, z, c, p] = b
                    place[y, z, c, b] = p
    return np.stack([owner.reshape(64, 32), place.reshape(64, 32)], 1)


TABLES = owner_tables()
COARSE_TABLE = np.array(
    [[(x + r) % 4 * 2 + (c ^ d) for r in range(4) for d in range(2)] for x in range(4) for c in range(2)], np.int32
)


def flip(x, bit):
    return lax.ppermute(x, ("y", "z", "c"), FLIPS[bit])


def from_x(x, k):
    return lax.ppermute(x, "x", [((i + k) % 4, i) for i in range(4)])


def swap_core(x):
    return lax.ppermute(x, "c", [(0, 1), (1, 0)])


def order_kernel(block, table, src, dst, sems):
    copies = []
    for p in range(src.shape[0] // block):
        rows = pl.ds(pl.multiple_of(table[p] * block, block), block)
        copies.append(pltpu.make_async_copy(src.at[rows], dst.at[pl.ds(p * block, block)], sems.at[p]))
        copies[-1].start()
    for copy in copies:
        copy.wait()


def in_order(table, x, block):
    return pl.pallas_call(
        functools.partial(order_kernel, block),
        out_shape=jax.ShapeDtypeStruct(x.shape, x.dtype),
        in_specs=[pl.BlockSpec(memory_space=pltpu.SMEM), pl.BlockSpec(memory_space=pl.ANY)],
        out_specs=pl.BlockSpec(memory_space=pltpu.VMEM),
        scratch_shapes=[pltpu.SemaphoreType.DMA((x.shape[0] // block,))],
        compiler_params=pltpu.CompilerParams(vmem_limit_bytes=8 << 20),
        cost_estimate=pl.CostEstimate(flops=0, bytes_accessed=2 * x.size * 2, transcendentals=0),
        name="order_centroids",
    )(table, x)


def finish_kernel(owner, a_own, a_got, b_own, b_got, out, sems):
    copies = []
    for p in range(32):
        py, pz = p // 8, p % 8
        rows = pl.ds(pl.multiple_of(owner[p] * BLOCK, BLOCK), BLOCK)
        a = a_own if p < 16 else a_got
        b = b_own if pz < 4 else b_got
        from_a = a.at[pl.ds(p % 16 * BLOCK, BLOCK)]
        from_b = b.at[pl.ds((py * 4 + pz % 4) * BLOCK, BLOCK)]
        copies.append(pltpu.make_async_copy(from_a, out.at[rows, pl.ds(0, NA)], sems.at[0, p]))
        copies.append(pltpu.make_async_copy(from_b, out.at[rows, pl.ds(NA, NB)], sems.at[1, p]))
        copies[-2].start()
        copies[-1].start()
    for copy in copies:
        copy.wait()


def finish(owner, a_own, a_got, b_own, b_got):
    return pl.pallas_call(
        finish_kernel,
        out_shape=jax.ShapeDtypeStruct((1024, D), BF16),
        in_specs=[pl.BlockSpec(memory_space=pltpu.SMEM)] + [pl.BlockSpec(memory_space=pl.ANY)] * 4,
        out_specs=pl.BlockSpec(memory_space=pltpu.VMEM),
        scratch_shapes=[pltpu.SemaphoreType.DMA((2, 32))],
        compiler_params=pltpu.CompilerParams(vmem_limit_bytes=8 << 20),
        cost_estimate=pl.CostEstimate(flops=0, bytes_accessed=4 * 1024 * D, transcendentals=0),
        name="finish_fine",
    )(owner, a_own, a_got, b_own, b_got)


def score_kernel(e0, e1, f, p_ref, top_ref, stat_ref, top_acc, sum_acc):
    t = pl.program_id(0)
    rows = jnp.concatenate([e0[...], e1[...]], axis=0)
    s = lax.dot_general(f[...], rows, ROW_DOT, preferred_element_type=F32)
    top = jnp.max(s, axis=0, keepdims=True)
    p = jnp.exp((s - top) * SCALE)
    p_ref[...] = p
    total = jnp.sum(p, axis=0, keepdims=True)
    top_ref[pl.ds(t, 1), :] = top

    @pl.when(t == 0)
    def _():
        top_acc[...] = top
        sum_acc[...] = total

    @pl.when(t > 0)
    def _():
        old = top_acc[...]
        new = jnp.maximum(old, top)
        sum_acc[...] = sum_acc[...] * jnp.exp((old - new) * SCALE) + total * jnp.exp((top - new) * SCALE)
        top_acc[...] = new

    @pl.when(t == 3)
    def _():
        m, l = top_acc[...], sum_acc[...]
        stat_ref[...] = jnp.concatenate([m[:, :ROWS], m[:, ROWS:], l[:, :ROWS], l[:, ROWS:]], axis=0)


def scores(e0, e1, f):
    whole = lambda *shape: pl.BlockSpec(shape, lambda t: (0,) * len(shape))
    return pl.pallas_call(
        score_kernel,
        grid=(4,),
        in_specs=[whole(ROWS, D), whole(ROWS, D), pl.BlockSpec((TILE, D), lambda t: (t, 0))],
        out_specs=[pl.BlockSpec((TILE, 2 * ROWS), lambda t: (t, 0)), whole(4, 2 * ROWS), whole(4, ROWS)],
        out_shape=[
            jax.ShapeDtypeStruct((1024, 2 * ROWS), F32),
            jax.ShapeDtypeStruct((4, 2 * ROWS), F32),
            jax.ShapeDtypeStruct((4, ROWS), F32),
        ],
        scratch_shapes=[pltpu.VMEM((1, 2 * ROWS), F32), pltpu.VMEM((1, 2 * ROWS), F32)],
        compiler_params=pltpu.CompilerParams(vmem_limit_bytes=16 << 20),
        cost_estimate=pl.CostEstimate(flops=2 * 1024 * 256 * D, bytes_accessed=6 << 20, transcendentals=1 << 18),
        name="fine_scores",
    )(e0, e1, f)


def two_rows(v):
    high = v.astype(BF16)
    low = (v - high.astype(F32)).astype(BF16)
    return jnp.concatenate([high, low, jnp.zeros((EXTRA - 2, v.shape[1]), BF16)], axis=0)


def sums_kernel(place, *refs):
    es, ps, tops, stats = refs[0:8], refs[8:12], refs[12:16], refs[16]
    a_send, a_keep, b_send, b_keep, m_keep, all_top, all_sum = refs[17:]
    t = pl.program_id(0)
    tile = lax.rem(t + 2, 4)

    @pl.when(t == 0)
    def _():
        x, c = place[0], place[1]
        for r in range(4):
            for d in range(2):
                ms, ls = [], []
                for src in range(8):
                    sr = lax.rem(x + (r + 4 - src // 2), 4)
                    sd = jnp.bitwise_xor(c, d ^ (src % 2))
                    at = sr * 4 + sd
                    ms.append(stats[src, pl.ds(at, 1), :])
                    ls.append(stats[src, pl.ds(at + 2, 1), :])
                top = ms[0]
                for m in ms[1:]:
                    top = jnp.maximum(top, m)
                total = jnp.zeros_like(top)
                for m, l in zip(ms, ls):
                    total = total + l * jnp.exp((m - top) * SCALE)
                all_top[pl.ds(r, 1), pl.ds(d * ROWS, ROWS)] = top
                all_sum[pl.ds(r, 1), pl.ds(d * ROWS, ROWS)] = total

    ones = jnp.ones((8, 2 * ROWS), BF16)
    out = jnp.zeros((TILE, D), F32)
    weight = jnp.zeros((8, TILE), F32)
    for r in range(4):
        top, total = all_top[pl.ds(r, 1), :], all_sum[pl.ds(r, 1), :]
        factor = jnp.exp((tops[r][pl.ds(tile, 1), :] - top) * SCALE) / total
        w = (ps[r][...] * factor).astype(BF16)
        rows = jnp.concatenate([es[2 * r][...], es[2 * r + 1][...]], axis=0)
        out = out + jnp.dot(w, rows, preferred_element_type=F32)
        weight = weight + lax.dot_general(ones, w, ROW_DOT, preferred_element_type=F32)
    weight = weight[:1, :]

    for i in range(2):

        @pl.when(t == i)
        def _():
            a_send[i * TILE : (i + 1) * TILE, :] = out[:, :NA].astype(BF16)
            a_send[512:, i * TILE : (i + 1) * TILE] = two_rows(weight)

        @pl.when(t == 2 + i)
        def _():
            m_keep[:, i * TILE : (i + 1) * TILE] = weight

    @pl.when(t == 0)
    def _():
        a_send[512:, 512:] = jnp.zeros((EXTRA, NA - 512), BF16)

    @pl.when(t >= 2)
    def _():
        a_keep[...] = out[:, :NA]

    b_keep[...] = out[: TILE // 2, NA:]
    b_send[...] = out[TILE // 2 :, NA:].astype(BF16)


def sums(place, es, ps, tops, stats):
    whole = lambda *shape: pl.BlockSpec(shape, lambda t, s: (0,) * len(shape))
    tile = lambda t: lax.rem(t + 2, 4)
    return pl.pallas_call(
        sums_kernel,
        grid_spec=pltpu.PrefetchScalarGridSpec(
            num_scalar_prefetch=1,
            grid=(4,),
            in_specs=[whole(ROWS, D)] * 8
            + [pl.BlockSpec((TILE, 2 * ROWS), lambda t, s: (tile(t), 0))] * 4
            + [whole(4, 2 * ROWS)] * 4
            + [whole(8, 16, ROWS)],
            out_specs=[
                whole(512 + EXTRA, NA),
                pl.BlockSpec((TILE, NA), lambda t, s: (jnp.maximum(t - 2, 0), 0)),
                pl.BlockSpec((TILE // 2, NB), lambda t, s: (tile(t), 0)),
                pl.BlockSpec((TILE // 2, NB), lambda t, s: (tile(t), 0)),
                whole(1, 512),
            ],
            scratch_shapes=[pltpu.VMEM((4, 2 * ROWS), F32), pltpu.VMEM((4, 2 * ROWS), F32)],
        ),
        out_shape=[
            jax.ShapeDtypeStruct((512 + EXTRA, NA), BF16),
            jax.ShapeDtypeStruct((512, NA), F32),
            jax.ShapeDtypeStruct((512, NB), BF16),
            jax.ShapeDtypeStruct((512, NB), F32),
            jax.ShapeDtypeStruct((1, 512), F32),
        ],
        compiler_params=pltpu.CompilerParams(vmem_limit_bytes=24 << 20),
        cost_estimate=pl.CostEstimate(flops=2 * 1024 * 1024 * D, bytes_accessed=14 << 20, transcendentals=0),
        name="fine_sums",
    )(place, *es, *ps, *tops, stats)


def coarse_kernel(s, top, total, fine, keep, send, m_keep):
    w = (jnp.exp(s[...] - top[...]) / total[...]).astype(BF16)
    out = jnp.dot(w, fine[...], preferred_element_type=F32)
    weight = lax.dot_general(jnp.ones((8, 1024), BF16), w, ROW_DOT, preferred_element_type=F32)[:1, :]
    keep[0] = out[:128]
    send[0, :128] = out[128:].astype(BF16)
    send[0, 128:, :128] = two_rows(weight[:, 128:])
    send[0, 128:, 128:] = jnp.zeros((EXTRA, D - 128), BF16)
    m_keep[0] = weight[:, :128]


def coarse_sums(s, top, total, fine):
    whole = lambda *shape: pl.BlockSpec(shape, lambda r: (0,) * len(shape))
    row = lambda *shape: pl.BlockSpec((1, *shape), lambda r: (r, 0, 0))
    return pl.pallas_call(
        coarse_kernel,
        grid=(4,),
        in_specs=[pl.BlockSpec((256, 1024), lambda r: (r, 0)), whole(1, 1024), whole(1, 1024), whole(1024, D)],
        out_specs=[row(128, D), row(128 + EXTRA, D), row(1, 128)],
        out_shape=[
            jax.ShapeDtypeStruct((4, 128, D), F32),
            jax.ShapeDtypeStruct((4, 128 + EXTRA, D), BF16),
            jax.ShapeDtypeStruct((4, 1, 128), F32),
        ],
        compiler_params=pltpu.CompilerParams(vmem_limit_bytes=24 << 20),
        cost_estimate=pl.CostEstimate(flops=2 * 1024 * 1024 * D, bytes_accessed=12 << 20, transcendentals=1 << 20),
        name="coarse_sums",
    )(s, top, total, fine)


def split(v):
    high = lax.reduce_precision(v, 8, 7)
    return high, lax.reduce_precision(v - high, 8, 7)


def with_mass(total, mass):
    high, low = split(mass)
    rows = jnp.pad(jnp.stack([high, low]), ((0, EXTRA - 2), (0, total.shape[1] - mass.shape[0])))
    return jnp.concatenate([total, rows], axis=0).astype(BF16)


def coarse_scores(fine, ordered):
    s = lax.dot_general(ordered, fine, ROW_DOT, preferred_element_type=F32) * SCALE
    top = jnp.max(s, axis=0, keepdims=True)
    return s, top, jnp.sum(jnp.exp(s - top), axis=0, keepdims=True)


def coarse_rows(keep, send, m_keep):
    got = swap_core(send).astype(F32)
    total = keep + got[:, :128]
    mass = m_keep[:, 0] + got[:, 128, :128] + got[:, 129, :128]
    out, m = total[0], mass[0]
    for k in (1, 3, 2):
        block = lax.ppermute(with_mass(total[k], mass[k]), "x", [(i, (i + k) % 4) for i in range(4)]).astype(F32)
        out = out + block[:128]
        m = m + block[128, :128] + block[129, :128]
    return (out / jnp.maximum(m, 1.0)[:, None]).astype(BF16)


def shards(embeddings, fine, coarse):
    y, z, x, c = (lax.axis_index(a) for a in ("y", "z", "x", "c"))
    o = y * 8 + z
    tables = lax.dynamic_index_in_dim(jnp.asarray(TABLES), o * 2 + c, 0, keepdims=False)
    owner = tables[0]
    coarse_order = lax.dynamic_index_in_dim(jnp.asarray(COARSE_TABLE), x * 2 + c, 0, keepdims=False)

    got = {0: embeddings}
    for r in (1, 3, 2):
        got[r] = from_x(embeddings, r)
    pairs = {r: (got[r], swap_core(got[r])) for r in (0, 1, 3, 2)}
    ordered = in_order(owner, fine, BLOCK)
    c_scores = coarse_scores(fine, in_order(coarse_order, coarse, 128))
    ps, tops, stats = {}, {}, {}
    for r in (0, 1, 3, 2):
        ps[r], tops[r], stats[r] = scores(*pairs[r], ordered)
    stats = jnp.concatenate([stats[r] for r in range(4)], axis=0)
    stats = lax.all_to_all(jnp.broadcast_to(stats[None], (8, 16, ROWS)), ("x", "c"), 0, 0)
    es = [block for r in range(4) for block in pairs[r]]
    a_send, a_keep, b_send, b_keep, m_keep = sums(
        jnp.stack([x, c]), es, [ps[r] for r in range(4)], [tops[r] for r in range(4)], stats
    )
    c_scores, a_keep, b_keep = lax.optimization_barrier((c_scores, a_keep, b_keep))
    c_sums = coarse_sums(*c_scores, fine)

    rows = 512
    m_keep = m_keep[0]
    for bit in (4, 3, 2, 1, 0):
        got = flip(a_send, bit).astype(F32)
        total = a_keep + got[:rows]
        mass = m_keep + got[rows, :rows] + got[rows + 1, :rows]
        if bit:
            rows //= 2
            a_keep, m_keep = total[:rows], mass[:rows]
            a_send = with_mass(total[rows:], mass[rows:])
    mass = jnp.maximum(mass, 1.0)[:, None]
    a = (total / mass).astype(BF16)
    b_keep, b_send = b_keep.reshape(4, 4, BLOCK, NB), b_send.reshape(4, 4, BLOCK, NB)
    for bit in (2, 1, 0, 4, 3):
        total = b_keep + flip(b_send, bit).astype(F32)
        if bit in (2, 1):
            half = total.shape[1] // 2
            b_keep, b_send = total[:, :half], total[:, half:].astype(BF16)
        elif bit in (0, 4):
            half = total.shape[0] // 2
            b_keep, b_send = total[:half], total[half:].astype(BF16)
    b = (total.reshape(BLOCK, NB) / mass).astype(BF16)

    for bit in (0, 1, 2, 3):
        a = jnp.concatenate([a, flip(a, bit)], axis=0)
    a_got = flip(a, 4)
    b = b.reshape(1, 1, BLOCK, NB)
    for bit, axis in ((3, 0), (4, 0), (0, 1), (1, 1)):
        b = jnp.concatenate([b, flip(b, bit)], axis=axis)
    b_got = flip(b, 2)
    new_fine = finish(owner, a, a_got, b.reshape(512, NB), b_got.reshape(512, NB))
    return new_fine, coarse_rows(*c_sums)


def solution(mesh):
    torus = Mesh(mesh.devices.reshape(4, 8, 4, 2), ("y", "z", "x", "c"))
    return jax.shard_map(
        shards,
        mesh=torus,
        in_specs=(P(("y", "z", "x", "c"), None), P(("x", "c"), None), P()),
        out_specs=(P(("x", "c"), None), P(("x", "c"), None)),
        check_vma=False,
    )
```

time: 328 us -> 198 us (0.60)
  waiting for transfers between devices: 180 us -> 81.1 us
  blocking collectives: 88.6 us -> 0 us
  starting transfers between devices: 0.12 us -> 50.3 us
  Pallas kernels: 0 us -> 35.5 us
  matrix products: 24.5 us -> 3.45 us
  local copies, waits for them, and re-layouts: 2.34 us -> 17.9 us
  between operations: 14.4 us -> 1.46 us
  other arithmetic: 16.5 us -> 4.98 us
    psum x1 -> x0, waiting for transfers between devices: 111 us -> none  [shards(): weighted, total_mass = lax.psum((fine_weighted, fine_mass), 'outer')]
    ppermute x0 -> x31, waiting for transfers between devices: none -> 75.6 us  [the longest x20 57.7 us: flip(): return lax.ppermute(x, ('y', 'z', 'c'), FLIPS[bit])]
    psum x2 -> x0, blocking collectives: 74.8 us -> none  [the longest x1 62.1 us: shards(): weighted, total_mass = lax.psum((fine_weighted, fine_mass), 'outer')]
    ppermute x0 -> x31, starting transfers between devices: none -> 46.9 us  [the longest x20 38.6 us: flip(): return lax.ppermute(x, ('y', 'z', 'c'), FLIPS[bit])]
    reduce_scatter x1 -> x0, waiting for transfers between devices: 42.9 us -> none  [shards(): lax.psum_scatter(coarse_weighted, 'inner', scatter_dimension=0, tiled=True)]
    pallas_call x0 -> x9, Pallas kernels: none -> 35.5 us  [the longest x4 12.4 us: scores(): pl.pallas_call(score_kernel, grid=(4,), in_specs=[whole(ROWS, D), whole(R...]
    all_gather x1 -> x0, waiting for transfers between devices: 24.9 us -> none  [shards(): gathered = lax.all_gather(embeddings, 'inner', axis=0, tiled=True)]
    dot_general x4 -> x1, matrix products: 24.5 us -> 3.45 us  [coarse_scores(): lax.dot_general(ordered, fine, ROW_DOT, preferred_element_type=F32) * SCALE]
  transfers between devices with their start and end apart: 3 -> 32, of which waited for: 3 -> 16; matrix products, arithmetic and copies ran while one was open for 6% -> 5% of each run, Pallas kernels for 0% -> 11%
where the time goes in v1:
time: 198 us; the launch traced here: 195 us
  waiting for transfers between devices  81.1 us (41%)
  starting transfers between devices  50.3 us (25%)
  Pallas kernels  35.5 us (18%)
  local copies, waits for them, and re-layouts  17.9 us (9%)
  other arithmetic  4.98 us (3%)
  matrix products  3.45 us (2%)
    ppermute x20, waiting for transfers between devices, flip(): return lax.ppermute(x, ('y', 'z', 'c'), FLIPS[bit])  57.7 us
    ppermute x20, starting transfers between devices, flip(): return lax.ppermute(x, ('y', 'z', 'c'), FLIPS[bit])  38.6 us
    ppermute x3, waiting for transfers between devices, from_x(): return lax.ppermute(x, 'x', [((i + k) % 4, i) for i in range(4)])  17.9 us
    unnamed x35, local copies, waits for them, and re-layouts  15.6 us
    pallas_call x4, Pallas kernels, scores(): pl.pallas_call(score_kernel, grid=(4,), in_specs=[whole(ROWS, D), whole(R...  12.4 us
    pallas_call x1, Pallas kernels, sums(): pl.pallas_call(sums_kernel, grid_spec=pltpu.PrefetchScalarGridSpec(num_sc...  7.52 us
    pallas_call x2, Pallas kernels, in_order(): pl.pallas_call(functools.partial(order_kernel, block), out_shape=jax.Shap...  7.24 us
    all_to_all x1, waiting for transfers between devices, shards(): lax.all_to_all(jnp.broadcast_to(stats[None], (8, 16, ROWS)), ('x', 'c'),...  5.46 us
  transfers between devices with their start and end apart: 32, of which 16 were waited for; matrix products, arithmetic and copies ran while one was open for 5% of the time, Pallas kernels for 11%

profile of v1, /device:TPU:80, one launch (start us, length us, event | category | flops | bytes accessed | tf_op | source)
XLA Modules:
  0.0 194.7 jit_solution(16333987789963589859)
XLA Ops:
  0.6 2.8 %collective-permute-start.1 = (bf16[128,1536]{1,0:T(8,128)(2,1)}, bf16[128,1536]{1,0:T(8,128)(2,1)}, u32[]{:S(2)}, u32[]{:S(2)}) collective-permute-start(bf16[128,1536]{1,0:T(8,128)(2,1)} %refs_0_.1), channel_id=1, source_target_pairs={{2,0},{4,2},{6,4},{0,6},{3,1},{5,3},{7,5},{1,7},{10,8},{12,10},{14... | collective-permute-start | bytes 1179656 | tf_op jit(solution)/shard_map/ppermute | solution.py:68
  3.5 0.8 collective-permute-start.3
  4.3 0.9 collective-permute-start.5
  5.2 0.7 constant_dynamic-slice_fusion
  5.8 14.8 %collective-permute-done.1.e0.refs_2_ = bf16[128,1536]{1,0:T(8,128)(2,1)} collective-permute-done((bf16[128,1536]{1,0:T(8,128)(2,1)}, bf16[128,1536]{1,0:T(8,128)(2,1)}, u32[]{:S(2)}, u32[]{:S(2)}) %collective-permute-start.1) | collective-permute-done | bytes 393248 | tf_op jit(solution)/shard_map/ppermute | solution.py:68
  21.1 3.2 %collective-permute-done.5.e0.refs_6_ = bf16[128,1536]{1,0:T(8,128)(2,1)} collective-permute-done((bf16[128,1536]{1,0:T(8,128)(2,1)}, bf16[128,1536]{1,0:T(8,128)(2,1)}, u32[]{:S(2)}, u32[]{:S(2)}) %collective-permute-start.5) | collective-permute-done | bytes 393248 | tf_op jit(solution)/shard_map/ppermute | solution.py:68
  24.3 1.9 copy-done.1
  26.2 5.1 %order_centroids.3.f = bf16[1024,1536]{1,0:T(8,128)(2,1)S(1)} custom-call(s32[32]{0:T(128)S(1)} %slice_bitcast_fusion.9.table.owner, bf16[1024,1536]{1,0:T(8,128)(2,1)S(1)} %copy-done.1), custom_call_target="tpu_custom_call" | custom-call | bytes 6291456 | tf_op jit(solution)/shard_map/order_centroids/pallas_call | solution.py:86
  31.3 0.7 dynamic-slice_bitcast_fusion.table
  32.0 1.9 copy-done
  33.9 2.2 %order_centroids.2 = bf16[1024,1536]{1,0:T(8,128)(2,1)S(1)} custom-call(s32[8]{0:T(128)S(1)} %dynamic-slice_bitcast_fusion.table, bf16[1024,1536]{1,0:T(8,128)(2,1)S(1)} %copy-done), custom_call_target="tpu_custom_call" | custom-call | bytes 6291456 | tf_op jit(solution)/shard_map/order_centroids/pallas_call | solution.py:86
  36.1 1.7 copy-done.3
  37.7 3.0 %fine_scores.4 = (f32[1024,256]{1,0:T(8,128)S(1)}, f32[4,256]{1,0:T(4,128)S(1)}, f32[4,128]{1,0:T(4,128)S(1)}) custom-call(bf16[128,1536]{1,0:T(8,128)(2,1)S(1)} %copy-done.5, bf16[128,1536]{1,0:T(8,128)(2,1)} %collective-permute-done.e1.refs_1_, bf16[1024,1536]{1,0:T(8,128)(2,1)S(1)} %order_centroids.3.f), custom_call_target="tpu_custom_call" | custom-call | flops 805306368 | bytes 6291456 | tf_op jit(solution)/shard_map/fine_scores/pallas_call | solution.py:158
  40.8 1.0 copy-done.6
  41.8 3.1 %fine_scores.5 = (f32[1024,256]{1,0:T(8,128)S(1)}, f32[4,256]{1,0:T(4,128)S(1)}, f32[4,128]{1,0:T(4,128)S(1)}) custom-call(bf16[128,1536]{1,0:T(8,128)(2,1)} %collective-permute-done.1.e0.refs_2_, bf16[128,1536]{1,0:T(8,128)(2,1)} %collective-permute-done.2.e1.refs_3_, bf16[1024,1536]{1,0:T(8,128)(2,1)S(1)} %order_centroids.3.f), custom_call_target="tpu_custom_call" | custom-call | flops 805306368 | bytes 6291456 | tf_op jit(solution)/shard_map/fine_scores/pallas_call | solution.py:158
  44.9 1.0 copy-done.8
  45.9 3.1 %fine_scores.6 = (f32[1024,256]{1,0:T(8,128)S(1)}, f32[4,256]{1,0:T(4,128)S(1)}, f32[4,128]{1,0:T(4,128)S(1)}) custom-call(bf16[128,1536]{1,0:T(8,128)(2,1)} %collective-permute-done.3.e0.refs_4_, bf16[128,1536]{1,0:T(8,128)(2,1)} %collective-permute-done.4.e1.refs_5_, bf16[1024,1536]{1,0:T(8,128)(2,1)S(1)} %order_centroids.3.f), custom_call_target="tpu_custom_call" | custom-call | flops 805306368 | bytes 6291456 | tf_op jit(solution)/shard_map/fine_scores/pallas_call | solution.py:158
  49.1 1.0 copy-done.10
  50.0 3.1 %fine_scores.7 = (f32[1024,256]{1,0:T(8,128)S(1)}, f32[4,256]{1,0:T(4,128)S(1)}, f32[4,128]{1,0:T(4,128)S(1)}) custom-call(bf16[128,1536]{1,0:T(8,128)(2,1)} %collective-permute-done.5.e0.refs_6_, bf16[128,1536]{1,0:T(8,128)(2,1)} %collective-permute-done.6.e1.refs_7_, bf16[1024,1536]{1,0:T(8,128)(2,1)S(1)} %order_centroids.3.f), custom_call_target="tpu_custom_call" | custom-call | flops 805306368 | bytes 6291456 | tf_op jit(solution)/shard_map/fine_scores/pallas_call | solution.py:158
  53.2 1.0 copy-done.12
  54.2 0.6 copy-done.14
  54.7 0.6 broadcast_in_dim.16
  55.4 3.4 %all-to-all-start = ((f32[8,16,128]{2,1,0:T(8,128)}), f32[8,16,128]{2,1,0:T(8,128)S(1)}, u32[]{:S(2)}, u32[]{:S(2)}) async-start(f32[8,16,128]{2,1,0:T(8,128)} %broadcast_in_dim.16), calls=%async_computation | async-start | bytes 131072 | tf_op jit(solution)/shard_map/all_to_all | solution.py:353
  58.8 5.5 %all-to-all-done.refs_16_ = f32[8,16,128]{2,1,0:T(8,128)S(1)} async-done(((f32[8,16,128]{2,1,0:T(8,128)}), f32[8,16,128]{2,1,0:T(8,128)S(1)}, u32[]{:S(2)}, u32[]{:S(2)}) %all-to-all-start) | async-done | bytes 65568 | tf_op jit(solution)/shard_map/all_to_all | solution.py:353
  64.3 1.2 copy-done.7
  65.5 1.2 copy-done.9
  66.7 1.2 copy-done.11
  67.9 1.2 copy-done.13
  69.2 0.7 copy-done.15
  69.8 7.5 %fine_sums.1 = (bf16[528,896]{1,0:T(8,128)(2,1)S(1)}, f32[512,896]{1,0:T(8,128)S(1)}, bf16[512,640]{1,0:T(8,128)(2,1)S(1)}, f32[512,640]{1,0:T(8,128)S(1)}, f32[1,512]{1,0:T(1,128)S(1)}) custom-call(s32[2]{0:T(128)S(1)} %pad_add_fusion.place, bf16[128,1536]{1,0:T(8,128)(2,1)S(1)} %copy-done.5, bf16[128,1536]{1,0:T(8,128)(2,1)} %collective-permute-done.e1.refs_1_, ...), custom_call_target="tpu_custom_call" | custom-call | flops 3221225472 | bytes 14680064 | tf_op jit(solution)/shard_map/fine_sums/pallas_call | solution.py:246
  77.4 1.4 collective-permute-start.7
  78.7 1.9 collective-permute-start.17
  80.7 3.4 %fusion.72 = (f32[1024]{0:T(1024)S(1)}, f32[1024,1024]{1,0:T(8,128)S(1)}) fusion(bf16[1024,1536]{1,0:T(8,128)(2,1)S(1)} %copy-done.4, bf16[1024,1536]{1,0:T(8,128)(2,1)S(1)} %copy-done.2), kind=kOutput, calls=%fused_computation.167 | convolution fusion | flops 3223321600 | bytes 10489856 | tf_op jit(solution)/shard_map/dot_general | solution.py:319
  84.1 0.6 exponential_reduce_fusion
  84.7 4.6 %collective-permute-done.17 = bf16[4,4,32,640]{3,2,1,0:T(8,128)(2,1)S(1)} collective-permute-done((bf16[4,4,32,640]{3,2,1,0:T(8,128)(2,1)S(1)}, bf16[4,4,32,640]{3,2,1,0:T(8,128)(2,1)S(1)}, u32[]{:S(2)}, u32[]{:S(2)}) %collective-permute-start.17) | collective-permute-done | bytes 655392 | tf_op jit(solution)/shard_map/ppermute | solution.py:64
  89.9 1.3 collective-permute-done.7
  91.7 0.5 collective-permute-start.8
  92.2 10.0 %collective-permute-done.18 = bf16[4,2,32,640]{3,2,1,0:T(8,128)(2,1)S(1)} collective-permute-done((bf16[4,2,32,640]{3,2,1,0:T(8,128)(2,1)S(1)}, bf16[4,2,32,640]{3,2,1,0:T(8,128)(2,1)S(1)}, u32[]{:S(2)}, u32[]{:S(2)}) %collective-permute-start.18) | collective-permute-done | bytes 327712 | tf_op jit(solution)/shard_map/ppermute | solution.py:64
  102.3 8.0 %collective-permute-start.19 = (bf16[4,1,32,640]{3,2,1,0:T(8,128)(2,1)S(1)}, bf16[4,1,32,640]{3,2,1,0:T(8,128)(2,1)S(1)}, u32[]{:S(2)}, u32[]{:S(2)}) collective-permute-start(bf16[4,1,32,640]{3,2,1,0:T(8,128)(2,1)S(1)} %slice.486), channel_id=1, source_target_pairs={{0,56},{1,9},{8,48},{9,1},{16,40},{17,57},{24,32},{25,49},{32,24},... | collective-permute-start | bytes 491528 | tf_op jit(solution)/shard_map/ppermute | solution.py:64
  110.3 4.5 %coarse_sums.1 = (f32[4,128,1536]{2,1,0:T(8,128)S(1)}, bf16[4,144,1536]{2,1,0:T(8,128)(2,1)S(1)}, f32[4,1,128]{2,1,0:T(1,128)S(1)}) custom-call(f32[1024,1024]{1,0:T(8,128)S(1)} %get-tuple-element.46.s, f32[1,1024]{1,0:T(1,128)S(1)} %bitcast.80, f32[1,1024]{1,0:T(1,128)S(1)} %bitcast.81, bf16[1024,1536]{1,0:T(8,128)(2,1)S(1)} %copy-done.2), custom_call_target="tpu_custom_call" | custom-call | flops 3221225472 | bytes 12582912 | tf_op jit(solution)/shard_map/coarse_sums/pallas_call | solution.py:291
  114.9 0.6 collective-permute-start.20
  115.9 3.6 %collective-permute-done.20 = bf16[2,1,32,640]{3,2,1,0:T(8,128)(2,1)S(1)} collective-permute-done((bf16[2,1,32,640]{3,2,1,0:T(8,128)(2,1)S(1)}, bf16[2,1,32,640]{3,2,1,0:T(8,128)(2,1)S(1)}, u32[]{:S(2)}, u32[]{:S(2)}) %collective-permute-start.20) | collective-permute-done | bytes 81952 | tf_op jit(solution)/shard_map/ppermute | solution.py:64
  119.6 2.6 %collective-permute-done.9 = bf16[144,896]{1,0:T(8,128)(2,1)S(1)} collective-permute-done((bf16[144,896]{1,0:T(8,128)(2,1)S(1)}, bf16[144,896]{1,0:T(8,128)(2,1)S(1)}, u32[]{:S(2)}, u32[]{:S(2)}) %collective-permute-start.9) | collective-permute-done | bytes 258080 | tf_op jit(solution)/shard_map/ppermute | solution.py:64
  123.1 0.8 fusion.70
  124.0 1.1 collective-permute-start.30
  125.1 4.1 %collective-permute-done.10 = bf16[80,896]{1,0:T(8,128)(2,1)S(1)} collective-permute-done((bf16[80,896]{1,0:T(8,128)(2,1)S(1)}, bf16[80,896]{1,0:T(8,128)(2,1)S(1)}, u32[]{:S(2)}, u32[]{:S(2)}) %collective-permute-start.10) | collective-permute-done | bytes 143392 | tf_op jit(solution)/shard_map/ppermute | solution.py:64
  129.4 3.8 %collective-permute-start.11 = (bf16[48,896]{1,0:T(8,128)(2,1)S(1)}, bf16[48,896]{1,0:T(8,128)(2,1)S(1)}, u32[]{:S(2)}, u32[]{:S(2)}) collective-permute-start(bf16[48,896]{1,0:T(8,128)(2,1)S(1)} %pad_maximum_fusion.12), channel_id=1, source_target_pairs={{0,56},{1,9},{8,48},{9,1},{16,40},{17,57},{24,32},{25,49},{32,24},... | collective-permute-start | bytes 258056 | tf_op jit(solution)/shard_map/ppermute | solution.py:64
  133.2 1.2 collective-permute-start.29
  134.5 3.0 %collective-permute-done.11 = bf16[48,896]{1,0:T(8,128)(2,1)S(1)} collective-permute-done((bf16[48,896]{1,0:T(8,128)(2,1)S(1)}, bf16[48,896]{1,0:T(8,128)(2,1)S(1)}, u32[]{:S(2)}, u32[]{:S(2)}) %collective-permute-start.11) | collective-permute-done | bytes 86048 | tf_op jit(solution)/shard_map/ppermute | solution.py:64
  137.6 3.3 %collective-permute-start.12 = (bf16[32,896]{1,0:T(8,128)(2,1)S(1)}, bf16[32,896]{1,0:T(8,128)(2,1)S(1)}, u32[]{:S(2)}, u32[]{:S(2)}) collective-permute-start(bf16[32,896]{1,0:T(8,128)(2,1)S(1)} %get-tuple-element.55), channel_id=1, source_target_pairs={{0,56},{1,9},{8,48},{9,1},{16,40},{17,57},{24,32},{25,49},{32,24},... | collective-permute-start | bytes 172040 | tf_op jit(solution)/shard_map/ppermute | solution.py:64
  141.0 4.1 %collective-permute-start.22 = (bf16[1,1,32,640]{3,2,1,0:T(8,128)(2,1)S(1)}, bf16[1,1,32,640]{3,2,1,0:T(8,128)(2,1)S(1)}, u32[]{:S(2)}, u32[]{:S(2)}) collective-permute-start(bf16[1,1,32,640]{3,2,1,0:T(8,128)(2,1)S(1)} %fusion.12), channel_id=1, source_target_pairs={{0,192},{1,65},{8,200},{9,73},{16,208},{17,81},{24,216},{25,89},{3... | collective-permute-start | bytes 122888 | tf_op jit(solution)/shard_map/ppermute | solution.py:64
  145.1 2.7 %collective-permute-start.13 = (bf16[64,896]{1,0:T(8,128)(2,1)S(1)}, bf16[64,896]{1,0:T(8,128)(2,1)S(1)}, u32[]{:S(2)}, u32[]{:S(2)}) collective-permute-start(bf16[64,896]{1,0:T(8,128)(2,1)S(1)} %pad_maximum_fusion.11), channel_id=1, source_target_pairs={{0,24},{1,41},{8,16},{9,33},{16,8},{17,25},{24,0},{25,17},{32,56},... | collective-permute-start | bytes 344072 | tf_op jit(solution)/shard_map/ppermute | solution.py:64
  148.3 3.1 %collective-permute-done.13 = bf16[64,896]{1,0:T(8,128)(2,1)S(1)} collective-permute-done((bf16[64,896]{1,0:T(8,128)(2,1)S(1)}, bf16[64,896]{1,0:T(8,128)(2,1)S(1)}, u32[]{:S(2)}, u32[]{:S(2)}) %collective-permute-start.13) | collective-permute-done | bytes 114720 | tf_op jit(solution)/shard_map/ppermute | solution.py:64
  151.6 0.9 collective-permute-start.28
  152.5 2.8 %collective-permute-start.24 = (bf16[4,1,32,640]{3,2,1,0:T(8,128)(2,1)S(1)}, bf16[4,1,32,640]{3,2,1,0:T(8,128)(2,1)S(1)}, u32[]{:S(2)}, u32[]{:S(2)}) collective-permute-start(bf16[4,1,32,640]{3,2,1,0:T(8,128)(2,1)S(1)} %pad_maximum_fusion.9), channel_id=1, source_target_pairs={{0,56},{1,9},{8,48},{9,1},{16,40},{17,57},{24,32},{25,49},{32,24},... | collective-permute-start | bytes 491528 | tf_op jit(solution)/shard_map/ppermute | solution.py:64
  155.3 2.3 %collective-permute-done.14 = bf16[128,896]{1,0:T(8,128)(2,1)S(1)} collective-permute-done((bf16[128,896]{1,0:T(8,128)(2,1)S(1)}, bf16[128,896]{1,0:T(8,128)(2,1)S(1)}, u32[]{:S(2)}, u32[]{:S(2)}) %collective-permute-start.14) | collective-permute-done | bytes 229408 | tf_op jit(solution)/shard_map/ppermute | solution.py:64
  157.6 3.4 %collective-permute-start.15 = (bf16[256,896]{1,0:T(8,128)(2,1)S(1)}, bf16[256,896]{1,0:T(8,128)(2,1)S(1)}, u32[]{:S(2)}, u32[]{:S(2)}) collective-permute-start(bf16[256,896]{1,0:T(8,128)(2,1)S(1)} %pad_maximum_fusion.2), channel_id=1, source_target_pairs={{0,192},{1,65},{8,200},{9,73},{16,208},{17,81},{24,216},{25,89},{3... | collective-permute-start | bytes 1376264 | tf_op jit(solution)/shard_map/ppermute | solution.py:64
  161.0 2.4 %collective-permute-done.24 = bf16[4,1,32,640]{3,2,1,0:T(8,128)(2,1)S(1)} collective-permute-done((bf16[4,1,32,640]{3,2,1,0:T(8,128)(2,1)S(1)}, bf16[4,1,32,640]{3,2,1,0:T(8,128)(2,1)S(1)}, u32[]{:S(2)}, u32[]{:S(2)}) %collective-permute-start.24) | collective-permute-done | bytes 163872 | tf_op jit(solution)/shard_map/ppermute | solution.py:64
  163.4 4.7 %collective-permute-start.25 = (bf16[4,2,32,640]{3,2,1,0:T(8,128)(2,1)S(1)}, bf16[4,2,32,640]{3,2,1,0:T(8,128)(2,1)S(1)}, u32[]{:S(2)}, u32[]{:S(2)}) collective-permute-start(bf16[4,2,32,640]{3,2,1,0:T(8,128)(2,1)S(1)} %pad_maximum_fusion.6), channel_id=1, source_target_pairs={{0,24},{1,41},{8,16},{9,33},{16,8},{17,25},{24,0},{25,17},{32,56},... | collective-permute-start | bytes 983048 | tf_op jit(solution)/shard_map/ppermute | solution.py:64
  168.5 3.0 %collective-permute-done.15 = bf16[256,896]{1,0:T(8,128)(2,1)S(1)} collective-permute-done((bf16[256,896]{1,0:T(8,128)(2,1)S(1)}, bf16[256,896]{1,0:T(8,128)(2,1)S(1)}, u32[]{:S(2)}, u32[]{:S(2)}) %collective-permute-start.15) | collective-permute-done | bytes 458784 | tf_op jit(solution)/shard_map/ppermute | solution.py:64
  171.6 8.2 %collective-permute-done.25 = bf16[4,2,32,640]{3,2,1,0:T(8,128)(2,1)S(1)} collective-permute-done((bf16[4,2,32,640]{3,2,1,0:T(8,128)(2,1)S(1)}, bf16[4,2,32,640]{3,2,1,0:T(8,128)(2,1)S(1)}, u32[]{:S(2)}, u32[]{:S(2)}) %collective-permute-start.25) | collective-permute-done | bytes 327712 | tf_op jit(solution)/shard_map/ppermute | solution.py:64
  180.1 1.0 fusion.1
  181.1 9.5 %collective-permute-done.26 = bf16[4,4,32,640]{3,2,1,0:T(8,128)(2,1)S(1)} collective-permute-done((bf16[4,4,32,640]{3,2,1,0:T(8,128)(2,1)S(1)}, bf16[4,4,32,640]{3,2,1,0:T(8,128)(2,1)S(1)}, u32[]{:S(2)}, u32[]{:S(2)}) %collective-permute-start.26) | collective-permute-done | bytes 655392 | tf_op jit(solution)/shard_map/ppermute | solution.py:64
  190.7 3.9 %finish_fine.1 = bf16[1024,1536]{1,0:T(8,128)(2,1)} custom-call(s32[32]{0:T(128)S(1)} %slice_bitcast_fusion.9.table.owner, bf16[512,896]{1,0:T(8,128)(2,1)S(1)} %constant_dynamic-update-slice_fusion.a_own, bf16[512,896]{1,0:T(8,128)(2,1)S(1)} %collective-permute-done.16.a_got, bf16[512,640]{1,0:T(8,128)(2,1)S(1)} %bitcast.77, bf16[512,640]{1,0:T(8,128)(2,1)S(1)} %bitcast.79), custom_call_target="tpu_custom_call" | custom-call | bytes 6291456 | tf_op jit(solution)/shard_map/finish_fine/pallas_call | solution.py:116
  (119 shorter events, 5.0 us)
Async XLA Ops:
  0.6 20.0 %collective-permute-start.1 = (bf16[128,1536]{1,0:T(8,128)(2,1)}, bf16[128,1536]{1,0:T(8,128)(2,1)}, u32[]{:S(2)}, u32[]{:S(2)}) collective-permute-start(bf16[128,1536]{1,0:T(8,128)(2,1)} %refs_0_.1), channel_id=1, source_target_pairs={{2,0},{4,2},{6,4},{0,6},{3,1},{5,3},{7,5},{1,7},{10,8},{12,10},{14... | collective-permute-start | bytes 1179656 | tf_op jit(solution)/shard_map/ppermute | solution.py:68
  3.5 17.2 %collective-permute-start.3 = (bf16[128,1536]{1,0:T(8,128)(2,1)}, bf16[128,1536]{1,0:T(8,128)(2,1)}, u32[]{:S(2)}, u32[]{:S(2)}) collective-permute-start(bf16[128,1536]{1,0:T(8,128)(2,1)} %refs_0_.1), channel_id=1, source_target_pairs={{4,0},{6,2},{0,4},{2,6},{5,1},{7,3},{1,5},{3,7},{12,8},{14,10},{8,... | collective-permute-start | bytes 1179656 | tf_op jit(solution)/shard_map/ppermute | solution.py:68
  4.3 20.0 %collective-permute-start.5 = (bf16[128,1536]{1,0:T(8,128)(2,1)}, bf16[128,1536]{1,0:T(8,128)(2,1)}, u32[]{:S(2)}, u32[]{:S(2)}) collective-permute-start(bf16[128,1536]{1,0:T(8,128)(2,1)} %refs_0_.1), channel_id=1, source_target_pairs={{6,0},{0,2},{2,4},{4,6},{7,1},{1,3},{3,5},{5,7},{14,8},{8,10},{10,... | collective-permute-start | bytes 1179656 | tf_op jit(solution)/shard_map/ppermute | solution.py:68
  5.2 32.6 %collective-permute-start = (bf16[128,1536]{1,0:T(8,128)(2,1)}, bf16[128,1536]{1,0:T(8,128)(2,1)}, u32[]{:S(2)}, u32[]{:S(2)}) collective-permute-start(bf16[128,1536]{1,0:T(8,128)(2,1)} %refs_0_.1), channel_id=1, source_target_pairs={{0,1},{1,0},{2,3},{3,2},{4,5},{5,4},{6,7},{7,6},{8,9},{9,8},{10,11... | collective-permute-start | bytes 1179656 | tf_op jit(solution)/shard_map/ppermute | solution.py:72
  20.6 21.2 %collective-permute-start.2 = (bf16[128,1536]{1,0:T(8,128)(2,1)}, bf16[128,1536]{1,0:T(8,128)(2,1)}, u32[]{:S(2)}, u32[]{:S(2)}) collective-permute-start(bf16[128,1536]{1,0:T(8,128)(2,1)} %collective-permute-done.1.e0.refs_2_), channel_id=1, source_target_pairs={{0,1},{1,0},{2,3},{3,2},{4,5},{5,4},{6,7},{7,6},{8,9},{9,8},{10,11... | collective-permute-start | bytes 1179656 | tf_op jit(solution)/shard_map/ppermute | solution.py:72
  20.6 25.3 %collective-permute-start.4 = (bf16[128,1536]{1,0:T(8,128)(2,1)}, bf16[128,1536]{1,0:T(8,128)(2,1)}, u32[]{:S(2)}, u32[]{:S(2)}) collective-permute-start(bf16[128,1536]{1,0:T(8,128)(2,1)} %collective-permute-done.3.e0.refs_4_), channel_id=1, source_target_pairs={{0,1},{1,0},{2,3},{3,2},{4,5},{5,4},{6,7},{7,6},{8,9},{9,8},{10,11... | collective-permute-start | bytes 1179656 | tf_op jit(solution)/shard_map/ppermute | solution.py:72
  24.3 25.7 %collective-permute-start.6 = (bf16[128,1536]{1,0:T(8,128)(2,1)}, bf16[128,1536]{1,0:T(8,128)(2,1)}, u32[]{:S(2)}, u32[]{:S(2)}) collective-permute-start(bf16[128,1536]{1,0:T(8,128)(2,1)} %collective-permute-done.5.e0.refs_6_), channel_id=1, source_target_pairs={{0,1},{1,0},{2,3},{3,2},{4,5},{5,4},{6,7},{7,6},{8,9},{9,8},{10,11... | collective-permute-start | bytes 1179656 | tf_op jit(solution)/shard_map/ppermute | solution.py:72
  24.3 1.9 copy-start.1
  32.0 1.9 copy-start
  33.9 3.8 %copy-start.5 = (bf16[128,1536]{1,0:T(8,128)(2,1)S(1)}, bf16[128,1536]{1,0:T(8,128)(2,1)}, u32[]{:S(2)}) copy-start(bf16[128,1536]{1,0:T(8,128)(2,1)} %refs_0_.1) | copy-start | bytes 1179652
  36.0 1.7 copy-start.3
  40.7 1.0 copy-start.6
  44.9 1.0 copy-start.8
  49.0 1.0 copy-start.10
  53.2 1.0 copy-start.12
  54.1 0.6 copy-start.14
  55.4 8.9 %all-to-all-start = ((f32[8,16,128]{2,1,0:T(8,128)}), f32[8,16,128]{2,1,0:T(8,128)S(1)}, u32[]{:S(2)}, u32[]{:S(2)}) async-start(f32[8,16,128]{2,1,0:T(8,128)} %broadcast_in_dim.16), calls=%async_computation | async-start | bytes 131072 | tf_op jit(solution)/shard_map/all_to_all | solution.py:353
  64.3 1.2 copy-start.7
  65.5 1.2 copy-start.9
  66.7 1.2 copy-start.11
  67.9 1.2 copy-start.13
  69.2 0.7 copy-start.15
  69.8 10.8 %copy-start.2 = (bf16[1024,1536]{1,0:T(8,128)(2,1)S(1)}, bf16[1024,1536]{1,0:T(8,128)(2,1)}, u32[]{:S(2)}) copy-start(bf16[1024,1536]{1,0:T(8,128)(2,1)} %fine.1) | copy-start | bytes 9437188
  69.8 10.8 %copy-start.4 = (bf16[1024,1536]{1,0:T(8,128)(2,1)S(1)}, bf16[1024,1536]{1,0:T(8,128)(2,1)}, u32[]{:S(2)}) copy-start(bf16[1024,1536]{1,0:T(8,128)(2,1)} %copy-done.3) | copy-start | bytes 9437188
  77.4 13.8 %collective-permute-start.7 = (bf16[528,896]{1,0:T(8,128)(2,1)S(1)}, bf16[528,896]{1,0:T(8,128)(2,1)S(1)}, u32[]{:S(2)}, u32[]{:S(2)}) collective-permute-start(bf16[528,896]{1,0:T(8,128)(2,1)S(1)} %get-tuple-element.42), channel_id=1, source_target_pairs={{0,64},{1,193},{8,72},{9,201},{16,80},{17,209},{24,88},{25,217},{3... | collective-permute-start | bytes 2838536 | tf_op jit(solution)/shard_map/ppermute | solution.py:64
  78.7 10.6 %collective-permute-start.17 = (bf16[4,4,32,640]{3,2,1,0:T(8,128)(2,1)S(1)}, bf16[4,4,32,640]{3,2,1,0:T(8,128)(2,1)S(1)}, u32[]{:S(2)}, u32[]{:S(2)}) collective-permute-start(bf16[4,4,32,640]{3,2,1,0:T(8,128)(2,1)S(1)} %bitcast.82), channel_id=1, source_target_pairs={{0,8},{1,57},{8,0},{9,17},{16,24},{17,9},{24,16},{25,33},{32,40},{... | collective-permute-start | bytes 1966088 | tf_op jit(solution)/shard_map/ppermute | solution.py:64
  89.5 12.7 %collective-permute-start.18 = (bf16[4,2,32,640]{3,2,1,0:T(8,128)(2,1)S(1)}, bf16[4,2,32,640]{3,2,1,0:T(8,128)(2,1)S(1)}, u32[]{:S(2)}, u32[]{:S(2)}) collective-permute-start(bf16[4,2,32,640]{3,2,1,0:T(8,128)(2,1)S(1)} %slice.484), channel_id=1, source_target_pairs={{0,24},{1,41},{8,16},{9,33},{16,8},{17,25},{24,0},{25,17},{32,56},... | collective-permute-start | bytes 983048 | tf_op jit(solution)/shard_map/ppermute | solution.py:64
  91.7 23.8 %collective-permute-start.8 = (bf16[272,896]{1,0:T(8,128)(2,1)S(1)}, bf16[272,896]{1,0:T(8,128)(2,1)S(1)}, u32[]{:S(2)}, u32[]{:S(2)}) collective-permute-start(bf16[272,896]{1,0:T(8,128)(2,1)S(1)} %pad_maximum_fusion.1), channel_id=1, source_target_pairs={{0,192},{1,65},{8,200},{9,73},{16,208},{17,81},{24,216},{25,89},{3... | collective-permute-start | bytes 1462280 | tf_op jit(solution)/shard_map/ppermute | solution.py:64
  102.3 12.6 %collective-permute-start.19 = (bf16[4,1,32,640]{3,2,1,0:T(8,128)(2,1)S(1)}, bf16[4,1,32,640]{3,2,1,0:T(8,128)(2,1)S(1)}, u32[]{:S(2)}, u32[]{:S(2)}) collective-permute-start(bf16[4,1,32,640]{3,2,1,0:T(8,128)(2,1)S(1)} %slice.486), channel_id=1, source_target_pairs={{0,56},{1,9},{8,48},{9,1},{16,40},{17,57},{24,32},{25,49},{32,24},... | collective-permute-start | bytes 491528 | tf_op jit(solution)/shard_map/ppermute | solution.py:64
  114.8 7.8 %collective-permute-start.27 = (bf16[4,144,1536]{2,1,0:T(8,128)(2,1)S(1)}, bf16[4,144,1536]{2,1,0:T(8,128)(2,1)S(1)}, u32[]{:S(2)}, u32[]{:S(2)}) collective-permute-start(bf16[4,144,1536]{2,1,0:T(8,128)(2,1)S(1)} %get-tuple-element.50), channel_id=1, source_target_pairs={{0,1},{1,0},{2,3},{3,2},{4,5},{5,4},{6,7},{7,6},{8,9},{9,8},{10,11... | collective-permute-start | bytes 5308424 | tf_op jit(solution)/shard_map/ppermute | solution.py:72
  114.9 4.5 %collective-permute-start.20 = (bf16[2,1,32,640]{3,2,1,0:T(8,128)(2,1)S(1)}, bf16[2,1,32,640]{3,2,1,0:T(8,128)(2,1)S(1)}, u32[]{:S(2)}, u32[]{:S(2)}) collective-permute-start(bf16[2,1,32,640]{3,2,1,0:T(8,128)(2,1)S(1)} %slice.488), channel_id=1, source_target_pairs={{0,64},{1,193},{8,72},{9,201},{16,80},{17,209},{24,88},{25,217},{3... | collective-permute-start | bytes 245768 | tf_op jit(solution)/shard_map/ppermute | solution.py:64
  115.8 6.4 %collective-permute-start.9 = (bf16[144,896]{1,0:T(8,128)(2,1)S(1)}, bf16[144,896]{1,0:T(8,128)(2,1)S(1)}, u32[]{:S(2)}, u32[]{:S(2)}) collective-permute-start(bf16[144,896]{1,0:T(8,128)(2,1)S(1)} %pad_maximum_fusion.7), channel_id=1, source_target_pairs={{0,8},{1,57},{8,0},{9,17},{16,24},{17,9},{24,16},{25,33},{32,40},{... | collective-permute-start | bytes 774152 | tf_op jit(solution)/shard_map/ppermute | solution.py:64
  119.5 21.4 %collective-permute-start.21 = (bf16[1,1,32,640]{3,2,1,0:T(8,128)(2,1)S(1)}, bf16[1,1,32,640]{3,2,1,0:T(8,128)(2,1)S(1)}, u32[]{:S(2)}, u32[]{:S(2)}) collective-permute-start(bf16[1,1,32,640]{3,2,1,0:T(8,128)(2,1)S(1)} %slice.490), channel_id=1, source_target_pairs={{0,192},{1,65},{8,200},{9,73},{16,208},{17,81},{24,216},{25,89},{3... | collective-permute-start | bytes 122888 | tf_op jit(solution)/shard_map/ppermute | solution.py:64
  122.5 6.7 %collective-permute-start.10 = (bf16[80,896]{1,0:T(8,128)(2,1)S(1)}, bf16[80,896]{1,0:T(8,128)(2,1)S(1)}, u32[]{:S(2)}, u32[]{:S(2)}) collective-permute-start(bf16[80,896]{1,0:T(8,128)(2,1)S(1)} %pad_maximum_fusion.10), channel_id=1, source_target_pairs={{0,24},{1,41},{8,16},{9,33},{16,8},{17,25},{24,0},{25,17},{32,56},... | collective-permute-start | bytes 430088 | tf_op jit(solution)/shard_map/ppermute | solution.py:64
  124.0 44.1 %collective-permute-start.30 = (bf16[144,1536]{1,0:T(8,128)(2,1)S(1)}, bf16[144,1536]{1,0:T(8,128)(2,1)S(1)}, u32[]{:S(2)}, u32[]{:S(2)}) collective-permute-start(bf16[144,1536]{1,0:T(8,128)(2,1)S(1)} %pad_maximum_fusion.5), channel_id=1, source_target_pairs={{0,4},{2,6},{4,0},{6,2},{1,5},{3,7},{5,1},{7,3},{8,12},{10,14},{12... | collective-permute-start | bytes 1327112 | tf_op jit(solution)/shard_map/ppermute | solution.py:330
  129.4 8.1 %collective-permute-start.11 = (bf16[48,896]{1,0:T(8,128)(2,1)S(1)}, bf16[48,896]{1,0:T(8,128)(2,1)S(1)}, u32[]{:S(2)}, u32[]{:S(2)}) collective-permute-start(bf16[48,896]{1,0:T(8,128)(2,1)S(1)} %pad_maximum_fusion.12), channel_id=1, source_target_pairs={{0,56},{1,9},{8,48},{9,1},{16,40},{17,57},{24,32},{25,49},{32,24},... | collective-permute-start | bytes 258056 | tf_op jit(solution)/shard_map/ppermute | solution.py:64
  133.2 35.0 %collective-permute-start.29 = (bf16[144,1536]{1,0:T(8,128)(2,1)S(1)}, bf16[144,1536]{1,0:T(8,128)(2,1)S(1)}, u32[]{:S(2)}, u32[]{:S(2)}) collective-permute-start(bf16[144,1536]{1,0:T(8,128)(2,1)S(1)} %pad_maximum_fusion.4), channel_id=1, source_target_pairs={{0,6},{2,0},{4,2},{6,4},{1,7},{3,1},{5,3},{7,5},{8,14},{10,8},{12,... | collective-permute-start | bytes 1327112 | tf_op jit(solution)/shard_map/ppermute | solution.py:330
  137.6 7.5 %collective-permute-start.12 = (bf16[32,896]{1,0:T(8,128)(2,1)S(1)}, bf16[32,896]{1,0:T(8,128)(2,1)S(1)}, u32[]{:S(2)}, u32[]{:S(2)}) collective-permute-start(bf16[32,896]{1,0:T(8,128)(2,1)S(1)} %get-tuple-element.55), channel_id=1, source_target_pairs={{0,56},{1,9},{8,48},{9,1},{16,40},{17,57},{24,32},{25,49},{32,24},... | collective-permute-start | bytes 172040 | tf_op jit(solution)/shard_map/ppermute | solution.py:64
  141.0 6.9 %collective-permute-start.22 = (bf16[1,1,32,640]{3,2,1,0:T(8,128)(2,1)S(1)}, bf16[1,1,32,640]{3,2,1,0:T(8,128)(2,1)S(1)}, u32[]{:S(2)}, u32[]{:S(2)}) collective-permute-start(bf16[1,1,32,640]{3,2,1,0:T(8,128)(2,1)S(1)} %fusion.12), channel_id=1, source_target_pairs={{0,192},{1,65},{8,200},{9,73},{16,208},{17,81},{24,216},{25,89},{3... | collective-permute-start | bytes 122888 | tf_op jit(solution)/shard_map/ppermute | solution.py:64
  145.1 6.3 %collective-permute-start.13 = (bf16[64,896]{1,0:T(8,128)(2,1)S(1)}, bf16[64,896]{1,0:T(8,128)(2,1)S(1)}, u32[]{:S(2)}, u32[]{:S(2)}) collective-permute-start(bf16[64,896]{1,0:T(8,128)(2,1)S(1)} %pad_maximum_fusion.11), channel_id=1, source_target_pairs={{0,24},{1,41},{8,16},{9,33},{16,8},{17,25},{24,0},{25,17},{32,56},... | collective-permute-start | bytes 344072 | tf_op jit(solution)/shard_map/ppermute | solution.py:64
  147.9 4.6 %collective-permute-start.23 = (bf16[2,1,32,640]{3,2,1,0:T(8,128)(2,1)S(1)}, bf16[2,1,32,640]{3,2,1,0:T(8,128)(2,1)S(1)}, u32[]{:S(2)}, u32[]{:S(2)}) collective-permute-start(bf16[2,1,32,640]{3,2,1,0:T(8,128)(2,1)S(1)} %pad_maximum_fusion.13), channel_id=1, source_target_pairs={{0,64},{1,193},{8,72},{9,201},{16,80},{17,209},{24,88},{25,217},{3... | collective-permute-start | bytes 245768 | tf_op jit(solution)/shard_map/ppermute | solution.py:64
  151.4 6.1 %collective-permute-start.14 = (bf16[128,896]{1,0:T(8,128)(2,1)S(1)}, bf16[128,896]{1,0:T(8,128)(2,1)S(1)}, u32[]{:S(2)}, u32[]{:S(2)}) collective-permute-start(bf16[128,896]{1,0:T(8,128)(2,1)S(1)} %pad_maximum_fusion.8), channel_id=1, source_target_pairs={{0,8},{1,57},{8,0},{9,17},{16,24},{17,9},{24,16},{25,33},{32,40},{... | collective-permute-start | bytes 688136 | tf_op jit(solution)/shard_map/ppermute | solution.py:64
  151.6 16.8 %collective-permute-start.28 = (bf16[144,1536]{1,0:T(8,128)(2,1)S(1)}, bf16[144,1536]{1,0:T(8,128)(2,1)S(1)}, u32[]{:S(2)}, u32[]{:S(2)}) collective-permute-start(bf16[144,1536]{1,0:T(8,128)(2,1)S(1)} %pad_maximum_fusion.3), channel_id=1, source_target_pairs={{0,2},{2,4},{4,6},{6,0},{1,3},{3,5},{5,7},{7,1},{8,10},{10,12},{12... | collective-permute-start | bytes 1327112 | tf_op jit(solution)/shard_map/ppermute | solution.py:330
  152.5 10.9 %collective-permute-start.24 = (bf16[4,1,32,640]{3,2,1,0:T(8,128)(2,1)S(1)}, bf16[4,1,32,640]{3,2,1,0:T(8,128)(2,1)S(1)}, u32[]{:S(2)}, u32[]{:S(2)}) collective-permute-start(bf16[4,1,32,640]{3,2,1,0:T(8,128)(2,1)S(1)} %pad_maximum_fusion.9), channel_id=1, source_target_pairs={{0,56},{1,9},{8,48},{9,1},{16,40},{17,57},{24,32},{25,49},{32,24},... | collective-permute-start | bytes 491528 | tf_op jit(solution)/shard_map/ppermute | solution.py:64
  157.6 13.9 %collective-permute-start.15 = (bf16[256,896]{1,0:T(8,128)(2,1)S(1)}, bf16[256,896]{1,0:T(8,128)(2,1)S(1)}, u32[]{:S(2)}, u32[]{:S(2)}) collective-permute-start(bf16[256,896]{1,0:T(8,128)(2,1)S(1)} %pad_maximum_fusion.2), channel_id=1, source_target_pairs={{0,192},{1,65},{8,200},{9,73},{16,208},{17,81},{24,216},{25,89},{3... | collective-permute-start | bytes 1376264 | tf_op jit(solution)/shard_map/ppermute | solution.py:64
  163.4 16.5 %collective-permute-start.25 = (bf16[4,2,32,640]{3,2,1,0:T(8,128)(2,1)S(1)}, bf16[4,2,32,640]{3,2,1,0:T(8,128)(2,1)S(1)}, u32[]{:S(2)}, u32[]{:S(2)}) collective-permute-start(bf16[4,2,32,640]{3,2,1,0:T(8,128)(2,1)S(1)} %pad_maximum_fusion.6), channel_id=1, source_target_pairs={{0,24},{1,41},{8,16},{9,33},{16,8},{17,25},{24,0},{25,17},{32,56},... | collective-permute-start | bytes 983048 | tf_op jit(solution)/shard_map/ppermute | solution.py:64
  171.5 19.1 %collective-permute-start.16 = (bf16[512,896]{1,0:T(8,128)(2,1)S(1)}, bf16[512,896]{1,0:T(8,128)(2,1)S(1)}, u32[]{:S(2)}, u32[]{:S(2)}) collective-permute-start(bf16[512,896]{1,0:T(8,128)(2,1)S(1)} %constant_dynamic-update-slice_fusion.a_own), channel_id=1, source_target_pairs={{0,64},{1,193},{8,72},{9,201},{16,80},{17,209},{24,88},{25,217},{3... | collective-permute-start | bytes 2752520 | tf_op jit(solution)/shard_map/ppermute | solution.py:64
  180.0 10.7 %collective-permute-start.26 = (bf16[4,4,32,640]{3,2,1,0:T(8,128)(2,1)S(1)}, bf16[4,4,32,640]{3,2,1,0:T(8,128)(2,1)S(1)}, u32[]{:S(2)}, u32[]{:S(2)}) collective-permute-start(bf16[4,4,32,640]{3,2,1,0:T(8,128)(2,1)S(1)} %pad_maximum_fusion), channel_id=1, source_target_pairs={{0,8},{1,57},{8,0},{9,17},{16,24},{17,9},{24,16},{25,33},{32,40},{... | collective-permute-start | bytes 1966088 | tf_op jit(solution)/shard_map/ppermute | solution.py:64

commit v2 on v0

v2 whole, which is shorter than its diff:
```python
import functools
import math

import jax
import jax.numpy as jnp
import numpy as np
from jax import lax
from jax.experimental import pallas as pl
from jax.experimental.pallas import tpu as pltpu
from jax.sharding import Mesh, PartitionSpec as P

D = 1536
ROWS = 128
HALF = ROWS // 2
BLOCK = 32
TILE = 8 * BLOCK
EXTRA = 16
WIDE = D + 128
CALL_OF = ((0, 0), (1, 0), (2, 0), (1, 2 * ROWS))
FIRST_BLOCK = (0, 2, 6, 4)
SCALE = 4.0 / math.sqrt(D)
BF16, F32 = jnp.bfloat16, jnp.float32
ROW_DOT = (((1,), (1,)), ((), ()))

Z_PAIRS = ((1, 0, 3, 2, 5, 4, 7, 6), (7, 2, 1, 4, 3, 6, 5, 0), (3, 6, 5, 0, 7, 2, 1, 4))


def partner(step, z, c):
    return (Z_PAIRS[step][(z - c) % 8] + c) % 8


def order(step, z, c):
    if step == 2:
        return sorted((z, partner(2, z, c)))
    return order(step + 1, z, c) + order(step + 1, partner(step, z, c), c)


X_PAIRS = ((1, 0, 3, 2), (3, 2, 1, 0))


def x_partner(step, x, c):
    return (X_PAIRS[step][(x - c) % 4] + c) % 4


def x_order(step, x, c):
    if step == 2:
        return [x]
    return x_order(step + 1, x, c) + x_order(step + 1, x_partner(step, x, c), c)


X_ORDER = np.array(
    [
        x_order(0, x, c) + [x_order(0, x, 1 - c).index(i) for i in x_order(0, x, c)]
        for x in range(4)
        for c in range(2)
    ],
    np.int32,
)
Z_ORDER = np.array([order(0, z, c) for z in range(8) for c in range(2)], np.int32)


def exchange(x, step):
    return lax.ppermute(x, ("z", "c"), [(z * 2 + c, partner(step, z, c) * 2 + c) for z in range(8) for c in range(2)])


def x_exchange(v, step):
    return lax.ppermute(
        v, ("x", "c"), [(x * 2 + c, x_partner(step, x, c) * 2 + c) for x in range(4) for c in range(2)]
    )


def shift(x, axis, k):
    n = {"x": 4, "y": 4}[axis]
    return lax.ppermute(x, axis, [(i, (i + k) % n) for i in range(n)])


def swap_core(x):
    return lax.ppermute(x, "c", [(0, 1), (1, 0)])


def ring_gather(h0, h1, axis, first=None):
    below0, above1 = shift(h0, axis, 1), shift(h1, axis, -1)
    below1, above0 = shift(h1, axis, 1), shift(h0, axis, -1)
    far = shift(below0, axis, 1), shift(above1, axis, -1)
    if first is not None:
        below1, above0, first = lax.optimization_barrier((below1, above0, first))
    return (below0, below1), (above0, above1), far, first


def place_kernel(rs, place, *refs):
    parts, out, sems = refs[: len(rs)], refs[-2], refs[-1]
    copies = []
    for i, (part, (r, h)) in enumerate(zip(parts, rs)):
        for j in range(4):
            row = lax.rem(place[0] + r, 4) * TILE + place[4 + 4 * h + j] * BLOCK
            rows = out.at[pl.ds(pl.multiple_of(row, BLOCK), BLOCK)]
            copies.append(pltpu.make_async_copy(part.at[pl.ds(j * BLOCK, BLOCK)], rows, sems.at[4 * i + j]))
    for copy in copies:
        copy.start()
    for copy in copies:
        copy.wait()


def put_rows(place, parts, rs, to=None):
    whole = [pl.BlockSpec(memory_space=pltpu.VMEM)] * len(parts)
    return pl.pallas_call(
        functools.partial(place_kernel, rs),
        out_shape=jax.ShapeDtypeStruct((1024, D), BF16),
        in_specs=[pl.BlockSpec(memory_space=pltpu.SMEM)] + whole + [pl.BlockSpec(memory_space=pl.ANY)] * (to is not None),
        out_specs=pl.BlockSpec(memory_space=pl.ANY),
        scratch_shapes=[pltpu.SemaphoreType.DMA((4 * len(parts),))],
        input_output_aliases={} if to is None else {len(parts) + 1: 0},
        compiler_params=pltpu.CompilerParams(vmem_limit_bytes=16 << 20),
        cost_estimate=pl.CostEstimate(flops=0, bytes_accessed=4 * 128 * len(parts) * D, transcendentals=0),
        name="put_rows",
    )(place, *parts, *([] if to is None else [to]))


def score_kernel(n, others, *refs):
    es, f, stats = refs[:n], refs[n], refs[n + 1 : n + 1 + others]
    p_ref, top_ref, stat_ref, top_acc, sum_acc = refs[n + 1 + others :]
    t = pl.program_id(0)
    rows = jnp.concatenate([e[...] for e in es], axis=0)
    s = lax.dot_general(f[...], rows, ROW_DOT, preferred_element_type=F32)
    top = jnp.max(s, axis=0, keepdims=True)
    p = jnp.exp((s - top) * SCALE)
    p_ref[...] = p
    total = jnp.sum(p, axis=0, keepdims=True)

    @pl.when(t == 0)
    def _():
        top_ref[:1, :] = top
        top_acc[...] = top
        sum_acc[...] = total

    @pl.when(t == 1)
    def _():
        top_ref[1:, :] = top
        old = top_acc[...]
        new = jnp.maximum(old, top)
        l = sum_acc[...] * jnp.exp((old - new) * SCALE) + total * jnp.exp((top - new) * SCALE)
        stat = []
        for at in range(0, rows.shape[0], 256):
            for v in (new, l):
                stat += [v[:, at : at + ROWS], v[:, at + ROWS : at + 256]]
        stat = jnp.concatenate(stat, axis=0)
        if stats:
            own, near = stats
            stat = jnp.concatenate([own[...], near[:4, :], stat, near[4:, :]], axis=0)
            for i in range(8):
                stat_ref[i] = stat
        else:
            stat_ref[...] = stat


def scores(es, f, *stats):
    rows = sum(e.shape[0] for e in es)
    whole = lambda *shape: pl.BlockSpec(shape, lambda t: (0,) * len(shape))
    stat = (8, 16, ROWS) if stats else (rows // 64, ROWS)
    return pl.pallas_call(
        functools.partial(score_kernel, len(es), len(stats)),
        grid=(2,),
        in_specs=[whole(*e.shape) for e in es]
        + [pl.BlockSpec((512, D), lambda t: (t, 0))]
        + [whole(*v.shape) for v in stats],
        out_specs=[pl.BlockSpec((512, rows), lambda t: (t, 0)), whole(2, rows), whole(*stat)],
        out_shape=[
            jax.ShapeDtypeStruct((1024, rows), F32),
            jax.ShapeDtypeStruct((2, rows), F32),
            jax.ShapeDtypeStruct(stat, F32),
        ],
        scratch_shapes=[pltpu.VMEM((1, rows), F32), pltpu.VMEM((1, rows), F32)],
        compiler_params=pltpu.CompilerParams(vmem_limit_bytes=58 << 20),
        cost_estimate=pl.CostEstimate(flops=2 * 1024 * rows * D, bytes_accessed=6 << 20, transcendentals=1024 * rows),
        name="fine_scores",
    )(*es, f, *stats)


def find_factors(place, tops, stats, factors):
    x, c = place[1], place[2]
    for r in range(4):
        for d in range(2):
            ms, ls = [], []
            for src in range(8):
                sr = lax.rem(x + (r + 4 - src // 2), 4)
                sd = jnp.bitwise_xor(c, d ^ (src % 2))
                at = sr * 4 + sd
                ms.append(stats[src, pl.ds(at, 1), :])
                ls.append(stats[src, pl.ds(at + 2, 1), :])
            top = ms[0]
            for m in ms[1:]:
                top = jnp.maximum(top, m)
            total = jnp.zeros_like(top)
            for m, l in zip(ms, ls):
                total = total + l * jnp.exp((m - top) * SCALE)
            call, at = CALL_OF[r]
            at += d * ROWS
            to = (FIRST_BLOCK[r] + d) * ROWS
            factors[:, to : to + ROWS] = jnp.exp((tops[call][:, at : at + ROWS] - top) * SCALE) / total


def tile_sums(place, tile, factors, ps, es):
    out = jnp.zeros((TILE, D), F32)
    mass = jnp.zeros((TILE, 128), F32)
    at, k = 0, 0
    for p in ps:
        cols = p.shape[1]
        blocks = [p[pl.ds(pl.multiple_of(place[4 + j] * BLOCK, BLOCK), BLOCK), :] for j in range(8)]
        w = (jnp.concatenate(blocks, axis=0) * factors[pl.ds(tile // 2, 1), at : at + cols]).astype(BF16)
        rows = []
        while sum(e.shape[0] for e in rows) < cols:
            rows.append(es[k][...])
            k += 1
        out = out + jnp.dot(w, jnp.concatenate(rows, axis=0), preferred_element_type=F32)
        mass = mass + jnp.dot(w, jnp.ones((cols, 128), BF16), preferred_element_type=F32)
        at += cols
    return out, mass


def put_halves(out, mass, keep, keep_mass, send):
    keep[...] = out[:128]
    keep_mass[...] = mass[:128]
    send[:, :D] = out[128:].astype(BF16)
    high = mass[128:].astype(BF16).astype(F32)
    lane = lax.broadcasted_iota(jnp.int32, (128, 128), 1)
    send[:, D:] = jnp.where(lane < 64, high, mass[128:] - high).astype(BF16)


def far_kernel(n, place, *refs):
    es, ps, tops, stats = refs[:n], refs[n : n + 3], refs[n + 3 : n + 6], refs[n + 6]
    keep, keep_mass, send, factors = refs[n + 7 :]
    find_factors(place, tops, stats, factors)
    out, mass = tile_sums(place, lax.rem(place[0] + 2, 4), factors, ps, es)
    put_halves(out, mass, keep, keep_mass, send)


def rest_kernel(n, place, *refs):
    es, ps, factors = refs[:n], refs[n : n + 3], refs[n + 3]
    outs = refs[n + 4 :]
    t = pl.program_id(0)
    out, mass = tile_sums(place, rest_tile(t, place), factors, ps, es)
    for i in range(3):

        @pl.when(t == i)
        def _():
            put_halves(out, mass, *outs[3 * i : 3 * i + 3])


def rest_tile(t, place):
    return lax.rem(place[0] + jnp.where(t == 0, 1, jnp.where(t == 1, 3, 0)), 4)


def fine_sums(place, es, ps, tops, stats):
    whole = lambda *shape: pl.BlockSpec(shape, lambda t, s: (0,) * len(shape))
    halves = [
        jax.ShapeDtypeStruct((128, D), F32),
        jax.ShapeDtypeStruct((128, 128), F32),
        jax.ShapeDtypeStruct((128, WIDE), BF16),
    ]
    specs = [whole(*half.shape) for half in halves]
    params = pltpu.CompilerParams(vmem_limit_bytes=58 << 20)
    *far, factors = pl.pallas_call(
        functools.partial(far_kernel, len(es)),
        grid_spec=pltpu.PrefetchScalarGridSpec(
            num_scalar_prefetch=1,
            grid=(1,),
            in_specs=[whole(*e.shape) for e in es]
            + [pl.BlockSpec((TILE, p.shape[1]), lambda t, s: (lax.rem(s[0] + 2, 4), 0)) for p in ps]
            + [whole(*top.shape) for top in tops]
            + [whole(8, 16, ROWS)],
            out_specs=specs + [whole(2, 1024)],
        ),
        out_shape=halves + [jax.ShapeDtypeStruct((2, 1024), F32)],
        compiler_params=params,
        cost_estimate=pl.CostEstimate(flops=2 * 256 * 1024 * D, bytes_accessed=5 << 20, transcendentals=0),
        name="far_sums",
    )(place, *es, *ps, *tops, stats)
    rest = pl.pallas_call(
        functools.partial(rest_kernel, len(es)),
        grid_spec=pltpu.PrefetchScalarGridSpec(
            num_scalar_prefetch=1,
            grid=(3,),
            in_specs=[whole(*e.shape) for e in es]
            + [pl.BlockSpec((TILE, p.shape[1]), lambda t, s: (rest_tile(t, s), 0)) for p in ps]
            + [whole(2, 1024)],
            out_specs=specs * 3,
        ),
        out_shape=halves * 3,
        compiler_params=params,
        cost_estimate=pl.CostEstimate(flops=2 * 768 * 1024 * D, bytes_accessed=10 << 20, transcendentals=0),
        name="rest_sums",
    )(place, *es, *ps, factors)
    return far, rest[:3], rest[3:6], rest[6:]


def load(ref, at, n):
    if isinstance(ref, tuple):
        return ref[0][at : at + n, :], ref[1][at : at + n, :]
    mass = ref[at : at + n, D:].astype(F32)
    mass = mass[:, :1] + mass[:, 64:65]
    return ref[at : at + n, :D].astype(F32), jnp.broadcast_to(mass, (n, 128))


def add(a, b):
    return a[0] + b[0], a[1] + b[1]


def store(ref, v):
    sums, mass = v
    ref[:, :D] = sums.astype(BF16)
    high = mass.astype(BF16).astype(F32)
    lane = lax.broadcasted_iota(jnp.int32, mass.shape, 1)
    ref[:, D:] = jnp.where(lane < 64, high, mass - high).astype(BF16)


def far_step(keep, mass, got, low, high):
    for at, out in ((0, low), (64, high)):
        store(out, add(load((keep, mass), at, 64), load(got, at, 64)))


def side_step(first, keep, mass, got, far, out):
    for at in (0, 64):
        v = add(load((keep, mass), at, 64), load(got, at, 64))
        if at == first:
            v = add(v, load(far, 0, 64))
        store(out.at[pl.ds(at, 64)], v)


def own_step(keep, mass, got, up, down, sums, masses, send):
    for at in (0, 64):
        v = add(load((keep, mass), at, 64), load(got, at, 64))
        v = add(v, add(load(up, at, 64), load(down, at, 64)))
        if at:
            store(send, v)
        else:
            sums[...], masses[...] = v


def half_step(keep, mass, got, out):
    store(out, add(load((keep, mass), 0, 64), load(got, 0, 64)))


def last_step(own, got, out):
    sums, mass = add(load(own, 0, 64), load(got, 0, 64))
    out[...] = (sums / jnp.maximum(mass[:, :1], 1.0)).astype(BF16)


def step(kernel, args, outs):
    whole = pl.BlockSpec(memory_space=pltpu.VMEM)
    out = pl.pallas_call(
        kernel,
        in_specs=[whole] * len(args),
        out_specs=[whole] * len(outs),
        out_shape=[jax.ShapeDtypeStruct(shape, t) for shape, t in outs],
        compiler_params=pltpu.CompilerParams(vmem_limit_bytes=16 << 20),
        cost_estimate=pl.CostEstimate(flops=1 << 20, bytes_accessed=2 << 20, transcendentals=0),
        name="add_" + getattr(kernel, "func", kernel).__name__,
    )(*args)
    return out if len(out) > 1 else out[0]


def coarse_kernel(place, s, top, total, fine, keep, send, m_keep):
    w = (jnp.exp(s[...] - top[...]) / total[...]).astype(BF16)
    out = jnp.dot(w, fine[...], preferred_element_type=F32)
    weight = lax.dot_general(jnp.ones((8, 1024), BF16), w, ROW_DOT, preferred_element_type=F32)[:1, :]
    first = place[2] == 0
    keep[0] = jnp.where(first, out[:128], out[128:])
    send[0, :128] = jnp.where(first, out[128:], out[:128]).astype(BF16)
    m_keep[0] = jnp.where(first, weight[:, :128], weight[:, 128:])
    sent = jnp.where(first, weight[:, 128:], weight[:, :128])
    high = sent.astype(BF16)
    low = (sent - high.astype(F32)).astype(BF16)
    send[0, 128:, :256] = jnp.broadcast_to(jnp.concatenate([high, low], axis=1), (EXTRA, 256))
    send[0, 128:, 256:] = jnp.zeros((EXTRA, D - 256), BF16)


def coarse_sums(place, s, top, total, fine):
    whole = lambda *shape: pl.BlockSpec(shape, lambda r, p: (0,) * len(shape))
    row = lambda *shape: pl.BlockSpec((1, *shape), lambda r, p: (r, 0, 0))
    swapped = pl.BlockSpec((1, 128 + EXTRA, D), lambda r, p: (p[16 + r], 0, 0))
    return pl.pallas_call(
        coarse_kernel,
        grid_spec=pltpu.PrefetchScalarGridSpec(
            num_scalar_prefetch=1,
            grid=(4,),
            in_specs=[pl.BlockSpec((256, 1024), lambda r, p: (p[12 + r], 0))]
            + [whole(1, 1024), whole(1, 1024), whole(1024, D)],
            out_specs=[row(128, D), swapped, row(1, 128)],
        ),
        out_shape=[
            jax.ShapeDtypeStruct((4, 128, D), F32),
            jax.ShapeDtypeStruct((4, 128 + EXTRA, D), BF16),
            jax.ShapeDtypeStruct((4, 1, 128), F32),
        ],
        compiler_params=pltpu.CompilerParams(vmem_limit_bytes=24 << 20),
        cost_estimate=pl.CostEstimate(flops=2 * 1024 * 1024 * D, bytes_accessed=12 << 20, transcendentals=1 << 20),
        name="coarse_sums",
    )(place, s, top, total, fine)


def split(v):
    high = lax.reduce_precision(v, 8, 7)
    return high, lax.reduce_precision(v - high, 8, 7)


def with_mass(total, mass, extra=EXTRA):
    rows = jnp.concatenate(split(mass), axis=1)
    rows = jnp.pad(rows, ((0, extra - rows.shape[0]), (0, total.shape[1] - rows.shape[1])))
    return jnp.concatenate([total, rows], axis=0).astype(BF16)


def coarse_scores(fine, coarse):
    s = lax.dot_general(coarse, fine, ROW_DOT, preferred_element_type=F32) * SCALE
    top = jnp.max(s, axis=0, keepdims=True)
    return s, top, jnp.sum(jnp.exp(s - top), axis=0, keepdims=True)


def coarse_rows(keep, send, m_keep):
    got = swap_core(send).astype(F32)
    total = keep + got[:, :128]
    mass = m_keep[:, 0] + got[:, 128, :128] + got[:, 128, 128:256]
    for step, n in ((0, 2), (1, 1)):
        got = x_exchange(with_mass(total[n:].reshape(n * 128, D), mass[n:], 8), step).astype(F32)
        total = total[:n] + got[: n * 128].reshape(n, 128, D)
        mass = mass[:n] + got[n * 128 : n * 128 + n, :128] + got[n * 128 : n * 128 + n, 128:256]
    return (total[0] / jnp.maximum(mass[0], 1.0)[:, None]).astype(BF16)


def shards(embeddings, fine, coarse):
    y, z, x, c = (lax.axis_index(a) for a in ("y", "z", "x", "c"))
    z_order = lax.dynamic_index_in_dim(jnp.asarray(Z_ORDER), z * 2 + c, 0, keepdims=False)
    x_places = lax.dynamic_index_in_dim(jnp.asarray(X_ORDER), x * 2 + c, 0, keepdims=False)
    place = jnp.concatenate([jnp.stack([y, x, c, z]), z_order, x_places])

    mine = [embeddings, swap_core(embeddings)]
    own = scores(mine, fine)
    below, above, far, own = ring_gather(embeddings[:HALF], embeddings[HALF:], "x", own)
    near = [*above, *map(swap_core, above), *below, *map(swap_core, below)]
    far = [*far, *map(swap_core, far)]
    calls = [own, scores(near, fine)]
    calls.append(scores(far, fine, calls[0][2], calls[1][2]))
    stats = lax.all_to_all(calls[2][2], ("x", "c"), 0, 0)
    far, up, down, own = fine_sums(
        place, [*mine, *near, *far], [call[0] for call in calls], [call[1] for call in calls], stats
    )

    sent = lambda n: ((n, WIDE), BF16)
    got = exchange(far[2], 0)
    rest, got = lax.optimization_barrier(((up, down, own), got))
    up, down, own = rest
    got_up, got_down, got_own = (exchange(v[2], 0) for v in rest)
    far0, far1 = step(far_step, [far[0], far[1], got], [sent(64), sent(64)])
    far0, far1 = shift(far0, "y", 1), shift(far1, "y", -1)
    up = step(functools.partial(side_step, 0), [up[0], up[1], got_up, far0], [sent(128)])
    down = step(functools.partial(side_step, 64), [down[0], down[1], got_down, far1], [sent(128)])
    up, down, got_own, coarse = lax.optimization_barrier((up, down, got_own, coarse))
    c_sums = coarse_sums(place, *coarse_scores(fine, coarse), fine)
    up, down = shift(up, "y", 1), shift(down, "y", -1)
    up, down, c_sums = lax.optimization_barrier((up, down, c_sums))
    sums, masses, send = step(
        own_step, [own[0], own[1], got_own, up, down], [((64, D), F32), ((64, 128), F32), sent(64)]
    )

    own = step(half_step, [sums, masses, exchange(send, 1)], [sent(64)])
    a = step(last_step, [own, exchange(own, 2)], [((64, D), BF16)])

    a0 = jnp.concatenate([a, exchange(a, 1)], axis=0)
    a1 = exchange(a0, 0)
    below0, above0 = shift(a0, "y", 1), shift(a0, "y", -1)
    a1, below0, above0 = lax.optimization_barrier((a1, below0, above0))
    above1, below1 = shift(a1, "y", -1), shift(a1, "y", 1)
    far0, far1 = shift(below0, "y", 1), shift(above1, "y", -1)
    new_fine = put_rows(place, [a0, a1, above0, below0], [(0, 0), (0, 1), (1, 0), (3, 0)])
    new_coarse = coarse_rows(*c_sums)
    far1, new_coarse, new_fine = lax.optimization_barrier((far1, new_coarse, new_fine))
    new_fine = put_rows(place, [above1, far0, far1, below1], [(1, 1), (2, 0), (2, 1), (3, 1)], new_fine)
    return new_fine, new_coarse


def solution(mesh):
    torus = Mesh(mesh.devices.reshape(4, 8, 4, 2), ("y", "z", "x", "c"))
    return jax.shard_map(
        shards,
        mesh=torus,
        in_specs=(P(("y", "z", "x", "c"), None), P(("x", "c"), None), P()),
        out_specs=(P(("x", "c"), None), P(("x", "c"), None)),
        check_vma=False,
    )
```

time: 328 us -> 154 us (0.47)
  waiting for transfers between devices: 180 us -> 58.4 us
  blocking collectives: 88.6 us -> 0 us
  starting transfers between devices: 0.12 us -> 39.9 us
  Pallas kernels: 0 us -> 37.4 us
  matrix products: 24.5 us -> 3.46 us
  other arithmetic: 16.5 us -> 3.2 us
  between operations: 14.4 us -> 1.24 us
  local copies, waits for them, and re-layouts: 2.34 us -> 8.16 us
    psum x1 -> x0, waiting for transfers between devices: 111 us -> none  [shards(): weighted, total_mass = lax.psum((fine_weighted, fine_mass), 'outer')]
    psum x2 -> x0, blocking collectives: 74.8 us -> none  [the longest x1 62.1 us: shards(): weighted, total_mass = lax.psum((fine_weighted, fine_mass), 'outer')]
    ppermute x0 -> x34, waiting for transfers between devices: none -> 54.2 us  [the longest x16 31.8 us: shift(): return lax.ppermute(x, axis, [(i, (i + k) % n) for i in range(n)])]
    reduce_scatter x1 -> x0, waiting for transfers between devices: 42.9 us -> none  [shards(): lax.psum_scatter(coarse_weighted, 'inner', scatter_dimension=0, tiled=True)]
    pallas_call x0 -> x14, Pallas kernels: none -> 37.4 us  [the longest x3 13.4 us: scores(): pl.pallas_call(functools.partial(score_kernel, len(es), len(stats)), grid...]
    ppermute x0 -> x34, starting transfers between devices: none -> 36.6 us  [the longest x16 17.6 us: shift(): return lax.ppermute(x, axis, [(i, (i + k) % n) for i in range(n)])]
    all_gather x1 -> x0, waiting for transfers between devices: 24.9 us -> none  [shards(): gathered = lax.all_gather(embeddings, 'inner', axis=0, tiled=True)]
    dot_general x4 -> x1, matrix products: 24.5 us -> 3.46 us  [coarse_scores(): lax.dot_general(coarse, fine, ROW_DOT, preferred_element_type=F32) * SCALE]
  transfers between devices with their start and end apart: 3 -> 35, of which waited for: 3 -> 17; matrix products, arithmetic and copies ran while one was open for 6% -> 6% of each run, Pallas kernels for 0% -> 17%
where the time goes in v2:
time: 154 us; the launch traced here: 152 us
  waiting for transfers between devices  58.4 us (38%)
  starting transfers between devices  39.9 us (26%)
  Pallas kernels  37.4 us (24%)
  local copies, waits for them, and re-layouts  8.16 us (5%)
  matrix products  3.46 us (2%)
  other arithmetic  3.2 us (2%)
    ppermute x16, waiting for transfers between devices, shift(): return lax.ppermute(x, axis, [(i, (i + k) % n) for i in range(n)])  31.8 us
    ppermute x8, waiting for transfers between devices, exchange(): lax.ppermute(x, ('z', 'c'), [(z * 2 + c, partner(step, z, c) * 2 + c) for...  19.5 us
    ppermute x16, starting transfers between devices, shift(): return lax.ppermute(x, axis, [(i, (i + k) % n) for i in range(n)])  17.6 us
    ppermute x8, starting transfers between devices, exchange(): lax.ppermute(x, ('z', 'c'), [(z * 2 + c, partner(step, z, c) * 2 + c) for...  16.8 us
    pallas_call x3, Pallas kernels, scores(): pl.pallas_call(functools.partial(score_kernel, len(es), len(stats)), grid...  13.4 us
    pallas_call x1, Pallas kernels, fine_sums(): pl.pallas_call(functools.partial(rest_kernel, len(es)), grid_spec=pltpu.P...  8.86 us
    unnamed x34, local copies, waits for them, and re-layouts  5.33 us
    pallas_call x1, Pallas kernels, fine_sums(): pl.pallas_call(functools.partial(far_kernel, len(es)), grid_spec=pltpu.Pr...  5.08 us
  transfers between devices with their start and end apart: 35, of which 17 were waited for; matrix products, arithmetic and copies ran while one was open for 6% of the time, Pallas kernels for 17%

profile of v2, /device:TPU:80, one launch (start us, length us, event | category | flops | bytes accessed | tf_op | source)
XLA Modules:
  0.0 151.8 jit_solution(10998356691476855936)
XLA Ops:
  0.7 1.2 fusion.23
  1.9 2.8 %collective-permute-start.3 = (bf16[64,1536]{1,0:T(8,128)(2,1)S(1)}, bf16[64,1536]{1,0:T(8,128)(2,1)S(1)}, u32[]{:S(2)}, u32[]{:S(2)}) collective-permute-start(bf16[64,1536]{1,0:T(8,128)(2,1)S(1)} %get-tuple-element.123), channel_id=1, source_target_pairs={{0,6},{2,0},{4,2},{6,4},{1,7},{3,1},{5,3},{7,5},{8,14},{10,8},{12,... | collective-permute-start | bytes 589832 | tf_op jit(solution)/shard_map/ppermute | solution.py:74
  4.8 0.8 collective-permute-start.1
  5.5 2.5 %collective-permute-start.2 = (bf16[64,1536]{1,0:T(8,128)(2,1)S(1)}, bf16[64,1536]{1,0:T(8,128)(2,1)}, u32[]{:S(2)}, u32[]{:S(2)}) collective-permute-start(bf16[64,1536]{1,0:T(8,128)(2,1)S(1)} %get-tuple-element.122), channel_id=1, source_target_pairs={{0,6},{2,0},{4,2},{6,4},{1,7},{3,1},{5,3},{7,5},{8,14},{10,8},{12,... | collective-permute-start | bytes 589832 | tf_op jit(solution)/shard_map/ppermute | solution.py:74
  8.1 1.9 %collective-permute-done.3.refs_1_.refs_3_ = bf16[64,1536]{1,0:T(8,128)(2,1)S(1)} collective-permute-done((bf16[64,1536]{1,0:T(8,128)(2,1)S(1)}, bf16[64,1536]{1,0:T(8,128)(2,1)S(1)}, u32[]{:S(2)}, u32[]{:S(2)}) %collective-permute-start.3) | collective-permute-done | bytes 196640 | tf_op jit(solution)/shard_map/ppermute | solution.py:74
  10.0 3.8 %collective-permute-done.6.refs_4_.refs_6_ = bf16[64,1536]{1,0:T(8,128)(2,1)} collective-permute-done((bf16[64,1536]{1,0:T(8,128)(2,1)S(1)}, bf16[64,1536]{1,0:T(8,128)(2,1)}, u32[]{:S(2)}, u32[]{:S(2)}) %collective-permute-start.6) | collective-permute-done | bytes 196640 | tf_op jit(solution)/shard_map/ppermute | solution.py:74
  13.8 2.0 %collective-permute-start.9 = (bf16[64,1536]{1,0:T(8,128)(2,1)}, bf16[64,1536]{1,0:T(8,128)(2,1)}, u32[]{:S(2)}, u32[]{:S(2)}) collective-permute-start(bf16[64,1536]{1,0:T(8,128)(2,1)} %collective-permute-done.6.refs_4_.refs_6_), channel_id=1, source_target_pairs={{0,2},{2,4},{4,6},{6,0},{1,3},{3,5},{5,7},{7,1},{8,10},{10,12},{12... | collective-permute-start | bytes 589832 | tf_op jit(solution)/shard_map/ppermute | solution.py:74
  15.9 3.9 %fine_scores.3 = (f32[1024,256]{1,0:T(8,128)}, f32[2,256]{1,0:T(2,128)}, f32[4,128]{1,0:T(4,128)}) custom-call(bf16[128,1536]{1,0:T(8,128)(2,1)} %refs_0_.5, bf16[128,1536]{1,0:T(8,128)(2,1)} %copy-done.11, bf16[1024,1536]{1,0:T(8,128)(2,1)} %fine.1), custom_call_target="tpu_custom_call" | custom-call | flops 805306368 | bytes 6291456 | tf_op jit(solution)/shard_map/fine_scores/pallas_call | solution.py:160
  19.9 0.5 collective-permute-start.4
  20.5 1.8 %collective-permute-done.9.refs_0_.refs_10_ = bf16[64,1536]{1,0:T(8,128)(2,1)} collective-permute-done((bf16[64,1536]{1,0:T(8,128)(2,1)}, bf16[64,1536]{1,0:T(8,128)(2,1)}, u32[]{:S(2)}, u32[]{:S(2)}) %collective-permute-start.9) | collective-permute-done | bytes 196640 | tf_op jit(solution)/shard_map/ppermute | solution.py:74
  22.3 0.6 collective-permute-start.12
  22.9 5.4 %fine_scores.4 = (f32[1024,512]{1,0:T(8,128)}, f32[2,512]{1,0:T(2,128)}, f32[8,128]{1,0:T(8,128)}) custom-call(bf16[64,1536]{1,0:T(8,128)(2,1)} %collective-permute-done.2.refs_0_.refs_2_, bf16[64,1536]{1,0:T(8,128)(2,1)} %copy-done.15, bf16[64,1536]{1,0:T(8,128)(2,1)} %collective-permute-done.4.refs_2_.refs_4_, bf16[64,1536]{1,0:T(8,128)(2,1)} %copy-done.16, ...), custom_call_target="tpu_custom_call" | custom-call | flops 1610612736 | bytes 6291456 | tf_op jit(solution)/shard_map/fine_scores/pallas_call | solution.py:160
  28.4 0.7 copy-done.12
  29.1 4.0 %fine_scores.5 = (f32[1024,256]{1,0:T(8,128)}, f32[2,256]{1,0:T(2,128)}, f32[8,16,128]{2,1,0:T(8,128)}) custom-call(bf16[64,1536]{1,0:T(8,128)(2,1)} %collective-permute-done.9.refs_0_.refs_10_, bf16[64,1536]{1,0:T(8,128)(2,1)} %collective-permute-done.10.refs_1_.refs_11_, bf16[64,1536]{1,0:T(8,128)(2,1)} %copy-done.12, bf16[64,1536]{1,0:T(8,128)(2,1)} %copy-done.13, ...), custom_call_target="tpu_custom_call" | custom-call | flops 805306368 | bytes 6291456 | tf_op jit(solution)/shard_map/fine_scores/pallas_call | solution.py:160
  33.1 3.4 %all-to-all-start = ((f32[8,16,128]{2,1,0:T(8,128)}), f32[8,16,128]{2,1,0:T(8,128)S(1)}, u32[]{:S(2)}, u32[]{:S(2)}) async-start(f32[8,16,128]{2,1,0:T(8,128)} %get-tuple-element.75), calls=%async_computation | async-start | bytes 131072 | tf_op jit(solution)/shard_map/all_to_all | solution.py:442
  36.4 0.7 dynamic-slice_bitcast_fusion
  37.2 0.6 concatenate.22.place
  37.8 4.2 %all-to-all-done.refs_20_ = f32[8,16,128]{2,1,0:T(8,128)S(1)} async-done(((f32[8,16,128]{2,1,0:T(8,128)}), f32[8,16,128]{2,1,0:T(8,128)S(1)}, u32[]{:S(2)}, u32[]{:S(2)}) %all-to-all-start) | async-done | bytes 65568 | tf_op jit(solution)/shard_map/all_to_all | solution.py:442
  42.0 0.6 copy-done.14
  42.6 5.1 %far_sums.1 = (f32[128,1536]{1,0:T(8,128)}, f32[128,128]{1,0:T(8,128)}, bf16[128,1664]{1,0:T(8,128)(2,1)}, f32[2,1024]{1,0:T(2,128)}) custom-call(s32[20]{0:T(128)} %concatenate.22.place, bf16[128,1536]{1,0:T(8,128)(2,1)} %refs_0_.5, bf16[128,1536]{1,0:T(8,128)(2,1)} %copy-done.11, bf16[64,1536]{1,0:T(8,128)(2,1)} %collective-permute-done.2.refs_0_.refs_2_, ...), custom_call_target="tpu_custom_call" | custom-call | flops 805306368 | bytes 5242880 | tf_op jit(solution)/shard_map/far_sums/pallas_call | solution.py:262
  47.7 2.2 %collective-permute-start.13 = (bf16[128,1664]{1,0:T(8,128)(2,1)}, bf16[128,1664]{1,0:T(8,128)(2,1)S(1)}, u32[]{:S(2)}, u32[]{:S(2)}) collective-permute-start(bf16[128,1664]{1,0:T(8,128)(2,1)} %get-tuple-element.86), channel_id=1, source_target_pairs={{0,8},{1,57},{8,0},{9,17},{16,24},{17,9},{24,16},{25,33},{32,40},{... | collective-permute-start | bytes 1277960 | tf_op jit(solution)/shard_map/ppermute | solution.py:63
  49.9 8.9 %rest_sums.1 = (f32[128,1536]{1,0:T(8,128)}, f32[128,128]{1,0:T(8,128)}, bf16[128,1664]{1,0:T(8,128)(2,1)}, f32[128,1536]{1,0:T(8,128)}, f32[128,128]{1,0:T(8,12...) custom-call(s32[20]{0:T(128)} %concatenate.22.place, ...), custom_call_target="tpu_custom_call" | custom-call | flops 2415919104 | bytes 10485760 | tf_op jit(solution)/shard_map/rest_sums/pallas_call | solution.py:278
  59.0 1.9 %collective-permute-start.16 = (bf16[128,1664]{1,0:T(8,128)(2,1)}, bf16[128,1664]{1,0:T(8,128)(2,1)S(1)}, u32[]{:S(2)}, u32[]{:S(2)}) collective-permute-start(bf16[128,1664]{1,0:T(8,128)(2,1)} %get-tuple-element.98), channel_id=1, source_target_pairs={{0,8},{1,57},{8,0},{9,17},{16,24},{17,9},{24,16},{25,33},{32,40},{... | collective-permute-start | bytes 1277960 | tf_op jit(solution)/shard_map/ppermute | solution.py:63
  61.2 1.4 collective-permute-start.15
  62.5 0.7 collective-permute-start.17
  63.3 3.8 %collective-permute-done.15.far = bf16[64,1664]{1,0:T(8,128)(2,1)S(1)} collective-permute-done((bf16[64,1664]{1,0:T(8,128)(2,1)S(1)}, bf16[64,1664]{1,0:T(8,128)(2,1)S(1)}, u32[]{:S(2)}, u32[]{:S(2)}) %collective-permute-start.15) | collective-permute-done | bytes 213024 | tf_op jit(solution)/shard_map/ppermute | solution.py:74
  67.2 1.1 copy-done.5
  68.3 0.8 copy-done.9
  69.2 0.3 add_side_step.2
  69.4 2.3 %collective-permute-done.16.got = bf16[128,1664]{1,0:T(8,128)(2,1)S(1)} collective-permute-done((bf16[128,1664]{1,0:T(8,128)(2,1)}, bf16[128,1664]{1,0:T(8,128)(2,1)S(1)}, u32[]{:S(2)}, u32[]{:S(2)}) %collective-permute-start.16) | collective-permute-done | bytes 426016 | tf_op jit(solution)/shard_map/ppermute | solution.py:63
  71.7 1.1 copy-done.4
  72.9 0.8 copy-done.8
  74.0 2.3 %collective-permute-done.18.got = bf16[128,1664]{1,0:T(8,128)(2,1)S(1)} collective-permute-done((bf16[128,1664]{1,0:T(8,128)(2,1)}, bf16[128,1664]{1,0:T(8,128)(2,1)S(1)}, u32[]{:S(2)}, u32[]{:S(2)}) %collective-permute-start.18) | collective-permute-done | bytes 426016 | tf_op jit(solution)/shard_map/ppermute | solution.py:63
  76.3 1.3 collective-permute-start.19
  77.6 0.7 collective-permute-start.20
  78.3 3.5 %fusion.24 = (f32[1024]{0:T(1024)S(1)}, f32[1024,1024]{1,0:T(8,128)S(1)}) fusion(bf16[1024,1536]{1,0:T(8,128)(2,1)S(1)} %copy-done, bf16[1024,1536]{1,0:T(8,128)(2,1)S(1)} %copy-done.1), kind=kOutput, calls=%fused_computation.49 | convolution fusion | flops 3223321600 | bytes 10489856 | tf_op jit(solution)/shard_map/dot_general | solution.py:413
  81.8 0.6 exponential_reduce_fusion
  82.5 5.0 %coarse_sums.1 = (f32[4,128,1536]{2,1,0:T(8,128)S(1)}, bf16[4,144,1536]{2,1,0:T(8,128)(2,1)S(1)}, f32[4,1,128]{2,1,0:T(1,128)S(1)}) custom-call(s32[20]{0:T(128)S(1)} %copy-done.10, f32[1024,1024]{1,0:T(8,128)S(1)} %get-tuple-element.129.s, f32[1,1024]{1,0:T(1,128)S(1)} %bitcast.39, f32[1,1024]{1,0:T(1,128)S(1)} %bitcast.40, bf16[1024,1536]{1,0:T(8,128)(2,1)S(1)} %copy-done.1), custom_call_target="tpu_custom_call" | custom-call | flops 3221225472 | bytes 12582912 | tf_op jit(solution)/shard_map/coarse_sums/pallas_call | solution.py:381
  87.6 0.4 add_own_step.1
  88.1 0.3 collective-permute-start.21
  88.4 2.9 %collective-permute-done.30 = bf16[4,144,1536]{2,1,0:T(8,128)(2,1)S(1)} collective-permute-done((bf16[4,144,1536]{2,1,0:T(8,128)(2,1)S(1)}, bf16[4,144,1536]{2,1,0:T(8,128)(2,1)S(1)}, u32[]{:S(2)}, u32[]{:S(2)}) %collective-permute-start.30) | collective-permute-done | bytes 1769504 | tf_op jit(solution)/shard_map/ppermute | solution.py:78
  91.3 0.5 convert_element_type.18
  91.8 0.6 slice_add_fusion
  92.5 0.7 collective-permute-start.31
  93.2 1.0 collective-permute-done.21.got
  94.4 4.1 %collective-permute-start.22 = (bf16[64,1664]{1,0:T(8,128)(2,1)S(1)}, bf16[64,1664]{1,0:T(8,128)(2,1)S(1)}, u32[]{:S(2)}, u32[]{:S(2)}) collective-permute-start(bf16[64,1664]{1,0:T(8,128)(2,1)S(1)} %add_half_step.1.own), channel_id=1, source_target_pairs={{0,24},{1,41},{8,48},{9,33},{16,40},{17,57},{24,0},{25,49},{32,56}... | collective-permute-start | bytes 638984 | tf_op jit(solution)/shard_map/ppermute | solution.py:63
  98.5 7.2 %collective-permute-done.22.got = bf16[64,1664]{1,0:T(8,128)(2,1)S(1)} collective-permute-done((bf16[64,1664]{1,0:T(8,128)(2,1)S(1)}, bf16[64,1664]{1,0:T(8,128)(2,1)S(1)}, u32[]{:S(2)}, u32[]{:S(2)}) %collective-permute-start.22) | collective-permute-done | bytes 213024 | tf_op jit(solution)/shard_map/ppermute | solution.py:63
  105.9 3.0 %collective-permute-start.23 = (bf16[64,1536]{1,0:T(8,128)(2,1)S(1)}, bf16[64,1536]{1,0:T(8,128)(2,1)S(1)}, u32[]{:S(2)}, u32[]{:S(2)}) collective-permute-start(bf16[64,1536]{1,0:T(8,128)(2,1)S(1)} %add_last_step.1), channel_id=1, source_target_pairs={{0,56},{1,9},{8,16},{9,1},{16,8},{17,25},{24,32},{25,17},{32,24},{... | collective-permute-start | bytes 589832 | tf_op jit(solution)/shard_map/ppermute | solution.py:63
  108.9 3.6 %collective-permute-done.23 = bf16[64,1536]{1,0:T(8,128)(2,1)S(1)} collective-permute-done((bf16[64,1536]{1,0:T(8,128)(2,1)S(1)}, bf16[64,1536]{1,0:T(8,128)(2,1)S(1)}, u32[]{:S(2)}, u32[]{:S(2)}) %collective-permute-start.23) | collective-permute-done | bytes 196640 | tf_op jit(solution)/shard_map/ppermute | solution.py:63
  112.6 5.0 %collective-permute-start.24 = (bf16[128,1536]{1,0:T(8,128)(2,1)S(1)}, bf16[128,1536]{1,0:T(8,128)(2,1)S(1)}, u32[]{:S(2)}, u32[]{:S(2)}) collective-permute-start(bf16[128,1536]{1,0:T(8,128)(2,1)S(1)} %pad_maximum_fusion.2.refs_0_), channel_id=1, source_target_pairs={{0,8},{1,57},{8,0},{9,17},{16,24},{17,9},{24,16},{25,33},{32,40},{... | collective-permute-start | bytes 1179656 | tf_op jit(solution)/shard_map/ppermute | solution.py:63
  117.5 1.7 %collective-permute-start.25 = (bf16[128,1536]{1,0:T(8,128)(2,1)S(1)}, bf16[128,1536]{1,0:T(8,128)(2,1)S(1)}, u32[]{:S(2)}, u32[]{:S(2)}) collective-permute-start(bf16[128,1536]{1,0:T(8,128)(2,1)S(1)} %pad_maximum_fusion.2.refs_0_), channel_id=1, source_target_pairs={{0,64},{64,128},{128,192},{192,0},{1,65},{65,129},{129,193},{193,1... | collective-permute-start | bytes 1179656 | tf_op jit(solution)/shard_map/ppermute | solution.py:74
  119.2 0.4 collective-permute-start.26
  120.4 2.9 %collective-permute-done.24.refs_1_ = bf16[128,1536]{1,0:T(8,128)(2,1)S(1)} collective-permute-done((bf16[128,1536]{1,0:T(8,128)(2,1)S(1)}, bf16[128,1536]{1,0:T(8,128)(2,1)S(1)}, u32[]{:S(2)}, u32[]{:S(2)}) %collective-permute-start.24) | collective-permute-done | bytes 393248 | tf_op jit(solution)/shard_map/ppermute | solution.py:63
  123.3 3.7 %collective-permute-done.25.refs_3_ = bf16[128,1536]{1,0:T(8,128)(2,1)S(1)} collective-permute-done((bf16[128,1536]{1,0:T(8,128)(2,1)S(1)}, bf16[128,1536]{1,0:T(8,128)(2,1)S(1)}, u32[]{:S(2)}, u32[]{:S(2)}) %collective-permute-start.25) | collective-permute-done | bytes 393248 | tf_op jit(solution)/shard_map/ppermute | solution.py:74
  127.0 3.4 %collective-permute-done.26.refs_2_ = bf16[128,1536]{1,0:T(8,128)(2,1)S(1)} collective-permute-done((bf16[128,1536]{1,0:T(8,128)(2,1)S(1)}, bf16[128,1536]{1,0:T(8,128)(2,1)S(1)}, u32[]{:S(2)}, u32[]{:S(2)}) %collective-permute-start.26) | collective-permute-done | bytes 393248 | tf_op jit(solution)/shard_map/ppermute | solution.py:74
  130.5 0.4 collective-permute-start.27
  130.9 1.6 %collective-permute-start.33 = (bf16[128,1536]{1,0:T(8,128)(2,1)S(1)}, bf16[128,1536]{1,0:T(8,128)(2,1)S(1)}, u32[]{:S(2)}, u32[]{:S(2)}) collective-permute-start(bf16[128,1536]{1,0:T(8,128)(2,1)S(1)} %collective-permute-done.24.refs_1_), channel_id=1, source_target_pairs={{0,64},{64,128},{128,192},{192,0},{1,65},{65,129},{129,193},{193,1... | collective-permute-start | bytes 1179656 | tf_op jit(solution)/shard_map/ppermute | solution.py:74
  132.5 0.9 collective-permute-start.28
  133.4 1.8 %put_rows.2.refs_4_ = bf16[1024,1536]{1,0:T(8,128)(2,1)} custom-call(s32[20]{0:T(128)S(1)} %copy-done.10, bf16[128,1536]{1,0:T(8,128)(2,1)S(1)} %pad_maximum_fusion.2.refs_0_, bf16[128,1536]{1,0:T(8,128)(2,1)S(1)} %collective-permute-done.24.refs_1_, bf16[128,1536]{1,0:T(8,128)(2,1)S(1)} %collective-permute-done.26.refs_2_, ...), custom_call_target="tpu_custom_call" | custom-call | bytes 3145728 | tf_op jit(solution)/shard_map/put_rows/pallas_call | solution.py:106
  135.2 6.8 %collective-permute-done.27.refs_0_ = bf16[128,1536]{1,0:T(8,128)(2,1)S(1)} collective-permute-done((bf16[128,1536]{1,0:T(8,128)(2,1)S(1)}, bf16[128,1536]{1,0:T(8,128)(2,1)S(1)}, u32[]{:S(2)}, u32[]{:S(2)}) %collective-permute-start.27) | collective-permute-done | bytes 393248 | tf_op jit(solution)/shard_map/ppermute | solution.py:74
  142.0 0.4 collective-permute-start.29
  142.5 0.9 fusion.3
  143.4 6.4 %collective-permute-done.29.refs_2_ = bf16[128,1536]{1,0:T(8,128)(2,1)S(1)} collective-permute-done((bf16[128,1536]{1,0:T(8,128)(2,1)S(1)}, bf16[128,1536]{1,0:T(8,128)(2,1)S(1)}, u32[]{:S(2)}, u32[]{:S(2)}) %collective-permute-start.29) | collective-permute-done | bytes 393248 | tf_op jit(solution)/shard_map/ppermute | solution.py:74
  149.8 1.8 %put_rows.3 = bf16[1024,1536]{1,0:T(8,128)(2,1)} custom-call(s32[20]{0:T(128)S(1)} %copy-done.10, bf16[128,1536]{1,0:T(8,128)(2,1)S(1)} %collective-permute-done.27.refs_0_, bf16[128,1536]{1,0:T(8,128)(2,1)S(1)} %collective-permute-done.28.refs_1_, bf16[128,1536]{1,0:T(8,128)(2,1)S(1)} %collective-permute-done.29.refs_2_, ...), custom_call_target="tpu_custom_call", output_to_operand_aliasing={{}: (5, {})} | custom-call | bytes 3145728 | tf_op jit(solution)/shard_map/put_rows/pallas_call | solution.py:106
  (79 shorter events, 2.7 us)
Async XLA Ops:
  0.6 77.7 %copy-start = (bf16[1024,1536]{1,0:T(8,128)(2,1)S(1)}, bf16[1024,1536]{1,0:T(8,128)(2,1)}, u32[]{:S(2)}) copy-start(bf16[1024,1536]{1,0:T(8,128)(2,1)} %param.7) | copy-start | bytes 9437188
  0.6 13.2 %collective-permute-start = (bf16[128,1536]{1,0:T(8,128)(2,1)}, bf16[128,1536]{1,0:T(8,128)(2,1)S(1)}, u32[]{:S(2)}, u32[]{:S(2)}) collective-permute-start(bf16[128,1536]{1,0:T(8,128)(2,1)} %refs_0_.5), channel_id=1, source_target_pairs={{0,1},{1,0},{2,3},{3,2},{4,5},{5,4},{6,7},{7,6},{8,9},{9,8},{10,11... | collective-permute-start | bytes 1179656 | tf_op jit(solution)/shard_map/ppermute | solution.py:78
  1.9 8.1 %collective-permute-start.3 = (bf16[64,1536]{1,0:T(8,128)(2,1)S(1)}, bf16[64,1536]{1,0:T(8,128)(2,1)S(1)}, u32[]{:S(2)}, u32[]{:S(2)}) collective-permute-start(bf16[64,1536]{1,0:T(8,128)(2,1)S(1)} %get-tuple-element.123), channel_id=1, source_target_pairs={{0,6},{2,0},{4,2},{6,4},{1,7},{3,1},{5,3},{7,5},{8,14},{10,8},{12,... | collective-permute-start | bytes 589832 | tf_op jit(solution)/shard_map/ppermute | solution.py:74
  4.8 9.1 %collective-permute-start.6 = (bf16[64,1536]{1,0:T(8,128)(2,1)S(1)}, bf16[64,1536]{1,0:T(8,128)(2,1)}, u32[]{:S(2)}, u32[]{:S(2)}) collective-permute-start(bf16[64,1536]{1,0:T(8,128)(2,1)S(1)} %get-tuple-element.122), channel_id=1, source_target_pairs={{0,2},{2,4},{4,6},{6,0},{1,3},{3,5},{5,7},{7,1},{8,10},{10,12},{12... | collective-permute-start | bytes 589832 | tf_op jit(solution)/shard_map/ppermute | solution.py:74
  4.8 15.0 %collective-permute-start.1 = (bf16[64,1536]{1,0:T(8,128)(2,1)S(1)}, bf16[64,1536]{1,0:T(8,128)(2,1)}, u32[]{:S(2)}, u32[]{:S(2)}) collective-permute-start(bf16[64,1536]{1,0:T(8,128)(2,1)S(1)} %get-tuple-element.123), channel_id=1, source_target_pairs={{0,2},{2,4},{4,6},{6,0},{1,3},{3,5},{5,7},{7,1},{8,10},{10,12},{12... | collective-permute-start | bytes 589832 | tf_op jit(solution)/shard_map/ppermute | solution.py:74
  5.5 14.3 %collective-permute-start.2 = (bf16[64,1536]{1,0:T(8,128)(2,1)S(1)}, bf16[64,1536]{1,0:T(8,128)(2,1)}, u32[]{:S(2)}, u32[]{:S(2)}) collective-permute-start(bf16[64,1536]{1,0:T(8,128)(2,1)S(1)} %get-tuple-element.122), channel_id=1, source_target_pairs={{0,6},{2,0},{4,2},{6,4},{1,7},{3,1},{5,3},{7,5},{8,14},{10,8},{12,... | collective-permute-start | bytes 589832 | tf_op jit(solution)/shard_map/ppermute | solution.py:74
  10.0 12.3 %copy-start.15 = (bf16[64,1536]{1,0:T(8,128)(2,1)}, bf16[64,1536]{1,0:T(8,128)(2,1)S(1)}, u32[]{:S(2)}) copy-start(bf16[64,1536]{1,0:T(8,128)(2,1)S(1)} %collective-permute-done.3.refs_1_.refs_3_) | copy-start | bytes 589828
  10.0 10.4 %collective-permute-start.5 = (bf16[64,1536]{1,0:T(8,128)(2,1)S(1)}, bf16[64,1536]{1,0:T(8,128)(2,1)S(1)}, u32[]{:S(2)}, u32[]{:S(2)}) collective-permute-start(bf16[64,1536]{1,0:T(8,128)(2,1)S(1)} %collective-permute-done.3.refs_1_.refs_3_), channel_id=1, source_target_pairs={{0,1},{1,0},{2,3},{3,2},{4,5},{5,4},{6,7},{7,6},{8,9},{9,8},{10,11... | collective-permute-start | bytes 589832 | tf_op jit(solution)/shard_map/ppermute | solution.py:78
  13.8 8.5 %collective-permute-start.10 = (bf16[64,1536]{1,0:T(8,128)(2,1)S(1)}, bf16[64,1536]{1,0:T(8,128)(2,1)}, u32[]{:S(2)}, u32[]{:S(2)}) collective-permute-start(bf16[64,1536]{1,0:T(8,128)(2,1)S(1)} %collective-permute-done.3.refs_1_.refs_3_), channel_id=1, source_target_pairs={{0,6},{2,0},{4,2},{6,4},{1,7},{3,1},{5,3},{7,5},{8,14},{10,8},{12,... | collective-permute-start | bytes 589832 | tf_op jit(solution)/shard_map/ppermute | solution.py:74
  13.8 2.0 %copy-start.11 = (bf16[128,1536]{1,0:T(8,128)(2,1)}, bf16[128,1536]{1,0:T(8,128)(2,1)S(1)}, u32[]{:S(2)}) copy-start(bf16[128,1536]{1,0:T(8,128)(2,1)S(1)} %collective-permute-done.refs_1_) | copy-start | bytes 1179652
  13.8 8.4 %collective-permute-start.9 = (bf16[64,1536]{1,0:T(8,128)(2,1)}, bf16[64,1536]{1,0:T(8,128)(2,1)}, u32[]{:S(2)}, u32[]{:S(2)}) collective-permute-start(bf16[64,1536]{1,0:T(8,128)(2,1)} %collective-permute-done.6.refs_4_.refs_6_), channel_id=1, source_target_pairs={{0,2},{2,4},{4,6},{6,0},{1,3},{3,5},{5,7},{7,1},{8,10},{10,12},{12... | collective-permute-start | bytes 589832 | tf_op jit(solution)/shard_map/ppermute | solution.py:74
  19.8 3.1 %collective-permute-start.7 = (bf16[64,1536]{1,0:T(8,128)(2,1)}, bf16[64,1536]{1,0:T(8,128)(2,1)}, u32[]{:S(2)}, u32[]{:S(2)}) collective-permute-start(bf16[64,1536]{1,0:T(8,128)(2,1)} %collective-permute-done.6.refs_4_.refs_6_), channel_id=1, source_target_pairs={{0,1},{1,0},{2,3},{3,2},{4,5},{5,4},{6,7},{7,6},{8,9},{9,8},{10,11... | collective-permute-start | bytes 589832 | tf_op jit(solution)/shard_map/ppermute | solution.py:78
  19.9 3.0 %collective-permute-start.4 = (bf16[64,1536]{1,0:T(8,128)(2,1)}, bf16[64,1536]{1,0:T(8,128)(2,1)}, u32[]{:S(2)}, u32[]{:S(2)}) collective-permute-start(bf16[64,1536]{1,0:T(8,128)(2,1)} %collective-permute-done.2.refs_0_.refs_2_), channel_id=1, source_target_pairs={{0,1},{1,0},{2,3},{3,2},{4,5},{5,4},{6,7},{7,6},{8,9},{9,8},{10,11... | collective-permute-start | bytes 589832 | tf_op jit(solution)/shard_map/ppermute | solution.py:78
  20.4 1.9 %copy-start.16 = (bf16[64,1536]{1,0:T(8,128)(2,1)}, bf16[64,1536]{1,0:T(8,128)(2,1)S(1)}, u32[]{:S(2)}) copy-start(bf16[64,1536]{1,0:T(8,128)(2,1)S(1)} %collective-permute-done.5.refs_3_.refs_5_) | copy-start | bytes 589828
  20.4 2.5 %collective-permute-start.8 = (bf16[64,1536]{1,0:T(8,128)(2,1)}, bf16[64,1536]{1,0:T(8,128)(2,1)}, u32[]{:S(2)}, u32[]{:S(2)}) collective-permute-start(bf16[64,1536]{1,0:T(8,128)(2,1)} %collective-permute-done.1.refs_5_.refs_7_), channel_id=1, source_target_pairs={{0,1},{1,0},{2,3},{3,2},{4,5},{5,4},{6,7},{7,6},{8,9},{9,8},{10,11... | collective-permute-start | bytes 589832 | tf_op jit(solution)/shard_map/ppermute | solution.py:78
  22.3 6.1 %collective-permute-start.11 = (bf16[64,1536]{1,0:T(8,128)(2,1)}, bf16[64,1536]{1,0:T(8,128)(2,1)S(1)}, u32[]{:S(2)}, u32[]{:S(2)}) collective-permute-start(bf16[64,1536]{1,0:T(8,128)(2,1)} %collective-permute-done.9.refs_0_.refs_10_), channel_id=1, source_target_pairs={{0,1},{1,0},{2,3},{3,2},{4,5},{5,4},{6,7},{7,6},{8,9},{9,8},{10,11... | collective-permute-start | bytes 589832 | tf_op jit(solution)/shard_map/ppermute | solution.py:78
  22.3 6.1 %collective-permute-start.12 = (bf16[64,1536]{1,0:T(8,128)(2,1)}, bf16[64,1536]{1,0:T(8,128)(2,1)S(1)}, u32[]{:S(2)}, u32[]{:S(2)}) collective-permute-start(bf16[64,1536]{1,0:T(8,128)(2,1)} %collective-permute-done.10.refs_1_.refs_11_), channel_id=1, source_target_pairs={{0,1},{1,0},{2,3},{3,2},{4,5},{5,4},{6,7},{7,6},{8,9},{9,8},{10,11... | collective-permute-start | bytes 589832 | tf_op jit(solution)/shard_map/ppermute | solution.py:78
  28.4 0.7 copy-start.12
  28.4 0.7 copy-start.13
  33.1 8.9 %all-to-all-start = ((f32[8,16,128]{2,1,0:T(8,128)}), f32[8,16,128]{2,1,0:T(8,128)S(1)}, u32[]{:S(2)}, u32[]{:S(2)}) async-start(f32[8,16,128]{2,1,0:T(8,128)} %get-tuple-element.75), calls=%async_computation | async-start | bytes 131072 | tf_op jit(solution)/shard_map/all_to_all | solution.py:442
  42.0 0.6 copy-start.14
  47.7 11.1 %collective-permute-start.13 = (bf16[128,1664]{1,0:T(8,128)(2,1)}, bf16[128,1664]{1,0:T(8,128)(2,1)S(1)}, u32[]{:S(2)}, u32[]{:S(2)}) collective-permute-start(bf16[128,1664]{1,0:T(8,128)(2,1)} %get-tuple-element.86), channel_id=1, source_target_pairs={{0,8},{1,57},{8,0},{9,17},{16,24},{17,9},{24,16},{25,33},{32,40},{... | collective-permute-start | bytes 1277960 | tf_op jit(solution)/shard_map/ppermute | solution.py:63
  49.9 11.1 %copy-start.3 = (f32[128,1536]{1,0:T(8,128)S(1)}, f32[128,1536]{1,0:T(8,128)}, u32[]{:S(2)}) copy-start(f32[128,1536]{1,0:T(8,128)} %get-tuple-element.92.keep) | copy-start | bytes 2359300
  49.9 11.1 %copy-start.7 = (f32[128,128]{1,0:T(8,128)S(1)}, f32[128,128]{1,0:T(8,128)}, u32[]{:S(2)}) copy-start(f32[128,128]{1,0:T(8,128)} %get-tuple-element.93.mass) | copy-start | bytes 196612
  58.7 19.6 %copy-start.1 = (bf16[1024,1536]{1,0:T(8,128)(2,1)S(1)}, bf16[1024,1536]{1,0:T(8,128)(2,1)}, u32[]{:S(2)}) copy-start(bf16[1024,1536]{1,0:T(8,128)(2,1)} %fine.1) | copy-start | bytes 9437188
  58.8 8.4 %collective-permute-start.14 = (bf16[128,1664]{1,0:T(8,128)(2,1)}, bf16[128,1664]{1,0:T(8,128)(2,1)S(1)}, u32[]{:S(2)}, u32[]{:S(2)}) collective-permute-start(bf16[128,1664]{1,0:T(8,128)(2,1)} %get-tuple-element.91), channel_id=1, source_target_pairs={{0,8},{1,57},{8,0},{9,17},{16,24},{17,9},{24,16},{25,33},{32,40},{... | collective-permute-start | bytes 1277960 | tf_op jit(solution)/shard_map/ppermute | solution.py:63
  59.0 12.8 %collective-permute-start.16 = (bf16[128,1664]{1,0:T(8,128)(2,1)}, bf16[128,1664]{1,0:T(8,128)(2,1)S(1)}, u32[]{:S(2)}, u32[]{:S(2)}) collective-permute-start(bf16[128,1664]{1,0:T(8,128)(2,1)} %get-tuple-element.98), channel_id=1, source_target_pairs={{0,8},{1,57},{8,0},{9,17},{16,24},{17,9},{24,16},{25,33},{32,40},{... | collective-permute-start | bytes 1277960 | tf_op jit(solution)/shard_map/ppermute | solution.py:63
  60.9 15.4 %collective-permute-start.18 = (bf16[128,1664]{1,0:T(8,128)(2,1)}, bf16[128,1664]{1,0:T(8,128)(2,1)S(1)}, u32[]{:S(2)}, u32[]{:S(2)}) collective-permute-start(bf16[128,1664]{1,0:T(8,128)(2,1)} %get-tuple-element.100), channel_id=1, source_target_pairs={{0,8},{1,57},{8,0},{9,17},{16,24},{17,9},{24,16},{25,33},{32,40},{... | collective-permute-start | bytes 1277960 | tf_op jit(solution)/shard_map/ppermute | solution.py:63
  61.2 5.9 %collective-permute-start.15 = (bf16[64,1664]{1,0:T(8,128)(2,1)S(1)}, bf16[64,1664]{1,0:T(8,128)(2,1)S(1)}, u32[]{:S(2)}, u32[]{:S(2)}) collective-permute-start(bf16[64,1664]{1,0:T(8,128)(2,1)S(1)} %get-tuple-element.95), channel_id=1, source_target_pairs={{0,64},{64,128},{128,192},{192,0},{1,65},{65,129},{129,193},{193,1... | collective-permute-start | bytes 638984 | tf_op jit(solution)/shard_map/ppermute | solution.py:74
  62.5 6.9 %collective-permute-start.17 = (bf16[64,1664]{1,0:T(8,128)(2,1)S(1)}, bf16[64,1664]{1,0:T(8,128)(2,1)S(1)}, u32[]{:S(2)}, u32[]{:S(2)}) collective-permute-start(bf16[64,1664]{1,0:T(8,128)(2,1)S(1)} %get-tuple-element.99), channel_id=1, source_target_pairs={{0,192},{64,0},{128,64},{192,128},{1,193},{65,1},{129,65},{193,129... | collective-permute-start | bytes 638984 | tf_op jit(solution)/shard_map/ppermute | solution.py:74
  67.2 1.1 copy-start.5
  68.3 0.8 copy-start.9
  71.7 1.1 copy-start.4
  72.9 0.8 copy-start.8
  76.3 11.2 %collective-permute-start.19 = (bf16[128,1664]{1,0:T(8,128)(2,1)S(1)}, bf16[128,1664]{1,0:T(8,128)(2,1)S(1)}, u32[]{:S(2)}, u32[]{:S(2)}) collective-permute-start(bf16[128,1664]{1,0:T(8,128)(2,1)S(1)} %add_side_step.2), channel_id=1, source_target_pairs={{0,64},{64,128},{128,192},{192,0},{1,65},{65,129},{129,193},{193,1... | collective-permute-start | bytes 1277960 | tf_op jit(solution)/shard_map/ppermute | solution.py:74
  77.6 9.9 %collective-permute-start.20 = (bf16[128,1664]{1,0:T(8,128)(2,1)S(1)}, bf16[128,1664]{1,0:T(8,128)(2,1)S(1)}, u32[]{:S(2)}, u32[]{:S(2)}) collective-permute-start(bf16[128,1664]{1,0:T(8,128)(2,1)S(1)} %add_side_step.3), channel_id=1, source_target_pairs={{0,192},{64,0},{128,64},{192,128},{1,193},{65,1},{129,65},{193,129... | collective-permute-start | bytes 1277960 | tf_op jit(solution)/shard_map/ppermute | solution.py:74
  81.8 0.6 copy-start.10
  82.4 5.2 %copy-start.2 = (f32[128,1536]{1,0:T(8,128)S(1)}, f32[128,1536]{1,0:T(8,128)}, u32[]{:S(2)}) copy-start(f32[128,1536]{1,0:T(8,128)} %get-tuple-element.87.keep) | copy-start | bytes 2359300
  82.5 5.2 %copy-start.6 = (f32[128,128]{1,0:T(8,128)S(1)}, f32[128,128]{1,0:T(8,128)}, u32[]{:S(2)}) copy-start(f32[128,128]{1,0:T(8,128)} %get-tuple-element.88.mass) | copy-start | bytes 196612
  87.5 3.8 %collective-permute-start.30 = (bf16[4,144,1536]{2,1,0:T(8,128)(2,1)S(1)}, bf16[4,144,1536]{2,1,0:T(8,128)(2,1)S(1)}, u32[]{:S(2)}, u32[]{:S(2)}) collective-permute-start(bf16[4,144,1536]{2,1,0:T(8,128)(2,1)S(1)} %get-tuple-element.116), channel_id=1, source_target_pairs={{0,1},{1,0},{2,3},{3,2},{4,5},{5,4},{6,7},{7,6},{8,9},{9,8},{10,11... | collective-permute-start | bytes 5308424 | tf_op jit(solution)/shard_map/ppermute | solution.py:78
  88.1 6.2 %collective-permute-start.21 = (bf16[64,1664]{1,0:T(8,128)(2,1)S(1)}, bf16[64,1664]{1,0:T(8,128)(2,1)S(1)}, u32[]{:S(2)}, u32[]{:S(2)}) collective-permute-start(bf16[64,1664]{1,0:T(8,128)(2,1)S(1)} %get-tuple-element.112), channel_id=1, source_target_pairs={{0,56},{1,9},{8,16},{9,1},{16,8},{17,25},{24,32},{25,17},{32,24},{... | collective-permute-start | bytes 638984 | tf_op jit(solution)/shard_map/ppermute | solution.py:63
  92.5 27.0 %collective-permute-start.31 = (bf16[264,1536]{1,0:T(8,128)(2,1)S(1)}, bf16[264,1536]{1,0:T(8,128)(2,1)S(1)}, u32[]{:S(2)}, u32[]{:S(2)}) collective-permute-start(bf16[264,1536]{1,0:T(8,128)(2,1)S(1)} %pad_maximum_fusion), channel_id=1, source_target_pairs={{0,2},{1,7},{2,0},{3,5},{4,6},{5,3},{6,4},{7,1},{8,10},{9,15},{10,... | collective-permute-start | bytes 2433032 | tf_op jit(solution)/shard_map/ppermute | solution.py:67
  94.4 11.3 %collective-permute-start.22 = (bf16[64,1664]{1,0:T(8,128)(2,1)S(1)}, bf16[64,1664]{1,0:T(8,128)(2,1)S(1)}, u32[]{:S(2)}, u32[]{:S(2)}) collective-permute-start(bf16[64,1664]{1,0:T(8,128)(2,1)S(1)} %add_half_step.1.own), channel_id=1, source_target_pairs={{0,24},{1,41},{8,48},{9,33},{16,40},{17,57},{24,0},{25,49},{32,56}... | collective-permute-start | bytes 638984 | tf_op jit(solution)/shard_map/ppermute | solution.py:63
  105.9 6.6 %collective-permute-start.23 = (bf16[64,1536]{1,0:T(8,128)(2,1)S(1)}, bf16[64,1536]{1,0:T(8,128)(2,1)S(1)}, u32[]{:S(2)}, u32[]{:S(2)}) collective-permute-start(bf16[64,1536]{1,0:T(8,128)(2,1)S(1)} %add_last_step.1), channel_id=1, source_target_pairs={{0,56},{1,9},{8,16},{9,1},{16,8},{17,25},{24,32},{25,17},{32,24},{... | collective-permute-start | bytes 589832 | tf_op jit(solution)/shard_map/ppermute | solution.py:63
  112.6 10.7 %collective-permute-start.24 = (bf16[128,1536]{1,0:T(8,128)(2,1)S(1)}, bf16[128,1536]{1,0:T(8,128)(2,1)S(1)}, u32[]{:S(2)}, u32[]{:S(2)}) collective-permute-start(bf16[128,1536]{1,0:T(8,128)(2,1)S(1)} %pad_maximum_fusion.2.refs_0_), channel_id=1, source_target_pairs={{0,8},{1,57},{8,0},{9,17},{16,24},{17,9},{24,16},{25,33},{32,40},{... | collective-permute-start | bytes 1179656 | tf_op jit(solution)/shard_map/ppermute | solution.py:63
  117.5 9.5 %collective-permute-start.25 = (bf16[128,1536]{1,0:T(8,128)(2,1)S(1)}, bf16[128,1536]{1,0:T(8,128)(2,1)S(1)}, u32[]{:S(2)}, u32[]{:S(2)}) collective-permute-start(bf16[128,1536]{1,0:T(8,128)(2,1)S(1)} %pad_maximum_fusion.2.refs_0_), channel_id=1, source_target_pairs={{0,64},{64,128},{128,192},{192,0},{1,65},{65,129},{129,193},{193,1... | collective-permute-start | bytes 1179656 | tf_op jit(solution)/shard_map/ppermute | solution.py:74
  119.2 11.3 %collective-permute-start.26 = (bf16[128,1536]{1,0:T(8,128)(2,1)S(1)}, bf16[128,1536]{1,0:T(8,128)(2,1)S(1)}, u32[]{:S(2)}, u32[]{:S(2)}) collective-permute-start(bf16[128,1536]{1,0:T(8,128)(2,1)S(1)} %pad_maximum_fusion.2.refs_0_), channel_id=1, source_target_pairs={{0,192},{64,0},{128,64},{192,128},{1,193},{65,1},{129,65},{193,129... | collective-permute-start | bytes 1179656 | tf_op jit(solution)/shard_map/ppermute | solution.py:74
  120.3 22.1 %collective-permute-start.32 = (bf16[136,1536]{1,0:T(8,128)(2,1)S(1)}, bf16[136,1536]{1,0:T(8,128)(2,1)S(1)}, u32[]{:S(2)}, u32[]{:S(2)}) collective-permute-start(bf16[136,1536]{1,0:T(8,128)(2,1)S(1)} %pad_maximum_fusion.1), channel_id=1, source_target_pairs={{0,6},{1,3},{2,4},{3,1},{4,2},{5,7},{6,0},{7,5},{8,14},{9,11},{10,... | collective-permute-start | bytes 1253384 | tf_op jit(solution)/shard_map/ppermute | solution.py:67
  130.5 11.6 %collective-permute-start.27 = (bf16[128,1536]{1,0:T(8,128)(2,1)S(1)}, bf16[128,1536]{1,0:T(8,128)(2,1)S(1)}, u32[]{:S(2)}, u32[]{:S(2)}) collective-permute-start(bf16[128,1536]{1,0:T(8,128)(2,1)S(1)} %collective-permute-done.24.refs_1_), channel_id=1, source_target_pairs={{0,192},{64,0},{128,64},{192,128},{1,193},{65,1},{129,65},{193,129... | collective-permute-start | bytes 1179656 | tf_op jit(solution)/shard_map/ppermute | solution.py:74
  130.9 18.9 %collective-permute-start.33 = (bf16[128,1536]{1,0:T(8,128)(2,1)S(1)}, bf16[128,1536]{1,0:T(8,128)(2,1)S(1)}, u32[]{:S(2)}, u32[]{:S(2)}) collective-permute-start(bf16[128,1536]{1,0:T(8,128)(2,1)S(1)} %collective-permute-done.24.refs_1_), channel_id=1, source_target_pairs={{0,64},{64,128},{128,192},{192,0},{1,65},{65,129},{129,193},{193,1... | collective-permute-start | bytes 1179656 | tf_op jit(solution)/shard_map/ppermute | solution.py:74
  132.5 17.3 %collective-permute-start.28 = (bf16[128,1536]{1,0:T(8,128)(2,1)S(1)}, bf16[128,1536]{1,0:T(8,128)(2,1)S(1)}, u32[]{:S(2)}, u32[]{:S(2)}) collective-permute-start(bf16[128,1536]{1,0:T(8,128)(2,1)S(1)} %collective-permute-done.25.refs_3_), channel_id=1, source_target_pairs={{0,64},{64,128},{128,192},{192,0},{1,65},{65,129},{129,193},{193,1... | collective-permute-start | bytes 1179656 | tf_op jit(solution)/shard_map/ppermute | solution.py:74
  142.0 7.8 %collective-permute-start.29 = (bf16[128,1536]{1,0:T(8,128)(2,1)S(1)}, bf16[128,1536]{1,0:T(8,128)(2,1)S(1)}, u32[]{:S(2)}, u32[]{:S(2)}) collective-permute-start(bf16[128,1536]{1,0:T(8,128)(2,1)S(1)} %collective-permute-done.27.refs_0_), channel_id=1, source_target_pairs={{0,192},{64,0},{128,64},{192,128},{1,193},{65,1},{129,65},{193,129... | collective-permute-start | bytes 1179656 | tf_op jit(solution)/shard_map/ppermute | solution.py:74

commit v3 on v2

--- a/solution.py
+++ b/solution.py
@@ -74,6 +74,11 @@
     return lax.ppermute(x, axis, [(i, (i + k) % n) for i in range(n)])
 
 
+def forward(x, k):
+    pairs = [(y * 2 + c, (y + k * (1 - 2 * c)) % 4 * 2 + c) for y in range(4) for c in range(2)]
+    return lax.ppermute(x, ("y", "c"), pairs)
+
+
 def swap_core(x):
     return lax.ppermute(x, "c", [(0, 1), (1, 0)])
 
@@ -92,7 +97,7 @@
     copies = []
     for i, (part, (r, h)) in enumerate(zip(parts, rs)):
         for j in range(4):
-            row = lax.rem(place[0] + r, 4) * TILE + place[4 + 4 * h + j] * BLOCK
+            row = lax.rem(place[0] + r + 2 * (r % 2) * place[2], 4) * TILE + place[4 + 4 * h + j] * BLOCK
             rows = out.at[pl.ds(pl.multiple_of(row, BLOCK), BLOCK)]
             copies.append(pltpu.make_async_copy(part.at[pl.ds(j * BLOCK, BLOCK)], rows, sems.at[4 * i + j]))
     for copy in copies:
@@ -226,28 +231,40 @@
     send[:, D:] = jnp.where(lane < 64, high, mass[128:] - high).astype(BF16)
 
 
-def far_kernel(n, place, *refs):
+def first_kernel(n, place, *refs):
     es, ps, tops, stats = refs[:n], refs[n : n + 3], refs[n + 3 : n + 6], refs[n + 6]
-    keep, keep_mass, send, factors = refs[n + 7 :]
-    find_factors(place, tops, stats, factors)
-    out, mass = tile_sums(place, lax.rem(place[0] + 2, 4), factors, ps, es)
-    put_halves(out, mass, keep, keep_mass, send)
-
-
-def rest_kernel(n, place, *refs):
-    es, ps, factors = refs[:n], refs[n : n + 3], refs[n + 3]
-    outs = refs[n + 4 :]
+    outs, factors = refs[n + 7 : n + 13], refs[n + 13]
     t = pl.program_id(0)
-    out, mass = tile_sums(place, rest_tile(t, place), factors, ps, es)
-    for i in range(3):
+
+    @pl.when(t == 0)
+    def _():
+        find_factors(place, tops, stats, factors)
+
+    out, mass = tile_sums(place, first_tile(t, place), factors, ps, es)
+    for i in range(2):
 
         @pl.when(t == i)
         def _():
             put_halves(out, mass, *outs[3 * i : 3 * i + 3])
 
 
+def rest_kernel(n, place, *refs):
+    es, ps, factors, outs = refs[:n], refs[n : n + 3], refs[n + 3], refs[n + 4 :]
+    t = pl.program_id(0)
+    out, mass = tile_sums(place, rest_tile(t, place), factors, ps, es)
+    for i in range(2):
+
+        @pl.when(t == i)
+        def _():
+            put_halves(out, mass, *outs[3 * i : 3 * i + 3])
+
+
+def first_tile(t, place):
+    return lax.rem(place[0] + 2 - t, 4)
+
+
 def rest_tile(t, place):
-    return lax.rem(place[0] + jnp.where(t == 0, 1, jnp.where(t == 1, 3, 0)), 4)
+    return lax.rem(place[0] + 3 + t, 4)
 
 
 def fine_sums(place, es, ps, tops, stats):
@@ -259,38 +276,38 @@
     ]
     specs = [whole(*half.shape) for half in halves]
     params = pltpu.CompilerParams(vmem_limit_bytes=58 << 20)
-    *far, factors = pl.pallas_call(
-        functools.partial(far_kernel, len(es)),
+    *first, factors = pl.pallas_call(
+        functools.partial(first_kernel, len(es)),
         grid_spec=pltpu.PrefetchScalarGridSpec(
             num_scalar_prefetch=1,
-            grid=(1,),
+            grid=(2,),
             in_specs=[whole(*e.shape) for e in es]
-            + [pl.BlockSpec((TILE, p.shape[1]), lambda t, s: (lax.rem(s[0] + 2, 4), 0)) for p in ps]
+            + [pl.BlockSpec((TILE, p.shape[1]), lambda t, s: (first_tile(t, s), 0)) for p in ps]
             + [whole(*top.shape) for top in tops]
             + [whole(8, 16, ROWS)],
-            out_specs=specs + [whole(2, 1024)],
+            out_specs=specs * 2 + [whole(2, 1024)],
         ),
-        out_shape=halves + [jax.ShapeDtypeStruct((2, 1024), F32)],
+        out_shape=halves * 2 + [jax.ShapeDtypeStruct((2, 1024), F32)],
         compiler_params=params,
-        cost_estimate=pl.CostEstimate(flops=2 * 256 * 1024 * D, bytes_accessed=5 << 20, transcendentals=0),
-        name="far_sums",
+        cost_estimate=pl.CostEstimate(flops=2 * 512 * 1024 * D, bytes_accessed=5 << 20, transcendentals=0),
+        name="first_sums",
     )(place, *es, *ps, *tops, stats)
     rest = pl.pallas_call(
         functools.partial(rest_kernel, len(es)),
         grid_spec=pltpu.PrefetchScalarGridSpec(
             num_scalar_prefetch=1,
-            grid=(3,),
+            grid=(2,),
             in_specs=[whole(*e.shape) for e in es]
             + [pl.BlockSpec((TILE, p.shape[1]), lambda t, s: (rest_tile(t, s), 0)) for p in ps]
             + [whole(2, 1024)],
-            out_specs=specs * 3,
+            out_specs=specs * 2,
         ),
-        out_shape=halves * 3,
+        out_shape=halves * 2,
         compiler_params=params,
-        cost_estimate=pl.CostEstimate(flops=2 * 768 * 1024 * D, bytes_accessed=10 << 20, transcendentals=0),
+        cost_estimate=pl.CostEstimate(flops=2 * 512 * 1024 * D, bytes_accessed=10 << 20, transcendentals=0),
         name="rest_sums",
     )(place, *es, *ps, factors)
-    return far, rest[:3], rest[3:6], rest[6:]
+    return first[:3], first[3:], rest[:3], rest[3:]
 
 
 def load(ref, at, n):
@@ -445,15 +462,14 @@
     )
 
     sent = lambda n: ((n, WIDE), BF16)
-    got = exchange(far[2], 0)
-    rest, got = lax.optimization_barrier(((up, down, own), got))
-    up, down, own = rest
-    got_up, got_down, got_own = (exchange(v[2], 0) for v in rest)
+    got, got_up = exchange(far[2], 0), exchange(up[2], 0)
+    (down, own), got = lax.optimization_barrier(((down, own), got))
+    got_down, got_own = exchange(down[2], 0), exchange(own[2], 0)
     far0, far1 = step(far_step, [far[0], far[1], got], [sent(64), sent(64)])
     far0, far1 = shift(far0, "y", 1), shift(far1, "y", -1)
     up = step(functools.partial(side_step, 0), [up[0], up[1], got_up, far0], [sent(128)])
     down = step(functools.partial(side_step, 64), [down[0], down[1], got_down, far1], [sent(128)])
-    up, down, got_own, coarse = lax.optimization_barrier((up, down, got_own, coarse))
+    got_own, coarse = lax.optimization_barrier((got_own, coarse))
     c_sums = coarse_sums(place, *coarse_scores(fine, coarse), fine)
     up, down = shift(up, "y", 1), shift(down, "y", -1)
     up, down, c_sums = lax.optimization_barrier((up, down, c_sums))
@@ -466,14 +482,14 @@
 
     a0 = jnp.concatenate([a, exchange(a, 1)], axis=0)
     a1 = exchange(a0, 0)
-    below0, above0 = shift(a0, "y", 1), shift(a0, "y", -1)
-    a1, below0, above0 = lax.optimization_barrier((a1, below0, above0))
-    above1, below1 = shift(a1, "y", -1), shift(a1, "y", 1)
-    far0, far1 = shift(below0, "y", 1), shift(above1, "y", -1)
-    new_fine = put_rows(place, [a0, a1, above0, below0], [(0, 0), (0, 1), (1, 0), (3, 0)])
+    back0, next0 = forward(a0, 1), forward(a0, -1)
+    a1, back0, next0 = lax.optimization_barrier((a1, back0, next0))
+    next1, back1 = forward(a1, -1), forward(a1, 1)
+    far0, far1 = forward(back0, 1), forward(next1, -1)
+    new_fine = put_rows(place, [a0, a1, next0, back0], [(0, 0), (0, 1), (1, 0), (3, 0)])
     new_coarse = coarse_rows(*c_sums)
     far1, new_coarse, new_fine = lax.optimization_barrier((far1, new_coarse, new_fine))
-    new_fine = put_rows(place, [above1, far0, far1, below1], [(1, 1), (2, 0), (2, 1), (3, 1)], new_fine)
+    new_fine = put_rows(place, [next1, far0, far1, back1], [(1, 1), (2, 0), (2, 1), (3, 1)], new_fine)
     return new_fine, new_coarse
 
 

time: 154 us -> 152 us (0.987)
  waiting for transfers between devices: 58.4 us -> 52.7 us
  starting transfers between devices: 39.9 us -> 44.7 us
  local copies, waits for them, and re-layouts: 8.16 us -> 5.29 us
    ppermute x16 -> x10, waiting for transfers between devices: 31.8 us -> 12.1 us  [shift(): return lax.ppermute(x, axis, [(i, (i + k) % n) for i in range(n)])]
    ppermute x0 -> x6, waiting for transfers between devices: none -> 17.9 us  [forward(): return lax.ppermute(x, ('y', 'c'), pairs)]
    ppermute x0 -> x6, starting transfers between devices: none -> 6.7 us  [forward(): return lax.ppermute(x, ('y', 'c'), pairs)]
    ppermute x16 -> x10, starting transfers between devices: 17.6 us -> 12.1 us  [shift(): return lax.ppermute(x, axis, [(i, (i + k) % n) for i in range(n)])]
    ppermute x8, waiting for transfers between devices: 19.5 us -> 15.7 us  [exchange(): lax.ppermute(x, ('z', 'c'), [(z * 2 + c, partner(step, z, c) * 2 + c) for...]
    ppermute x8, starting transfers between devices: 16.8 us -> 20.1 us  [exchange(): lax.ppermute(x, ('z', 'c'), [(z * 2 + c, partner(step, z, c) * 2 + c) for...]
    unnamed x34 -> x32, local copies, waits for them, and re-layouts: 5.33 us -> 2.47 us
    pallas_call x1, Pallas kernels: 5.08 us -> 7.17 us  [fine_sums(): pl.pallas_call(functools.partial(first_kernel, len(es)), grid_spec=pltpu....]
  transfers between devices with their start and end apart: 35 -> 35, of which waited for: 17 -> 16; matrix products, arithmetic and copies ran while one was open for 6% -> 6% of each run, Pallas kernels for 17% -> 17%
where the time goes in v3:
time: 152 us; the launch traced here: 149 us
  waiting for transfers between devices  52.7 us (35%)
  starting transfers between devices  44.7 us (29%)
  Pallas kernels  38.9 us (26%)
  local copies, waits for them, and re-layouts  5.29 us (3%)
  matrix products  3.45 us (2%)
  other arithmetic  3.2 us (2%)
    ppermute x8, starting transfers between devices, exchange(): lax.ppermute(x, ('z', 'c'), [(z * 2 + c, partner(step, z, c) * 2 + c) for...  20.1 us
    ppermute x6, waiting for transfers between devices, forward(): return lax.ppermute(x, ('y', 'c'), pairs)  17.9 us
    ppermute x8, waiting for transfers between devices, exchange(): lax.ppermute(x, ('z', 'c'), [(z * 2 + c, partner(step, z, c) * 2 + c) for...  15.7 us
    pallas_call x3, Pallas kernels, scores(): pl.pallas_call(functools.partial(score_kernel, len(es), len(stats)), grid...  13.4 us
    ppermute x10, waiting for transfers between devices, shift(): return lax.ppermute(x, axis, [(i, (i + k) % n) for i in range(n)])  12.1 us
    ppermute x10, starting transfers between devices, shift(): return lax.ppermute(x, axis, [(i, (i + k) % n) for i in range(n)])  12.1 us
    pallas_call x1, Pallas kernels, fine_sums(): pl.pallas_call(functools.partial(rest_kernel, len(es)), grid_spec=pltpu.P...  7.17 us
    pallas_call x1, Pallas kernels, fine_sums(): pl.pallas_call(functools.partial(first_kernel, len(es)), grid_spec=pltpu....  7.17 us
  transfers between devices with their start and end apart: 35, of which 16 were waited for; matrix products, arithmetic and copies ran while one was open for 6% of the time, Pallas kernels for 17%

profile of v3, /device:TPU:80, one launch (start us, length us, event | category | flops | bytes accessed | tf_op | source)
XLA Modules:
  0.0 149.4 jit_solution(15699473646184603525)
XLA Ops:
  0.7 1.2 fusion.23
  1.9 2.8 %collective-permute-start.3 = (bf16[64,1536]{1,0:T(8,128)(2,1)S(1)}, bf16[64,1536]{1,0:T(8,128)(2,1)S(1)}, u32[]{:S(2)}, u32[]{:S(2)}) collective-permute-start(bf16[64,1536]{1,0:T(8,128)(2,1)S(1)} %get-tuple-element.113), channel_id=1, source_target_pairs={{0,6},{2,0},{4,2},{6,4},{1,7},{3,1},{5,3},{7,5},{8,14},{10,8},{12,... | collective-permute-start | bytes 589832 | tf_op jit(solution)/shard_map/ppermute | solution.py:74
  4.8 0.8 collective-permute-start.1
  5.5 2.5 %collective-permute-start.2 = (bf16[64,1536]{1,0:T(8,128)(2,1)S(1)}, bf16[64,1536]{1,0:T(8,128)(2,1)}, u32[]{:S(2)}, u32[]{:S(2)}) collective-permute-start(bf16[64,1536]{1,0:T(8,128)(2,1)S(1)} %get-tuple-element.112), channel_id=1, source_target_pairs={{0,6},{2,0},{4,2},{6,4},{1,7},{3,1},{5,3},{7,5},{8,14},{10,8},{12,... | collective-permute-start | bytes 589832 | tf_op jit(solution)/shard_map/ppermute | solution.py:74
  8.1 1.9 %collective-permute-done.3.refs_1_.refs_3_ = bf16[64,1536]{1,0:T(8,128)(2,1)S(1)} collective-permute-done((bf16[64,1536]{1,0:T(8,128)(2,1)S(1)}, bf16[64,1536]{1,0:T(8,128)(2,1)S(1)}, u32[]{:S(2)}, u32[]{:S(2)}) %collective-permute-start.3) | collective-permute-done | bytes 196640 | tf_op jit(solution)/shard_map/ppermute | solution.py:74
  10.0 3.8 %collective-permute-done.6.refs_4_.refs_6_ = bf16[64,1536]{1,0:T(8,128)(2,1)} collective-permute-done((bf16[64,1536]{1,0:T(8,128)(2,1)S(1)}, bf16[64,1536]{1,0:T(8,128)(2,1)}, u32[]{:S(2)}, u32[]{:S(2)}) %collective-permute-start.6) | collective-permute-done | bytes 196640 | tf_op jit(solution)/shard_map/ppermute | solution.py:74
  13.8 2.0 %collective-permute-start.9 = (bf16[64,1536]{1,0:T(8,128)(2,1)}, bf16[64,1536]{1,0:T(8,128)(2,1)}, u32[]{:S(2)}, u32[]{:S(2)}) collective-permute-start(bf16[64,1536]{1,0:T(8,128)(2,1)} %collective-permute-done.6.refs_4_.refs_6_), channel_id=1, source_target_pairs={{0,2},{2,4},{4,6},{6,0},{1,3},{3,5},{5,7},{7,1},{8,10},{10,12},{12... | collective-permute-start | bytes 589832 | tf_op jit(solution)/shard_map/ppermute | solution.py:74
  15.9 3.9 %fine_scores.3 = (f32[1024,256]{1,0:T(8,128)}, f32[2,256]{1,0:T(2,128)}, f32[4,128]{1,0:T(4,128)}) custom-call(bf16[128,1536]{1,0:T(8,128)(2,1)} %refs_0_.5, bf16[128,1536]{1,0:T(8,128)(2,1)} %copy-done.11, bf16[1024,1536]{1,0:T(8,128)(2,1)} %fine.1), custom_call_target="tpu_custom_call" | custom-call | flops 805306368 | bytes 6291456 | tf_op jit(solution)/shard_map/fine_scores/pallas_call | solution.py:165
  19.9 0.5 collective-permute-start.4
  20.5 1.8 %collective-permute-done.9.refs_0_.refs_10_ = bf16[64,1536]{1,0:T(8,128)(2,1)} collective-permute-done((bf16[64,1536]{1,0:T(8,128)(2,1)}, bf16[64,1536]{1,0:T(8,128)(2,1)}, u32[]{:S(2)}, u32[]{:S(2)}) %collective-permute-start.9) | collective-permute-done | bytes 196640 | tf_op jit(solution)/shard_map/ppermute | solution.py:74
  22.3 0.5 collective-permute-start.12
  22.8 5.4 %fine_scores.4 = (f32[1024,512]{1,0:T(8,128)}, f32[2,512]{1,0:T(2,128)}, f32[8,128]{1,0:T(8,128)}) custom-call(bf16[64,1536]{1,0:T(8,128)(2,1)} %collective-permute-done.2.refs_0_.refs_2_, bf16[64,1536]{1,0:T(8,128)(2,1)} %copy-done.13, bf16[64,1536]{1,0:T(8,128)(2,1)} %collective-permute-done.4.refs_2_.refs_4_, bf16[64,1536]{1,0:T(8,128)(2,1)} %copy-done.14, ...), custom_call_target="tpu_custom_call" | custom-call | flops 1610612736 | bytes 6291456 | tf_op jit(solution)/shard_map/fine_scores/pallas_call | solution.py:165
  28.3 0.7 copy-done.12
  29.0 4.0 %fine_scores.5 = (f32[1024,256]{1,0:T(8,128)}, f32[2,256]{1,0:T(2,128)}, f32[8,16,128]{2,1,0:T(8,128)}) custom-call(bf16[64,1536]{1,0:T(8,128)(2,1)} %collective-permute-done.9.refs_0_.refs_10_, bf16[64,1536]{1,0:T(8,128)(2,1)} %collective-permute-done.10.refs_1_.refs_11_, bf16[64,1536]{1,0:T(8,128)(2,1)} %copy-done.12, ...), custom_call_target="tpu_custom_call" | custom-call | flops 805306368 | bytes 6291456 | tf_op jit(solution)/shard_map/fine_scores/pallas_call | solution.py:165
  32.9 3.4 %all-to-all-start = ((f32[8,16,128]{2,1,0:T(8,128)}), f32[8,16,128]{2,1,0:T(8,128)S(1)}, u32[]{:S(2)}, u32[]{:S(2)}) async-start(f32[8,16,128]{2,1,0:T(8,128)} %get-tuple-element.70), calls=%async_computation | async-start | bytes 131072 | tf_op jit(solution)/shard_map/all_to_all | solution.py:459
  36.3 0.7 dynamic-slice_bitcast_fusion
  37.0 0.6 concatenate.22.place
  37.6 4.2 %all-to-all-done.refs_20_ = f32[8,16,128]{2,1,0:T(8,128)S(1)} async-done(((f32[8,16,128]{2,1,0:T(8,128)}), f32[8,16,128]{2,1,0:T(8,128)S(1)}, u32[]{:S(2)}, u32[]{:S(2)}) %all-to-all-start) | async-done | bytes 65568 | tf_op jit(solution)/shard_map/all_to_all | solution.py:459
  41.8 0.6 copy-done.15
  42.5 7.2 %first_sums.1 = (f32[128,1536]{1,0:T(8,128)}, f32[128,128]{1,0:T(8,128)}, bf16[128,1664]{1,0:T(8,128)(2,1)}, f32[128,1536]{1,0:T(8,128)}, f32[128,128]{1,0:T(8,1...) custom-call(s32[20]{0:T(128)} %concatenate.22.place, bf16[128,1536]{1,0:T(8,128)(2,1)} %refs_0_.5, ...), custom_call_target="tpu_custom_call" | custom-call | flops 1610612736 | bytes 5242880 | tf_op jit(solution)/shard_map/first_sums/pallas_call | solution.py:279
  49.6 2.2 %collective-permute-start.13 = (bf16[128,1664]{1,0:T(8,128)(2,1)}, bf16[128,1664]{1,0:T(8,128)(2,1)S(1)}, u32[]{:S(2)}, u32[]{:S(2)}) collective-permute-start(bf16[128,1664]{1,0:T(8,128)(2,1)} %get-tuple-element.78), channel_id=1, source_target_pairs={{0,8},{1,57},{8,0},{9,17},{16,24},{17,9},{24,16},{25,33},{32,40},{... | collective-permute-start | bytes 1277960 | tf_op jit(solution)/shard_map/ppermute | solution.py:63
  51.9 7.2 %rest_sums.1 = (f32[128,1536]{1,0:T(8,128)}, f32[128,128]{1,0:T(8,128)}, bf16[128,1664]{1,0:T(8,128)(2,1)}, f32[128,1536]{1,0:T(8,128)}, f32[128,128]{1,0:T(8,128)}, /*index=5*/bf16[128,1664]{1,0:T(8,128)(2,1)}) custom-call(s32[20]{0:T(128)} %concatenate.22.place, bf16[128,1536]{1,0:T(8,128)(2,1)} %refs_0_.5, bf16[128,1536]{1,0:T(8,128)(2,1)} %copy-done.11, ...), custom_call_target="tpu_custom_call" | custom-call | flops 1610612736 | bytes 10485760 | tf_op jit(solution)/shard_map/rest_sums/pallas_call | solution.py:295
  59.1 2.0 %collective-permute-start.14 = (bf16[128,1664]{1,0:T(8,128)(2,1)}, bf16[128,1664]{1,0:T(8,128)(2,1)S(1)}, u32[]{:S(2)}, u32[]{:S(2)}) collective-permute-start(bf16[128,1664]{1,0:T(8,128)(2,1)} %get-tuple-element.81), channel_id=1, source_target_pairs={{0,8},{1,57},{8,0},{9,17},{16,24},{17,9},{24,16},{25,33},{32,40},{... | collective-permute-start | bytes 1277960 | tf_op jit(solution)/shard_map/ppermute | solution.py:63
  61.2 0.2 add_far_step.1
  61.4 1.4 collective-permute-start.16
  62.8 0.7 collective-permute-start.19
  63.6 3.8 %collective-permute-done.16.far = bf16[64,1664]{1,0:T(8,128)(2,1)S(1)} collective-permute-done((bf16[64,1664]{1,0:T(8,128)(2,1)S(1)}, bf16[64,1664]{1,0:T(8,128)(2,1)S(1)}, u32[]{:S(2)}, u32[]{:S(2)}) %collective-permute-start.16) | collective-permute-done | bytes 213024 | tf_op jit(solution)/shard_map/ppermute | solution.py:74
  67.4 1.3 add_side_step.2
  68.7 1.4 collective-permute-start.17
  70.1 2.1 %collective-permute-done.18.got = bf16[128,1664]{1,0:T(8,128)(2,1)S(1)} collective-permute-done((bf16[128,1664]{1,0:T(8,128)(2,1)}, bf16[128,1664]{1,0:T(8,128)(2,1)S(1)}, u32[]{:S(2)}, u32[]{:S(2)}) %collective-permute-start.18) | collective-permute-done | bytes 426016 | tf_op jit(solution)/shard_map/ppermute | solution.py:63
  72.1 1.1 copy-done.4
  73.3 0.2 add_side_step.3
  73.5 0.5 collective-permute-start.20
  74.0 3.5 %fusion.24 = (f32[1024]{0:T(1024)S(1)}, f32[1024,1024]{1,0:T(8,128)S(1)}) fusion(bf16[1024,1536]{1,0:T(8,128)(2,1)S(1)} %copy-done, bf16[1024,1536]{1,0:T(8,128)(2,1)S(1)} %copy-done.1), kind=kOutput, calls=%fused_computation.49 | convolution fusion | flops 3223321600 | bytes 10489856 | tf_op jit(solution)/shard_map/dot_general | solution.py:430
  77.5 0.6 exponential_reduce_fusion
  78.2 5.0 %coarse_sums.1 = (f32[4,128,1536]{2,1,0:T(8,128)S(1)}, bf16[4,144,1536]{2,1,0:T(8,128)(2,1)S(1)}, f32[4,1,128]{2,1,0:T(1,128)S(1)}) custom-call(s32[20]{0:T(128)S(1)} %copy-done.10, f32[1024,1024]{1,0:T(8,128)S(1)} %get-tuple-element.119.s, f32[1,1024]{1,0:T(1,128)S(1)} %bitcast.39, f32[1,1024]{1,0:T(1,128)S(1)} %bitcast.40, bf16[1024,1536]{1,0:T(8,128)(2,1)S(1)} %copy-done.1), custom_call_target="tpu_custom_call" | custom-call | flops 3221225472 | bytes 12582912 | tf_op jit(solution)/shard_map/coarse_sums/pallas_call | solution.py:398
  83.2 0.8 collective-permute-done.20.down
  84.0 0.4 add_own_step.1
  84.4 0.6 collective-permute-start.21
  85.0 2.7 %collective-permute-done.30 = bf16[4,144,1536]{2,1,0:T(8,128)(2,1)S(1)} collective-permute-done((bf16[4,144,1536]{2,1,0:T(8,128)(2,1)S(1)}, bf16[4,144,1536]{2,1,0:T(8,128)(2,1)S(1)}, u32[]{:S(2)}, u32[]{:S(2)}) %collective-permute-start.30) | collective-permute-done | bytes 1769504 | tf_op jit(solution)/shard_map/ppermute | solution.py:83
  87.7 0.5 convert_element_type.18
  88.2 0.6 slice_add_fusion
  88.9 0.7 collective-permute-start.31
  89.6 1.0 collective-permute-done.21.got
  90.7 5.0 %collective-permute-start.22 = (bf16[64,1664]{1,0:T(8,128)(2,1)S(1)}, bf16[64,1664]{1,0:T(8,128)(2,1)S(1)}, u32[]{:S(2)}, u32[]{:S(2)}) collective-permute-start(bf16[64,1664]{1,0:T(8,128)(2,1)S(1)} %add_half_step.1.own), channel_id=1, source_target_pairs={{0,24},{1,41},{8,48},{9,33},{16,40},{17,57},{24,0},{25,49},{32,56}... | collective-permute-start | bytes 638984 | tf_op jit(solution)/shard_map/ppermute | solution.py:63
  95.8 6.3 %collective-permute-done.22.got = bf16[64,1664]{1,0:T(8,128)(2,1)S(1)} collective-permute-done((bf16[64,1664]{1,0:T(8,128)(2,1)S(1)}, bf16[64,1664]{1,0:T(8,128)(2,1)S(1)}, u32[]{:S(2)}, u32[]{:S(2)}) %collective-permute-start.22) | collective-permute-done | bytes 213024 | tf_op jit(solution)/shard_map/ppermute | solution.py:63
  102.0 0.2 add_last_step.1
  102.2 1.9 %collective-permute-start.23 = (bf16[64,1536]{1,0:T(8,128)(2,1)S(1)}, bf16[64,1536]{1,0:T(8,128)(2,1)S(1)}, u32[]{:S(2)}, u32[]{:S(2)}) collective-permute-start(bf16[64,1536]{1,0:T(8,128)(2,1)S(1)} %add_last_step.1), channel_id=1, source_target_pairs={{0,56},{1,9},{8,16},{9,1},{16,8},{17,25},{24,32},{25,17},{32,24},{... | collective-permute-start | bytes 589832 | tf_op jit(solution)/shard_map/ppermute | solution.py:63
  104.1 4.3 %collective-permute-done.23 = bf16[64,1536]{1,0:T(8,128)(2,1)S(1)} collective-permute-done((bf16[64,1536]{1,0:T(8,128)(2,1)S(1)}, bf16[64,1536]{1,0:T(8,128)(2,1)S(1)}, u32[]{:S(2)}, u32[]{:S(2)}) %collective-permute-start.23) | collective-permute-done | bytes 196640 | tf_op jit(solution)/shard_map/ppermute | solution.py:63
  108.5 8.2 %collective-permute-start.24 = (bf16[128,1536]{1,0:T(8,128)(2,1)S(1)}, bf16[128,1536]{1,0:T(8,128)(2,1)S(1)}, u32[]{:S(2)}, u32[]{:S(2)}) collective-permute-start(bf16[128,1536]{1,0:T(8,128)(2,1)S(1)} %pad_maximum_fusion.2.refs_0_), channel_id=1, source_target_pairs={{0,8},{1,57},{8,0},{9,17},{16,24},{17,9},{24,16},{25,33},{32,40},{... | collective-permute-start | bytes 1179656 | tf_op jit(solution)/shard_map/ppermute | solution.py:63
  116.7 2.5 %collective-permute-start.25 = (bf16[128,1536]{1,0:T(8,128)(2,1)S(1)}, bf16[128,1536]{1,0:T(8,128)(2,1)S(1)}, u32[]{:S(2)}, u32[]{:S(2)}) collective-permute-start(bf16[128,1536]{1,0:T(8,128)(2,1)S(1)} %pad_maximum_fusion.2.refs_0_), channel_id=1, source_target_pairs={{0,64},{1,193},{64,128},{65,1},{128,192},{129,65},{192,0},{193,129... | collective-permute-start | bytes 1179656 | tf_op jit(solution)/shard_map/ppermute | solution.py:79
  119.6 0.2 slice_add_fusion.1
  119.9 0.5 collective-permute-start.32
  120.4 2.0 %collective-permute-done.24.refs_1_ = bf16[128,1536]{1,0:T(8,128)(2,1)S(1)} collective-permute-done((bf16[128,1536]{1,0:T(8,128)(2,1)S(1)}, bf16[128,1536]{1,0:T(8,128)(2,1)S(1)}, u32[]{:S(2)}, u32[]{:S(2)}) %collective-permute-start.24) | collective-permute-done | bytes 393248 | tf_op jit(solution)/shard_map/ppermute | solution.py:63
  122.5 5.9 %collective-permute-done.25.refs_3_ = bf16[128,1536]{1,0:T(8,128)(2,1)S(1)} collective-permute-done((bf16[128,1536]{1,0:T(8,128)(2,1)S(1)}, bf16[128,1536]{1,0:T(8,128)(2,1)S(1)}, u32[]{:S(2)}, u32[]{:S(2)}) %collective-permute-start.25) | collective-permute-done | bytes 393248 | tf_op jit(solution)/shard_map/ppermute | solution.py:79
  128.4 1.5 %collective-permute-done.26.refs_2_ = bf16[128,1536]{1,0:T(8,128)(2,1)S(1)} collective-permute-done((bf16[128,1536]{1,0:T(8,128)(2,1)S(1)}, bf16[128,1536]{1,0:T(8,128)(2,1)S(1)}, u32[]{:S(2)}, u32[]{:S(2)}) %collective-permute-start.26) | collective-permute-done | bytes 393248 | tf_op jit(solution)/shard_map/ppermute | solution.py:79
  129.9 1.0 collective-permute-start.27
  130.9 1.1 collective-permute-start.33
  131.9 2.2 %collective-permute-start.28 = (bf16[128,1536]{1,0:T(8,128)(2,1)S(1)}, bf16[128,1536]{1,0:T(8,128)(2,1)S(1)}, u32[]{:S(2)}, u32[]{:S(2)}) collective-permute-start(bf16[128,1536]{1,0:T(8,128)(2,1)S(1)} %collective-permute-done.25.refs_3_), channel_id=1, source_target_pairs={{0,64},{1,193},{64,128},{65,1},{128,192},{129,65},{192,0},{193,129... | collective-permute-start | bytes 1179656 | tf_op jit(solution)/shard_map/ppermute | solution.py:79
  134.1 1.8 %put_rows.2.refs_4_ = bf16[1024,1536]{1,0:T(8,128)(2,1)} custom-call(s32[20]{0:T(128)S(1)} %copy-done.10, bf16[128,1536]{1,0:T(8,128)(2,1)S(1)} %pad_maximum_fusion.2.refs_0_, bf16[128,1536]{1,0:T(8,128)(2,1)S(1)} %collective-permute-done.24.refs_1_, bf16[128,1536]{1,0:T(8,128)(2,1)S(1)} %collective-permute-done.26.refs_2_, ...), custom_call_target="tpu_custom_call" | custom-call | bytes 3145728 | tf_op jit(solution)/shard_map/put_rows/pallas_call | solution.py:111
  135.9 3.7 %collective-permute-done.27.refs_0_ = bf16[128,1536]{1,0:T(8,128)(2,1)S(1)} collective-permute-done((bf16[128,1536]{1,0:T(8,128)(2,1)S(1)}, bf16[128,1536]{1,0:T(8,128)(2,1)S(1)}, u32[]{:S(2)}, u32[]{:S(2)}) %collective-permute-start.27) | collective-permute-done | bytes 393248 | tf_op jit(solution)/shard_map/ppermute | solution.py:79
  139.7 0.9 fusion.3
  140.6 6.8 %collective-permute-done.29.refs_2_ = bf16[128,1536]{1,0:T(8,128)(2,1)S(1)} collective-permute-done((bf16[128,1536]{1,0:T(8,128)(2,1)S(1)}, bf16[128,1536]{1,0:T(8,128)(2,1)S(1)}, u32[]{:S(2)}, u32[]{:S(2)}) %collective-permute-start.29) | collective-permute-done | bytes 393248 | tf_op jit(solution)/shard_map/ppermute | solution.py:79
  147.4 1.8 %put_rows.3 = bf16[1024,1536]{1,0:T(8,128)(2,1)} custom-call(s32[20]{0:T(128)S(1)} %copy-done.10, bf16[128,1536]{1,0:T(8,128)(2,1)S(1)} %collective-permute-done.27.refs_0_, bf16[128,1536]{1,0:T(8,128)(2,1)S(1)} %collective-permute-done.28.refs_1_, bf16[128,1536]{1,0:T(8,128)(2,1)S(1)} %collective-permute-done.29.refs_2_, ...), custom_call_target="tpu_custom_call", output_to_operand_aliasing={{}: (5, {})} | custom-call | bytes 3145728 | tf_op jit(solution)/shard_map/put_rows/pallas_call | solution.py:111
  (77 shorter events, 1.5 us)
Async XLA Ops:
  0.6 73.4 %copy-start = (bf16[1024,1536]{1,0:T(8,128)(2,1)S(1)}, bf16[1024,1536]{1,0:T(8,128)(2,1)}, u32[]{:S(2)}) copy-start(bf16[1024,1536]{1,0:T(8,128)(2,1)} %param.7) | copy-start | bytes 9437188
  0.6 13.2 %collective-permute-start = (bf16[128,1536]{1,0:T(8,128)(2,1)}, bf16[128,1536]{1,0:T(8,128)(2,1)S(1)}, u32[]{:S(2)}, u32[]{:S(2)}) collective-permute-start(bf16[128,1536]{1,0:T(8,128)(2,1)} %refs_0_.5), channel_id=1, source_target_pairs={{0,1},{1,0},{2,3},{3,2},{4,5},{5,4},{6,7},{7,6},{8,9},{9,8},{10,11... | collective-permute-start | bytes 1179656 | tf_op jit(solution)/shard_map/ppermute | solution.py:83
  1.9 8.1 %collective-permute-start.3 = (bf16[64,1536]{1,0:T(8,128)(2,1)S(1)}, bf16[64,1536]{1,0:T(8,128)(2,1)S(1)}, u32[]{:S(2)}, u32[]{:S(2)}) collective-permute-start(bf16[64,1536]{1,0:T(8,128)(2,1)S(1)} %get-tuple-element.113), channel_id=1, source_target_pairs={{0,6},{2,0},{4,2},{6,4},{1,7},{3,1},{5,3},{7,5},{8,14},{10,8},{12,... | collective-permute-start | bytes 589832 | tf_op jit(solution)/shard_map/ppermute | solution.py:74
  4.8 9.1 %collective-permute-start.6 = (bf16[64,1536]{1,0:T(8,128)(2,1)S(1)}, bf16[64,1536]{1,0:T(8,128)(2,1)}, u32[]{:S(2)}, u32[]{:S(2)}) collective-permute-start(bf16[64,1536]{1,0:T(8,128)(2,1)S(1)} %get-tuple-element.112), channel_id=1, source_target_pairs={{0,2},{2,4},{4,6},{6,0},{1,3},{3,5},{5,7},{7,1},{8,10},{10,12},{12... | collective-permute-start | bytes 589832 | tf_op jit(solution)/shard_map/ppermute | solution.py:74
  4.8 15.0 %collective-permute-start.1 = (bf16[64,1536]{1,0:T(8,128)(2,1)S(1)}, bf16[64,1536]{1,0:T(8,128)(2,1)}, u32[]{:S(2)}, u32[]{:S(2)}) collective-permute-start(bf16[64,1536]{1,0:T(8,128)(2,1)S(1)} %get-tuple-element.113), channel_id=1, source_target_pairs={{0,2},{2,4},{4,6},{6,0},{1,3},{3,5},{5,7},{7,1},{8,10},{10,12},{12... | collective-permute-start | bytes 589832 | tf_op jit(solution)/shard_map/ppermute | solution.py:74
  5.5 14.4 %collective-permute-start.2 = (bf16[64,1536]{1,0:T(8,128)(2,1)S(1)}, bf16[64,1536]{1,0:T(8,128)(2,1)}, u32[]{:S(2)}, u32[]{:S(2)}) collective-permute-start(bf16[64,1536]{1,0:T(8,128)(2,1)S(1)} %get-tuple-element.112), channel_id=1, source_target_pairs={{0,6},{2,0},{4,2},{6,4},{1,7},{3,1},{5,3},{7,5},{8,14},{10,8},{12,... | collective-permute-start | bytes 589832 | tf_op jit(solution)/shard_map/ppermute | solution.py:74
  10.0 10.5 %copy-start.13 = (bf16[64,1536]{1,0:T(8,128)(2,1)}, bf16[64,1536]{1,0:T(8,128)(2,1)S(1)}, u32[]{:S(2)}) copy-start(bf16[64,1536]{1,0:T(8,128)(2,1)S(1)} %collective-permute-done.3.refs_1_.refs_3_) | copy-start | bytes 589828
  10.0 10.4 %collective-permute-start.5 = (bf16[64,1536]{1,0:T(8,128)(2,1)S(1)}, bf16[64,1536]{1,0:T(8,128)(2,1)S(1)}, u32[]{:S(2)}, u32[]{:S(2)}) collective-permute-start(bf16[64,1536]{1,0:T(8,128)(2,1)S(1)} %collective-permute-done.3.refs_1_.refs_3_), channel_id=1, source_target_pairs={{0,1},{1,0},{2,3},{3,2},{4,5},{5,4},{6,7},{7,6},{8,9},{9,8},{10,11... | collective-permute-start | bytes 589832 | tf_op jit(solution)/shard_map/ppermute | solution.py:83
  13.8 8.5 %collective-permute-start.10 = (bf16[64,1536]{1,0:T(8,128)(2,1)S(1)}, bf16[64,1536]{1,0:T(8,128)(2,1)}, u32[]{:S(2)}, u32[]{:S(2)}) collective-permute-start(bf16[64,1536]{1,0:T(8,128)(2,1)S(1)} %collective-permute-done.3.refs_1_.refs_3_), channel_id=1, source_target_pairs={{0,6},{2,0},{4,2},{6,4},{1,7},{3,1},{5,3},{7,5},{8,14},{10,8},{12,... | collective-permute-start | bytes 589832 | tf_op jit(solution)/shard_map/ppermute | solution.py:74
  13.8 2.0 %copy-start.11 = (bf16[128,1536]{1,0:T(8,128)(2,1)}, bf16[128,1536]{1,0:T(8,128)(2,1)S(1)}, u32[]{:S(2)}) copy-start(bf16[128,1536]{1,0:T(8,128)(2,1)S(1)} %collective-permute-done.refs_1_) | copy-start | bytes 1179652
  13.8 8.4 %collective-permute-start.9 = (bf16[64,1536]{1,0:T(8,128)(2,1)}, bf16[64,1536]{1,0:T(8,128)(2,1)}, u32[]{:S(2)}, u32[]{:S(2)}) collective-permute-start(bf16[64,1536]{1,0:T(8,128)(2,1)} %collective-permute-done.6.refs_4_.refs_6_), channel_id=1, source_target_pairs={{0,2},{2,4},{4,6},{6,0},{1,3},{3,5},{5,7},{7,1},{8,10},{10,12},{12... | collective-permute-start | bytes 589832 | tf_op jit(solution)/shard_map/ppermute | solution.py:74
  19.8 3.0 %collective-permute-start.7 = (bf16[64,1536]{1,0:T(8,128)(2,1)}, bf16[64,1536]{1,0:T(8,128)(2,1)}, u32[]{:S(2)}, u32[]{:S(2)}) collective-permute-start(bf16[64,1536]{1,0:T(8,128)(2,1)} %collective-permute-done.6.refs_4_.refs_6_), channel_id=1, source_target_pairs={{0,1},{1,0},{2,3},{3,2},{4,5},{5,4},{6,7},{7,6},{8,9},{9,8},{10,11... | collective-permute-start | bytes 589832 | tf_op jit(solution)/shard_map/ppermute | solution.py:83
  19.9 2.9 %collective-permute-start.4 = (bf16[64,1536]{1,0:T(8,128)(2,1)}, bf16[64,1536]{1,0:T(8,128)(2,1)}, u32[]{:S(2)}, u32[]{:S(2)}) collective-permute-start(bf16[64,1536]{1,0:T(8,128)(2,1)} %collective-permute-done.2.refs_0_.refs_2_), channel_id=1, source_target_pairs={{0,1},{1,0},{2,3},{3,2},{4,5},{5,4},{6,7},{7,6},{8,9},{9,8},{10,11... | collective-permute-start | bytes 589832 | tf_op jit(solution)/shard_map/ppermute | solution.py:83
  20.4 1.9 %copy-start.14 = (bf16[64,1536]{1,0:T(8,128)(2,1)}, bf16[64,1536]{1,0:T(8,128)(2,1)S(1)}, u32[]{:S(2)}) copy-start(bf16[64,1536]{1,0:T(8,128)(2,1)S(1)} %collective-permute-done.5.refs_3_.refs_5_) | copy-start | bytes 589828
  20.4 2.4 %collective-permute-start.8 = (bf16[64,1536]{1,0:T(8,128)(2,1)}, bf16[64,1536]{1,0:T(8,128)(2,1)}, u32[]{:S(2)}, u32[]{:S(2)}) collective-permute-start(bf16[64,1536]{1,0:T(8,128)(2,1)} %collective-permute-done.1.refs_5_.refs_7_), channel_id=1, source_target_pairs={{0,1},{1,0},{2,3},{3,2},{4,5},{5,4},{6,7},{7,6},{8,9},{9,8},{10,11... | collective-permute-start | bytes 589832 | tf_op jit(solution)/shard_map/ppermute | solution.py:83
  22.3 6.0 %collective-permute-start.11 = (bf16[64,1536]{1,0:T(8,128)(2,1)}, bf16[64,1536]{1,0:T(8,128)(2,1)S(1)}, u32[]{:S(2)}, u32[]{:S(2)}) collective-permute-start(bf16[64,1536]{1,0:T(8,128)(2,1)} %collective-permute-done.9.refs_0_.refs_10_), channel_id=1, source_target_pairs={{0,1},{1,0},{2,3},{3,2},{4,5},{5,4},{6,7},{7,6},{8,9},{9,8},{10,11... | collective-permute-start | bytes 589832 | tf_op jit(solution)/shard_map/ppermute | solution.py:83
  22.3 6.0 %collective-permute-start.12 = (bf16[64,1536]{1,0:T(8,128)(2,1)}, bf16[64,1536]{1,0:T(8,128)(2,1)}, u32[]{:S(2)}, u32[]{:S(2)}) collective-permute-start(bf16[64,1536]{1,0:T(8,128)(2,1)} %collective-permute-done.10.refs_1_.refs_11_), channel_id=1, source_target_pairs={{0,1},{1,0},{2,3},{3,2},{4,5},{5,4},{6,7},{7,6},{8,9},{9,8},{10,11... | collective-permute-start | bytes 589832 | tf_op jit(solution)/shard_map/ppermute | solution.py:83
  28.3 0.7 copy-start.12
  32.9 8.9 %all-to-all-start = ((f32[8,16,128]{2,1,0:T(8,128)}), f32[8,16,128]{2,1,0:T(8,128)S(1)}, u32[]{:S(2)}, u32[]{:S(2)}) async-start(f32[8,16,128]{2,1,0:T(8,128)} %get-tuple-element.70), calls=%async_computation | async-start | bytes 131072 | tf_op jit(solution)/shard_map/all_to_all | solution.py:459
  41.8 0.6 copy-start.15
  49.6 9.5 %collective-permute-start.13 = (bf16[128,1664]{1,0:T(8,128)(2,1)}, bf16[128,1664]{1,0:T(8,128)(2,1)S(1)}, u32[]{:S(2)}, u32[]{:S(2)}) collective-permute-start(bf16[128,1664]{1,0:T(8,128)(2,1)} %get-tuple-element.78), channel_id=1, source_target_pairs={{0,8},{1,57},{8,0},{9,17},{16,24},{17,9},{24,16},{25,33},{32,40},{... | collective-permute-start | bytes 1277960 | tf_op jit(solution)/shard_map/ppermute | solution.py:63
  51.8 11.8 %collective-permute-start.15 = (bf16[128,1664]{1,0:T(8,128)(2,1)}, bf16[128,1664]{1,0:T(8,128)(2,1)}, u32[]{:S(2)}, u32[]{:S(2)}) collective-permute-start(bf16[128,1664]{1,0:T(8,128)(2,1)} %get-tuple-element.85), channel_id=1, source_target_pairs={{0,8},{1,57},{8,0},{9,17},{16,24},{17,9},{24,16},{25,33},{32,40},{... | collective-permute-start | bytes 1277960 | tf_op jit(solution)/shard_map/ppermute | solution.py:63
  51.9 9.3 %copy-start.3 = (f32[128,1536]{1,0:T(8,128)S(1)}, f32[128,1536]{1,0:T(8,128)}, u32[]{:S(2)}) copy-start(f32[128,1536]{1,0:T(8,128)} %get-tuple-element.86.keep) | copy-start | bytes 2359300
  51.9 9.3 %copy-start.7 = (f32[128,128]{1,0:T(8,128)S(1)}, f32[128,128]{1,0:T(8,128)}, u32[]{:S(2)}) copy-start(f32[128,128]{1,0:T(8,128)} %get-tuple-element.87.mass) | copy-start | bytes 196612
  51.9 15.5 %copy-start.5 = (f32[128,1536]{1,0:T(8,128)S(1)}, f32[128,1536]{1,0:T(8,128)}, u32[]{:S(2)}) copy-start(f32[128,1536]{1,0:T(8,128)} %get-tuple-element.83.keep) | copy-start | bytes 2359300
  51.9 15.5 %copy-start.9 = (f32[128,128]{1,0:T(8,128)S(1)}, f32[128,128]{1,0:T(8,128)}, u32[]{:S(2)}) copy-start(f32[128,128]{1,0:T(8,128)} %get-tuple-element.84.mass) | copy-start | bytes 196612
  59.1 13.0 %copy-start.8 = (f32[128,128]{1,0:T(8,128)S(1)}, f32[128,128]{1,0:T(8,128)}, u32[]{:S(2)}) copy-start(f32[128,128]{1,0:T(8,128)} %get-tuple-element.91.mass) | copy-start | bytes 196612
  59.1 14.9 %copy-start.1 = (bf16[1024,1536]{1,0:T(8,128)(2,1)S(1)}, bf16[1024,1536]{1,0:T(8,128)(2,1)}, u32[]{:S(2)}) copy-start(bf16[1024,1536]{1,0:T(8,128)(2,1)} %fine.1) | copy-start | bytes 9437188
  59.1 10.9 %collective-permute-start.14 = (bf16[128,1664]{1,0:T(8,128)(2,1)}, bf16[128,1664]{1,0:T(8,128)(2,1)S(1)}, u32[]{:S(2)}, u32[]{:S(2)}) collective-permute-start(bf16[128,1664]{1,0:T(8,128)(2,1)} %get-tuple-element.81), channel_id=1, source_target_pairs={{0,8},{1,57},{8,0},{9,17},{16,24},{17,9},{24,16},{25,33},{32,40},{... | collective-permute-start | bytes 1277960 | tf_op jit(solution)/shard_map/ppermute | solution.py:63
  61.1 11.0 %collective-permute-start.18 = (bf16[128,1664]{1,0:T(8,128)(2,1)}, bf16[128,1664]{1,0:T(8,128)(2,1)S(1)}, u32[]{:S(2)}, u32[]{:S(2)}) collective-permute-start(bf16[128,1664]{1,0:T(8,128)(2,1)} %get-tuple-element.92), channel_id=1, source_target_pairs={{0,8},{1,57},{8,0},{9,17},{16,24},{17,9},{24,16},{25,33},{32,40},{... | collective-permute-start | bytes 1277960 | tf_op jit(solution)/shard_map/ppermute | solution.py:63
  61.4 5.9 %collective-permute-start.16 = (bf16[64,1664]{1,0:T(8,128)(2,1)S(1)}, bf16[64,1664]{1,0:T(8,128)(2,1)S(1)}, u32[]{:S(2)}, u32[]{:S(2)}) collective-permute-start(bf16[64,1664]{1,0:T(8,128)(2,1)S(1)} %get-tuple-element.89), channel_id=1, source_target_pairs={{0,64},{64,128},{128,192},{192,0},{1,65},{65,129},{129,193},{193,1... | collective-permute-start | bytes 638984 | tf_op jit(solution)/shard_map/ppermute | solution.py:74
  62.8 7.3 %collective-permute-start.19 = (bf16[64,1664]{1,0:T(8,128)(2,1)S(1)}, bf16[64,1664]{1,0:T(8,128)(2,1)S(1)}, u32[]{:S(2)}, u32[]{:S(2)}) collective-permute-start(bf16[64,1664]{1,0:T(8,128)(2,1)S(1)} %get-tuple-element.93), channel_id=1, source_target_pairs={{0,192},{64,0},{128,64},{192,128},{1,193},{65,1},{129,65},{193,129... | collective-permute-start | bytes 638984 | tf_op jit(solution)/shard_map/ppermute | solution.py:74
  68.7 14.5 %collective-permute-start.17 = (bf16[128,1664]{1,0:T(8,128)(2,1)S(1)}, bf16[128,1664]{1,0:T(8,128)(2,1)S(1)}, u32[]{:S(2)}, u32[]{:S(2)}) collective-permute-start(bf16[128,1664]{1,0:T(8,128)(2,1)S(1)} %add_side_step.2), channel_id=1, source_target_pairs={{0,64},{64,128},{128,192},{192,0},{1,65},{65,129},{129,193},{193,1... | collective-permute-start | bytes 1277960 | tf_op jit(solution)/shard_map/ppermute | solution.py:74
  72.1 1.1 copy-start.4
  73.5 10.5 %collective-permute-start.20 = (bf16[128,1664]{1,0:T(8,128)(2,1)S(1)}, bf16[128,1664]{1,0:T(8,128)(2,1)S(1)}, u32[]{:S(2)}, u32[]{:S(2)}) collective-permute-start(bf16[128,1664]{1,0:T(8,128)(2,1)S(1)} %add_side_step.3), channel_id=1, source_target_pairs={{0,192},{64,0},{128,64},{192,128},{1,193},{65,1},{129,65},{193,129... | collective-permute-start | bytes 1277960 | tf_op jit(solution)/shard_map/ppermute | solution.py:74
  77.5 0.6 copy-start.10
  78.1 5.8 %copy-start.2 = (f32[128,1536]{1,0:T(8,128)S(1)}, f32[128,1536]{1,0:T(8,128)}, u32[]{:S(2)}) copy-start(f32[128,1536]{1,0:T(8,128)} %get-tuple-element.79.keep) | copy-start | bytes 2359300
  78.2 5.8 %copy-start.6 = (f32[128,128]{1,0:T(8,128)S(1)}, f32[128,128]{1,0:T(8,128)}, u32[]{:S(2)}) copy-start(f32[128,128]{1,0:T(8,128)} %get-tuple-element.80.mass) | copy-start | bytes 196612
  84.0 3.7 %collective-permute-start.30 = (bf16[4,144,1536]{2,1,0:T(8,128)(2,1)S(1)}, bf16[4,144,1536]{2,1,0:T(8,128)(2,1)S(1)}, u32[]{:S(2)}, u32[]{:S(2)}) collective-permute-start(bf16[4,144,1536]{2,1,0:T(8,128)(2,1)S(1)} %get-tuple-element.106), channel_id=1, source_target_pairs={{0,1},{1,0},{2,3},{3,2},{4,5},{5,4},{6,7},{7,6},{8,9},{9,8},{10,11... | collective-permute-start | bytes 5308424 | tf_op jit(solution)/shard_map/ppermute | solution.py:83
  84.4 6.2 %collective-permute-start.21 = (bf16[64,1664]{1,0:T(8,128)(2,1)S(1)}, bf16[64,1664]{1,0:T(8,128)(2,1)S(1)}, u32[]{:S(2)}, u32[]{:S(2)}) collective-permute-start(bf16[64,1664]{1,0:T(8,128)(2,1)S(1)} %get-tuple-element.102), channel_id=1, source_target_pairs={{0,56},{1,9},{8,16},{9,1},{16,8},{17,25},{24,32},{25,17},{32,24},{... | collective-permute-start | bytes 638984 | tf_op jit(solution)/shard_map/ppermute | solution.py:63
  88.9 30.3 %collective-permute-start.31 = (bf16[264,1536]{1,0:T(8,128)(2,1)S(1)}, bf16[264,1536]{1,0:T(8,128)(2,1)S(1)}, u32[]{:S(2)}, u32[]{:S(2)}) collective-permute-start(bf16[264,1536]{1,0:T(8,128)(2,1)S(1)} %pad_maximum_fusion), channel_id=1, source_target_pairs={{0,2},{1,7},{2,0},{3,5},{4,6},{5,3},{6,4},{7,1},{8,10},{9,15},{10,... | collective-permute-start | bytes 2433032 | tf_op jit(solution)/shard_map/ppermute | solution.py:67
  90.7 11.3 %collective-permute-start.22 = (bf16[64,1664]{1,0:T(8,128)(2,1)S(1)}, bf16[64,1664]{1,0:T(8,128)(2,1)S(1)}, u32[]{:S(2)}, u32[]{:S(2)}) collective-permute-start(bf16[64,1664]{1,0:T(8,128)(2,1)S(1)} %add_half_step.1.own), channel_id=1, source_target_pairs={{0,24},{1,41},{8,48},{9,33},{16,40},{17,57},{24,0},{25,49},{32,56}... | collective-permute-start | bytes 638984 | tf_op jit(solution)/shard_map/ppermute | solution.py:63
  102.2 6.2 %collective-permute-start.23 = (bf16[64,1536]{1,0:T(8,128)(2,1)S(1)}, bf16[64,1536]{1,0:T(8,128)(2,1)S(1)}, u32[]{:S(2)}, u32[]{:S(2)}) collective-permute-start(bf16[64,1536]{1,0:T(8,128)(2,1)S(1)} %add_last_step.1), channel_id=1, source_target_pairs={{0,56},{1,9},{8,16},{9,1},{16,8},{17,25},{24,32},{25,17},{32,24},{... | collective-permute-start | bytes 589832 | tf_op jit(solution)/shard_map/ppermute | solution.py:63
  108.5 14.0 %collective-permute-start.24 = (bf16[128,1536]{1,0:T(8,128)(2,1)S(1)}, bf16[128,1536]{1,0:T(8,128)(2,1)S(1)}, u32[]{:S(2)}, u32[]{:S(2)}) collective-permute-start(bf16[128,1536]{1,0:T(8,128)(2,1)S(1)} %pad_maximum_fusion.2.refs_0_), channel_id=1, source_target_pairs={{0,8},{1,57},{8,0},{9,17},{16,24},{17,9},{24,16},{25,33},{32,40},{... | collective-permute-start | bytes 1179656 | tf_op jit(solution)/shard_map/ppermute | solution.py:63
  116.7 11.7 %collective-permute-start.25 = (bf16[128,1536]{1,0:T(8,128)(2,1)S(1)}, bf16[128,1536]{1,0:T(8,128)(2,1)S(1)}, u32[]{:S(2)}, u32[]{:S(2)}) collective-permute-start(bf16[128,1536]{1,0:T(8,128)(2,1)S(1)} %pad_maximum_fusion.2.refs_0_), channel_id=1, source_target_pairs={{0,64},{1,193},{64,128},{65,1},{128,192},{129,65},{192,0},{193,129... | collective-permute-start | bytes 1179656 | tf_op jit(solution)/shard_map/ppermute | solution.py:79
  119.2 10.7 %collective-permute-start.26 = (bf16[128,1536]{1,0:T(8,128)(2,1)S(1)}, bf16[128,1536]{1,0:T(8,128)(2,1)S(1)}, u32[]{:S(2)}, u32[]{:S(2)}) collective-permute-start(bf16[128,1536]{1,0:T(8,128)(2,1)S(1)} %pad_maximum_fusion.2.refs_0_), channel_id=1, source_target_pairs={{0,192},{1,65},{64,0},{65,129},{128,64},{129,193},{192,128},{193,1... | collective-permute-start | bytes 1179656 | tf_op jit(solution)/shard_map/ppermute | solution.py:79
  119.9 19.7 %collective-permute-start.32 = (bf16[136,1536]{1,0:T(8,128)(2,1)S(1)}, bf16[136,1536]{1,0:T(8,128)(2,1)S(1)}, u32[]{:S(2)}, u32[]{:S(2)}) collective-permute-start(bf16[136,1536]{1,0:T(8,128)(2,1)S(1)} %pad_maximum_fusion.1), channel_id=1, source_target_pairs={{0,6},{1,3},{2,4},{3,1},{4,2},{5,7},{6,0},{7,5},{8,14},{9,11},{10,... | collective-permute-start | bytes 1253384 | tf_op jit(solution)/shard_map/ppermute | solution.py:67
  129.9 9.7 %collective-permute-start.27 = (bf16[128,1536]{1,0:T(8,128)(2,1)S(1)}, bf16[128,1536]{1,0:T(8,128)(2,1)S(1)}, u32[]{:S(2)}, u32[]{:S(2)}) collective-permute-start(bf16[128,1536]{1,0:T(8,128)(2,1)S(1)} %collective-permute-done.24.refs_1_), channel_id=1, source_target_pairs={{0,192},{1,65},{64,0},{65,129},{128,64},{129,193},{192,128},{193,1... | collective-permute-start | bytes 1179656 | tf_op jit(solution)/shard_map/ppermute | solution.py:79
  130.9 16.5 %collective-permute-start.33 = (bf16[128,1536]{1,0:T(8,128)(2,1)S(1)}, bf16[128,1536]{1,0:T(8,128)(2,1)S(1)}, u32[]{:S(2)}, u32[]{:S(2)}) collective-permute-start(bf16[128,1536]{1,0:T(8,128)(2,1)S(1)} %collective-permute-done.24.refs_1_), channel_id=1, source_target_pairs={{0,64},{1,193},{64,128},{65,1},{128,192},{129,65},{192,0},{193,129... | collective-permute-start | bytes 1179656 | tf_op jit(solution)/shard_map/ppermute | solution.py:79
  131.9 15.5 %collective-permute-start.28 = (bf16[128,1536]{1,0:T(8,128)(2,1)S(1)}, bf16[128,1536]{1,0:T(8,128)(2,1)S(1)}, u32[]{:S(2)}, u32[]{:S(2)}) collective-permute-start(bf16[128,1536]{1,0:T(8,128)(2,1)S(1)} %collective-permute-done.25.refs_3_), channel_id=1, source_target_pairs={{0,64},{1,193},{64,128},{65,1},{128,192},{129,65},{192,0},{193,129... | collective-permute-start | bytes 1179656 | tf_op jit(solution)/shard_map/ppermute | solution.py:79
  139.6 7.8 %collective-permute-start.29 = (bf16[128,1536]{1,0:T(8,128)(2,1)S(1)}, bf16[128,1536]{1,0:T(8,128)(2,1)S(1)}, u32[]{:S(2)}, u32[]{:S(2)}) collective-permute-start(bf16[128,1536]{1,0:T(8,128)(2,1)S(1)} %collective-permute-done.27.refs_0_), channel_id=1, source_target_pairs={{0,192},{1,65},{64,0},{65,129},{128,64},{129,193},{192,128},{193,1... | collective-permute-start | bytes 1179656 | tf_op jit(solution)/shard_map/ppermute | solution.py:79

commit v4 on v3

--- a/solution.py
+++ b/solution.py
@@ -95,11 +95,11 @@
 def place_kernel(rs, place, *refs):
     parts, out, sems = refs[: len(rs)], refs[-2], refs[-1]
     copies = []
-    for i, (part, (r, h)) in enumerate(zip(parts, rs)):
-        for j in range(4):
-            row = lax.rem(place[0] + r + 2 * (r % 2) * place[2], 4) * TILE + place[4 + 4 * h + j] * BLOCK
-            rows = out.at[pl.ds(pl.multiple_of(row, BLOCK), BLOCK)]
-            copies.append(pltpu.make_async_copy(part.at[pl.ds(j * BLOCK, BLOCK)], rows, sems.at[4 * i + j]))
+    for part, (r, first) in zip(parts, rs):
+        for j in range(part.shape[0] // BLOCK):
+            at = lax.rem(place[0] + r + 2 * (r % 2) * place[2], 4) * TILE + place[4 + first + j] * BLOCK
+            rows = out.at[pl.ds(pl.multiple_of(at, BLOCK), BLOCK)]
+            copies.append(pltpu.make_async_copy(part.at[pl.ds(j * BLOCK, BLOCK)], rows, sems.at[len(copies)]))
     for copy in copies:
         copy.start()
     for copy in copies:
@@ -113,7 +113,7 @@
         out_shape=jax.ShapeDtypeStruct((1024, D), BF16),
         in_specs=[pl.BlockSpec(memory_space=pltpu.SMEM)] + whole + [pl.BlockSpec(memory_space=pl.ANY)] * (to is not None),
         out_specs=pl.BlockSpec(memory_space=pl.ANY),
-        scratch_shapes=[pltpu.SemaphoreType.DMA((4 * len(parts),))],
+        scratch_shapes=[pltpu.SemaphoreType.DMA((sum(part.shape[0] for part in parts) // BLOCK,))],
         input_output_aliases={} if to is None else {len(parts) + 1: 0},
         compiler_params=pltpu.CompilerParams(vmem_limit_bytes=16 << 20),
         cost_estimate=pl.CostEstimate(flops=0, bytes_accessed=4 * 128 * len(parts) * D, transcendentals=0),
@@ -480,16 +480,23 @@
     own = step(half_step, [sums, masses, exchange(send, 1)], [sent(64)])
     a = step(last_step, [own, exchange(own, 2)], [((64, D), BF16)])
 
-    a0 = jnp.concatenate([a, exchange(a, 1)], axis=0)
+    b = exchange(a, 1)
+    back_a, next_a = forward(a, 1), forward(a, -1)
+    a0 = jnp.concatenate([a, b], axis=0)
     a1 = exchange(a0, 0)
-    back0, next0 = forward(a0, 1), forward(a0, -1)
-    a1, back0, next0 = lax.optimization_barrier((a1, back0, next0))
+    back_b, next_b = forward(b, 1), forward(b, -1)
+    far_a = forward(back_a, 1)
+    a1, back_b, next_b = lax.optimization_barrier((a1, back_b, next_b))
     next1, back1 = forward(a1, -1), forward(a1, 1)
-    far0, far1 = forward(back0, 1), forward(next1, -1)
-    new_fine = put_rows(place, [a0, a1, next0, back0], [(0, 0), (0, 1), (1, 0), (3, 0)])
+    far_b, far1 = forward(back_b, 1), forward(next1, -1)
+    new_fine = put_rows(
+        place, [a0, a1, next_a, next_b, back_a, back_b], [(0, 0), (0, 4), (1, 0), (1, 2), (3, 0), (3, 2)]
+    )
     new_coarse = coarse_rows(*c_sums)
     far1, new_coarse, new_fine = lax.optimization_barrier((far1, new_coarse, new_fine))
-    new_fine = put_rows(place, [next1, far0, far1, back1], [(1, 1), (2, 0), (2, 1), (3, 1)], new_fine)
+    new_fine = put_rows(
+        place, [next1, far_a, far_b, far1, back1], [(1, 4), (2, 0), (2, 2), (2, 4), (3, 4)], new_fine
+    )
     return new_fine, new_coarse
 
 

time: 152 us -> 156 us (1.026); the launches traced: 149 us -> 156 us
  starting transfers between devices: 44.7 us -> 50 us
    ppermute x6 -> x9, starting transfers between devices: 6.7 us -> 11.9 us  [forward(): return lax.ppermute(x, ('y', 'c'), pairs)]
    ppermute x6 -> x9, waiting for transfers between devices: 17.9 us -> 21.1 us  [forward(): return lax.ppermute(x, ('y', 'c'), pairs)]
    ppermute x8, waiting for transfers between devices: 15.7 us -> 13.7 us  [exchange(): lax.ppermute(x, ('z', 'c'), [(z * 2 + c, partner(step, z, c) * 2 + c) for...]
  transfers between devices with their start and end apart: 35 -> 38, of which waited for: 16 -> 16; matrix products, arithmetic and copies ran while one was open for 6% -> 6% of each run, Pallas kernels for 17% -> 17%
where the time goes in v4:
time: 156 us
  waiting for transfers between devices  53.7 us (34%)
  starting transfers between devices  50 us (32%)
  Pallas kernels  38.9 us (25%)
  local copies, waits for them, and re-layouts  5.4 us (3%)
  matrix products  3.45 us (2%)
  other arithmetic  3.2 us (2%)
    ppermute x9, waiting for transfers between devices, forward(): return lax.ppermute(x, ('y', 'c'), pairs)  21.1 us
    ppermute x8, starting transfers between devices, exchange(): lax.ppermute(x, ('z', 'c'), [(z * 2 + c, partner(step, z, c) * 2 + c) for...  20 us
    ppermute x8, waiting for transfers between devices, exchange(): lax.ppermute(x, ('z', 'c'), [(z * 2 + c, partner(step, z, c) * 2 + c) for...  13.7 us
    pallas_call x3, Pallas kernels, scores(): pl.pallas_call(functools.partial(score_kernel, len(es), len(stats)), grid...  13.4 us
    ppermute x10, starting transfers between devices, shift(): return lax.ppermute(x, axis, [(i, (i + k) % n) for i in range(n)])  12.1 us
    ppermute x10, waiting for transfers between devices, shift(): return lax.ppermute(x, axis, [(i, (i + k) % n) for i in range(n)])  12.1 us
    ppermute x9, starting transfers between devices, forward(): return lax.ppermute(x, ('y', 'c'), pairs)  11.9 us
    pallas_call x1, Pallas kernels, fine_sums(): pl.pallas_call(functools.partial(rest_kernel, len(es)), grid_spec=pltpu.P...  7.18 us
  transfers between devices with their start and end apart: 38, of which 16 were waited for; matrix products, arithmetic and copies ran while one was open for 6% of the time, Pallas kernels for 17%

profile of v4, /device:TPU:80, one launch (start us, length us, event | category | flops | bytes accessed | tf_op | source)
XLA Modules:
  0.0 155.9 jit_solution(15895145672295481427)
XLA Ops:
  0.7 1.2 fusion.23
  1.9 2.8 %collective-permute-start.3 = (bf16[64,1536]{1,0:T(8,128)(2,1)S(1)}, bf16[64,1536]{1,0:T(8,128)(2,1)S(1)}, u32[]{:S(2)}, u32[]{:S(2)}) collective-permute-start(bf16[64,1536]{1,0:T(8,128)(2,1)S(1)} %get-tuple-element.113), channel_id=1, source_target_pairs={{0,6},{2,0},{4,2},{6,4},{1,7},{3,1},{5,3},{7,5},{8,14},{10,8},{12,... | collective-permute-start | bytes 589832 | tf_op jit(solution)/shard_map/ppermute | solution.py:74
  4.8 0.8 collective-permute-start.1
  5.5 2.5 %collective-permute-start.2 = (bf16[64,1536]{1,0:T(8,128)(2,1)S(1)}, bf16[64,1536]{1,0:T(8,128)(2,1)}, u32[]{:S(2)}, u32[]{:S(2)}) collective-permute-start(bf16[64,1536]{1,0:T(8,128)(2,1)S(1)} %get-tuple-element.112), channel_id=1, source_target_pairs={{0,6},{2,0},{4,2},{6,4},{1,7},{3,1},{5,3},{7,5},{8,14},{10,8},{12,... | collective-permute-start | bytes 589832 | tf_op jit(solution)/shard_map/ppermute | solution.py:74
  8.1 1.9 %collective-permute-done.3.refs_1_.refs_3_ = bf16[64,1536]{1,0:T(8,128)(2,1)S(1)} collective-permute-done((bf16[64,1536]{1,0:T(8,128)(2,1)S(1)}, bf16[64,1536]{1,0:T(8,128)(2,1)S(1)}, u32[]{:S(2)}, u32[]{:S(2)}) %collective-permute-start.3) | collective-permute-done | bytes 196640 | tf_op jit(solution)/shard_map/ppermute | solution.py:74
  10.0 3.8 %collective-permute-done.6.refs_4_.refs_6_ = bf16[64,1536]{1,0:T(8,128)(2,1)} collective-permute-done((bf16[64,1536]{1,0:T(8,128)(2,1)S(1)}, bf16[64,1536]{1,0:T(8,128)(2,1)}, u32[]{:S(2)}, u32[]{:S(2)}) %collective-permute-start.6) | collective-permute-done | bytes 196640 | tf_op jit(solution)/shard_map/ppermute | solution.py:74
  13.8 2.0 %collective-permute-start.9 = (bf16[64,1536]{1,0:T(8,128)(2,1)}, bf16[64,1536]{1,0:T(8,128)(2,1)}, u32[]{:S(2)}, u32[]{:S(2)}) collective-permute-start(bf16[64,1536]{1,0:T(8,128)(2,1)} %collective-permute-done.6.refs_4_.refs_6_), channel_id=1, source_target_pairs={{0,2},{2,4},{4,6},{6,0},{1,3},{3,5},{5,7},{7,1},{8,10},{10,12},{12... | collective-permute-start | bytes 589832 | tf_op jit(solution)/shard_map/ppermute | solution.py:74
  15.9 4.0 %fine_scores.3 = (f32[1024,256]{1,0:T(8,128)}, f32[2,256]{1,0:T(2,128)}, f32[4,128]{1,0:T(4,128)}) custom-call(bf16[128,1536]{1,0:T(8,128)(2,1)} %refs_0_.5, bf16[128,1536]{1,0:T(8,128)(2,1)} %copy-done.11, bf16[1024,1536]{1,0:T(8,128)(2,1)} %fine.1), custom_call_target="tpu_custom_call" | custom-call | flops 805306368 | bytes 6291456 | tf_op jit(solution)/shard_map/fine_scores/pallas_call | solution.py:165
  19.9 0.5 collective-permute-start.4
  20.5 1.7 %collective-permute-done.9.refs_0_.refs_10_ = bf16[64,1536]{1,0:T(8,128)(2,1)} collective-permute-done((bf16[64,1536]{1,0:T(8,128)(2,1)}, bf16[64,1536]{1,0:T(8,128)(2,1)}, u32[]{:S(2)}, u32[]{:S(2)}) %collective-permute-start.9) | collective-permute-done | bytes 196640 | tf_op jit(solution)/shard_map/ppermute | solution.py:74
  22.3 0.5 collective-permute-start.12
  22.8 5.4 %fine_scores.4 = (f32[1024,512]{1,0:T(8,128)}, f32[2,512]{1,0:T(2,128)}, f32[8,128]{1,0:T(8,128)}) custom-call(bf16[64,1536]{1,0:T(8,128)(2,1)} %collective-permute-done.2.refs_0_.refs_2_, bf16[64,1536]{1,0:T(8,128)(2,1)} %copy-done.13, bf16[64,1536]{1,0:T(8,128)(2,1)} %collective-permute-done.4.refs_2_.refs_4_, bf16[64,1536]{1,0:T(8,128)(2,1)} %copy-done.14, ...), custom_call_target="tpu_custom_call" | custom-call | flops 1610612736 | bytes 6291456 | tf_op jit(solution)/shard_map/fine_scores/pallas_call | solution.py:165
  28.3 0.7 copy-done.12
  28.9 4.0 %fine_scores.5 = (f32[1024,256]{1,0:T(8,128)}, f32[2,256]{1,0:T(2,128)}, f32[8,16,128]{2,1,0:T(8,128)}) custom-call(bf16[64,1536]{1,0:T(8,128)(2,1)} %collective-permute-done.9.refs_0_.refs_10_, bf16[64,1536]{1,0:T(8,128)(2,1)} %collective-permute-done.10.refs_1_.refs_11_, bf16[64,1536]{1,0:T(8,128)(2,1)} %copy-done.12, ...), custom_call_target="tpu_custom_call" | custom-call | flops 805306368 | bytes 6291456 | tf_op jit(solution)/shard_map/fine_scores/pallas_call | solution.py:165
  32.9 3.4 %all-to-all-start = ((f32[8,16,128]{2,1,0:T(8,128)}), f32[8,16,128]{2,1,0:T(8,128)S(1)}, u32[]{:S(2)}, u32[]{:S(2)}) async-start(f32[8,16,128]{2,1,0:T(8,128)} %get-tuple-element.70), calls=%async_computation | async-start | bytes 131072 | tf_op jit(solution)/shard_map/all_to_all | solution.py:459
  36.3 0.7 dynamic-slice_bitcast_fusion
  37.0 0.7 concatenate.22.place
  37.7 4.2 %all-to-all-done.refs_20_ = f32[8,16,128]{2,1,0:T(8,128)S(1)} async-done(((f32[8,16,128]{2,1,0:T(8,128)}), f32[8,16,128]{2,1,0:T(8,128)S(1)}, u32[]{:S(2)}, u32[]{:S(2)}) %all-to-all-start) | async-done | bytes 65568 | tf_op jit(solution)/shard_map/all_to_all | solution.py:459
  41.8 0.6 copy-done.15
  42.5 7.1 %first_sums.1 = (f32[128,1536]{1,0:T(8,128)}, f32[128,128]{1,0:T(8,128)}, bf16[128,1664]{1,0:T(8,128)(2,1)}, f32[128,1536]{1,0:T(8,128)}, f32[128,128]{1,0:T(8,1...) custom-call(s32[20]{0:T(128)} %concatenate.22.place, bf16[128,1536]{1,0:T(8,128)(2,1)} %refs_0_.5, ...), custom_call_target="tpu_custom_call" | custom-call | flops 1610612736 | bytes 5242880 | tf_op jit(solution)/shard_map/first_sums/pallas_call | solution.py:279
  49.6 2.2 %collective-permute-start.13 = (bf16[128,1664]{1,0:T(8,128)(2,1)}, bf16[128,1664]{1,0:T(8,128)(2,1)S(1)}, u32[]{:S(2)}, u32[]{:S(2)}) collective-permute-start(bf16[128,1664]{1,0:T(8,128)(2,1)} %get-tuple-element.78), channel_id=1, source_target_pairs={{0,8},{1,57},{8,0},{9,17},{16,24},{17,9},{24,16},{25,33},{32,40},{... | collective-permute-start | bytes 1277960 | tf_op jit(solution)/shard_map/ppermute | solution.py:63
  51.9 7.2 %rest_sums.1 = (f32[128,1536]{1,0:T(8,128)}, f32[128,128]{1,0:T(8,128)}, bf16[128,1664]{1,0:T(8,128)(2,1)}, f32[128,1536]{1,0:T(8,128)}, f32[128,128]{1,0:T(8,128)}, /*index=5*/bf16[128,1664]{1,0:T(8,128)(2,1)}) custom-call(s32[20]{0:T(128)} %concatenate.22.place, bf16[128,1536]{1,0:T(8,128)(2,1)} %refs_0_.5, bf16[128,1536]{1,0:T(8,128)(2,1)} %copy-done.11, ...), custom_call_target="tpu_custom_call" | custom-call | flops 1610612736 | bytes 10485760 | tf_op jit(solution)/shard_map/rest_sums/pallas_call | solution.py:295
  59.1 2.0 %collective-permute-start.14 = (bf16[128,1664]{1,0:T(8,128)(2,1)}, bf16[128,1664]{1,0:T(8,128)(2,1)S(1)}, u32[]{:S(2)}, u32[]{:S(2)}) collective-permute-start(bf16[128,1664]{1,0:T(8,128)(2,1)} %get-tuple-element.81), channel_id=1, source_target_pairs={{0,8},{1,57},{8,0},{9,17},{16,24},{17,9},{24,16},{25,33},{32,40},{... | collective-permute-start | bytes 1277960 | tf_op jit(solution)/shard_map/ppermute | solution.py:63
  61.4 1.4 collective-permute-start.16
  62.8 0.7 collective-permute-start.19
  63.5 3.8 %collective-permute-done.16.far = bf16[64,1664]{1,0:T(8,128)(2,1)S(1)} collective-permute-done((bf16[64,1664]{1,0:T(8,128)(2,1)S(1)}, bf16[64,1664]{1,0:T(8,128)(2,1)S(1)}, u32[]{:S(2)}, u32[]{:S(2)}) %collective-permute-start.16) | collective-permute-done | bytes 213024 | tf_op jit(solution)/shard_map/ppermute | solution.py:74
  67.3 1.3 add_side_step.2
  68.7 1.4 collective-permute-start.17
  70.0 2.1 %collective-permute-done.18.got = bf16[128,1664]{1,0:T(8,128)(2,1)S(1)} collective-permute-done((bf16[128,1664]{1,0:T(8,128)(2,1)}, bf16[128,1664]{1,0:T(8,128)(2,1)S(1)}, u32[]{:S(2)}, u32[]{:S(2)}) %collective-permute-start.18) | collective-permute-done | bytes 426016 | tf_op jit(solution)/shard_map/ppermute | solution.py:63
  72.1 1.1 copy-done.4
  73.2 0.2 add_side_step.3
  73.5 0.5 collective-permute-start.20
  74.0 3.5 %fusion.24 = (f32[1024]{0:T(1024)S(1)}, f32[1024,1024]{1,0:T(8,128)S(1)}) fusion(bf16[1024,1536]{1,0:T(8,128)(2,1)S(1)} %copy-done, bf16[1024,1536]{1,0:T(8,128)(2,1)S(1)} %copy-done.1), kind=kOutput, calls=%fused_computation.49 | convolution fusion | flops 3223321600 | bytes 10489856 | tf_op jit(solution)/shard_map/dot_general | solution.py:430
  77.5 0.6 exponential_reduce_fusion
  78.1 5.0 %coarse_sums.1 = (f32[4,128,1536]{2,1,0:T(8,128)S(1)}, bf16[4,144,1536]{2,1,0:T(8,128)(2,1)S(1)}, f32[4,1,128]{2,1,0:T(1,128)S(1)}) custom-call(s32[20]{0:T(128)S(1)} %copy-done.10, f32[1024,1024]{1,0:T(8,128)S(1)} %get-tuple-element.119.s, f32[1,1024]{1,0:T(1,128)S(1)} %bitcast.39, f32[1,1024]{1,0:T(1,128)S(1)} %bitcast.40, bf16[1024,1536]{1,0:T(8,128)(2,1)S(1)} %copy-done.1), custom_call_target="tpu_custom_call" | custom-call | flops 3221225472 | bytes 12582912 | tf_op jit(solution)/shard_map/coarse_sums/pallas_call | solution.py:398
  83.2 0.8 collective-permute-done.20.down
  84.0 0.4 add_own_step.1
  84.4 0.6 collective-permute-start.21
  85.0 2.7 %collective-permute-done.32 = bf16[4,144,1536]{2,1,0:T(8,128)(2,1)S(1)} collective-permute-done((bf16[4,144,1536]{2,1,0:T(8,128)(2,1)S(1)}, bf16[4,144,1536]{2,1,0:T(8,128)(2,1)S(1)}, u32[]{:S(2)}, u32[]{:S(2)}) %collective-permute-start.32) | collective-permute-done | bytes 1769504 | tf_op jit(solution)/shard_map/ppermute | solution.py:83
  87.7 0.5 convert_element_type.18
  88.1 0.6 slice_add_fusion
  88.9 0.7 collective-permute-start.33
  89.6 1.0 collective-permute-done.21.got
  90.7 5.0 %collective-permute-start.22 = (bf16[64,1664]{1,0:T(8,128)(2,1)S(1)}, bf16[64,1664]{1,0:T(8,128)(2,1)S(1)}, u32[]{:S(2)}, u32[]{:S(2)}) collective-permute-start(bf16[64,1664]{1,0:T(8,128)(2,1)S(1)} %add_half_step.1.own), channel_id=1, source_target_pairs={{0,24},{1,41},{8,48},{9,33},{16,40},{17,57},{24,0},{25,49},{32,56}... | collective-permute-start | bytes 638984 | tf_op jit(solution)/shard_map/ppermute | solution.py:63
  95.7 6.3 %collective-permute-done.22.got = bf16[64,1664]{1,0:T(8,128)(2,1)S(1)} collective-permute-done((bf16[64,1664]{1,0:T(8,128)(2,1)S(1)}, bf16[64,1664]{1,0:T(8,128)(2,1)S(1)}, u32[]{:S(2)}, u32[]{:S(2)}) %collective-permute-start.22) | collective-permute-done | bytes 213024 | tf_op jit(solution)/shard_map/ppermute | solution.py:63
  102.2 1.9 %collective-permute-start.23 = (bf16[64,1536]{1,0:T(8,128)(2,1)S(1)}, bf16[64,1536]{1,0:T(8,128)(2,1)S(1)}, u32[]{:S(2)}, u32[]{:S(2)}) collective-permute-start(bf16[64,1536]{1,0:T(8,128)(2,1)S(1)} %add_last_step.1), channel_id=1, source_target_pairs={{0,56},{1,9},{8,16},{9,1},{16,8},{17,25},{24,32},{25,17},{32,24},{... | collective-permute-start | bytes 589832 | tf_op jit(solution)/shard_map/ppermute | solution.py:63
  104.2 4.3 %collective-permute-done.23 = bf16[64,1536]{1,0:T(8,128)(2,1)S(1)} collective-permute-done((bf16[64,1536]{1,0:T(8,128)(2,1)S(1)}, bf16[64,1536]{1,0:T(8,128)(2,1)S(1)}, u32[]{:S(2)}, u32[]{:S(2)}) %collective-permute-start.23) | collective-permute-done | bytes 196640 | tf_op jit(solution)/shard_map/ppermute | solution.py:63
  108.5 8.0 %collective-permute-start.24 = (bf16[128,1536]{1,0:T(8,128)(2,1)S(1)}, bf16[128,1536]{1,0:T(8,128)(2,1)S(1)}, u32[]{:S(2)}, u32[]{:S(2)}) collective-permute-start(bf16[128,1536]{1,0:T(8,128)(2,1)S(1)} %pad_maximum_fusion.2.refs_0_), channel_id=1, source_target_pairs={{0,8},{1,57},{8,0},{9,17},{16,24},{17,9},{24,16},{25,33},{32,40},{... | collective-permute-start | bytes 1179656 | tf_op jit(solution)/shard_map/ppermute | solution.py:63
  116.5 2.5 %collective-permute-start.25 = (bf16[64,1536]{1,0:T(8,128)(2,1)S(1)}, bf16[64,1536]{1,0:T(8,128)(2,1)S(1)}, u32[]{:S(2)}, u32[]{:S(2)}) collective-permute-start(bf16[64,1536]{1,0:T(8,128)(2,1)S(1)} %collective-permute-done.23), channel_id=1, source_target_pairs={{0,64},{1,193},{64,128},{65,1},{128,192},{129,65},{192,0},{193,129... | collective-permute-start | bytes 589832 | tf_op jit(solution)/shard_map/ppermute | solution.py:79
  119.4 0.2 slice_add_fusion.1
  119.8 0.7 collective-permute-start.34
  120.5 3.9 %collective-permute-done.25.refs_5_ = bf16[64,1536]{1,0:T(8,128)(2,1)S(1)} collective-permute-done((bf16[64,1536]{1,0:T(8,128)(2,1)S(1)}, bf16[64,1536]{1,0:T(8,128)(2,1)S(1)}, u32[]{:S(2)}, u32[]{:S(2)}) %collective-permute-start.25) | collective-permute-done | bytes 196640 | tf_op jit(solution)/shard_map/ppermute | solution.py:79
  124.4 1.7 %collective-permute-done.26.refs_3_ = bf16[64,1536]{1,0:T(8,128)(2,1)S(1)} collective-permute-done((bf16[64,1536]{1,0:T(8,128)(2,1)S(1)}, bf16[64,1536]{1,0:T(8,128)(2,1)S(1)}, u32[]{:S(2)}, u32[]{:S(2)}) %collective-permute-start.26) | collective-permute-done | bytes 196640 | tf_op jit(solution)/shard_map/ppermute | solution.py:79
  126.1 2.0 %collective-permute-start.28 = (bf16[64,1536]{1,0:T(8,128)(2,1)S(1)}, bf16[64,1536]{1,0:T(8,128)(2,1)S(1)}, u32[]{:S(2)}, u32[]{:S(2)}) collective-permute-start(bf16[64,1536]{1,0:T(8,128)(2,1)S(1)} %add_last_step.1), channel_id=1, source_target_pairs={{0,64},{1,193},{64,128},{65,1},{128,192},{129,65},{192,0},{193,129... | collective-permute-start | bytes 589832 | tf_op jit(solution)/shard_map/ppermute | solution.py:79
  128.1 3.6 %collective-permute-done.28.refs_4_ = bf16[64,1536]{1,0:T(8,128)(2,1)S(1)} collective-permute-done((bf16[64,1536]{1,0:T(8,128)(2,1)S(1)}, bf16[64,1536]{1,0:T(8,128)(2,1)S(1)}, u32[]{:S(2)}, u32[]{:S(2)}) %collective-permute-start.28) | collective-permute-done | bytes 196640 | tf_op jit(solution)/shard_map/ppermute | solution.py:79
  131.8 2.0 %collective-permute-start.29 = (bf16[64,1536]{1,0:T(8,128)(2,1)S(1)}, bf16[64,1536]{1,0:T(8,128)(2,1)S(1)}, u32[]{:S(2)}, u32[]{:S(2)}) collective-permute-start(bf16[64,1536]{1,0:T(8,128)(2,1)S(1)} %collective-permute-done.28.refs_4_), channel_id=1, source_target_pairs={{0,64},{1,193},{64,128},{65,1},{128,192},{129,65},{192,0},{193,129... | collective-permute-start | bytes 589832 | tf_op jit(solution)/shard_map/ppermute | solution.py:79
  133.8 3.3 %collective-permute-start.36 = (bf16[128,1536]{1,0:T(8,128)(2,1)S(1)}, bf16[128,1536]{1,0:T(8,128)(2,1)S(1)}, u32[]{:S(2)}, u32[]{:S(2)}) collective-permute-start(bf16[128,1536]{1,0:T(8,128)(2,1)S(1)} %collective-permute-done.24.refs_1_), channel_id=1, source_target_pairs={{0,64},{1,193},{64,128},{65,1},{128,192},{129,65},{192,0},{193,129... | collective-permute-start | bytes 1179656 | tf_op jit(solution)/shard_map/ppermute | solution.py:79
  137.1 5.2 %collective-permute-done.35.refs_2_ = bf16[64,1536]{1,0:T(8,128)(2,1)S(1)} collective-permute-done((bf16[64,1536]{1,0:T(8,128)(2,1)S(1)}, bf16[64,1536]{1,0:T(8,128)(2,1)S(1)}, u32[]{:S(2)}, u32[]{:S(2)}) %collective-permute-start.35) | collective-permute-done | bytes 196640 | tf_op jit(solution)/shard_map/ppermute | solution.py:79
  142.3 1.9 %collective-permute-start.30 = (bf16[64,1536]{1,0:T(8,128)(2,1)S(1)}, bf16[64,1536]{1,0:T(8,128)(2,1)S(1)}, u32[]{:S(2)}, u32[]{:S(2)}) collective-permute-start(bf16[64,1536]{1,0:T(8,128)(2,1)S(1)} %collective-permute-done.25.refs_5_), channel_id=1, source_target_pairs={{0,64},{1,193},{64,128},{65,1},{128,192},{129,65},{192,0},{193,129... | collective-permute-start | bytes 589832 | tf_op jit(solution)/shard_map/ppermute | solution.py:79
  144.2 1.8 %put_rows.2.refs_5_ = bf16[1024,1536]{1,0:T(8,128)(2,1)} custom-call(s32[20]{0:T(128)S(1)} %copy-done.10, bf16[128,1536]{1,0:T(8,128)(2,1)S(1)} %pad_maximum_fusion.2.refs_0_, bf16[128,1536]{1,0:T(8,128)(2,1)S(1)} %collective-permute-done.24.refs_1_, bf16[64,1536]{1,0:T(8,128)(2,1)S(1)} %collective-permute-done.35.refs_2_, ...), custom_call_target="tpu_custom_call" | custom-call | bytes 4718592 | tf_op jit(solution)/shard_map/put_rows/pallas_call | solution.py:111
  146.0 0.2 collective-permute-start.31
  146.3 0.9 fusion.3
  147.2 6.6 %collective-permute-done.31.refs_3_ = bf16[128,1536]{1,0:T(8,128)(2,1)S(1)} collective-permute-done((bf16[128,1536]{1,0:T(8,128)(2,1)S(1)}, bf16[128,1536]{1,0:T(8,128)(2,1)S(1)}, u32[]{:S(2)}, u32[]{:S(2)}) %collective-permute-start.31) | collective-permute-done | bytes 393248 | tf_op jit(solution)/shard_map/ppermute | solution.py:79
  153.9 1.8 %put_rows.3 = bf16[1024,1536]{1,0:T(8,128)(2,1)} custom-call(s32[20]{0:T(128)S(1)} %copy-done.10, bf16[128,1536]{1,0:T(8,128)(2,1)S(1)} %collective-permute-done.27.refs_0_, bf16[64,1536]{1,0:T(8,128)(2,1)S(1)} %collective-permute-done.29.refs_1_, bf16[64,1536]{1,0:T(8,128)(2,1)S(1)} %collective-permute-done.30.refs_2_, ...), custom_call_target="tpu_custom_call", output_to_operand_aliasing={{}: (6, {})} | custom-call | bytes 3932160 | tf_op jit(solution)/shard_map/put_rows/pallas_call | solution.py:111
  (83 shorter events, 1.9 us)
Async XLA Ops:
  0.6 73.4 %copy-start = (bf16[1024,1536]{1,0:T(8,128)(2,1)S(1)}, bf16[1024,1536]{1,0:T(8,128)(2,1)}, u32[]{:S(2)}) copy-start(bf16[1024,1536]{1,0:T(8,128)(2,1)} %param.7) | copy-start | bytes 9437188
  0.6 13.2 %collective-permute-start = (bf16[128,1536]{1,0:T(8,128)(2,1)}, bf16[128,1536]{1,0:T(8,128)(2,1)S(1)}, u32[]{:S(2)}, u32[]{:S(2)}) collective-permute-start(bf16[128,1536]{1,0:T(8,128)(2,1)} %refs_0_.5), channel_id=1, source_target_pairs={{0,1},{1,0},{2,3},{3,2},{4,5},{5,4},{6,7},{7,6},{8,9},{9,8},{10,11... | collective-permute-start | bytes 1179656 | tf_op jit(solution)/shard_map/ppermute | solution.py:83
  1.9 8.1 %collective-permute-start.3 = (bf16[64,1536]{1,0:T(8,128)(2,1)S(1)}, bf16[64,1536]{1,0:T(8,128)(2,1)S(1)}, u32[]{:S(2)}, u32[]{:S(2)}) collective-permute-start(bf16[64,1536]{1,0:T(8,128)(2,1)S(1)} %get-tuple-element.113), channel_id=1, source_target_pairs={{0,6},{2,0},{4,2},{6,4},{1,7},{3,1},{5,3},{7,5},{8,14},{10,8},{12,... | collective-permute-start | bytes 589832 | tf_op jit(solution)/shard_map/ppermute | solution.py:74
  4.8 9.1 %collective-permute-start.6 = (bf16[64,1536]{1,0:T(8,128)(2,1)S(1)}, bf16[64,1536]{1,0:T(8,128)(2,1)}, u32[]{:S(2)}, u32[]{:S(2)}) collective-permute-start(bf16[64,1536]{1,0:T(8,128)(2,1)S(1)} %get-tuple-element.112), channel_id=1, source_target_pairs={{0,2},{2,4},{4,6},{6,0},{1,3},{3,5},{5,7},{7,1},{8,10},{10,12},{12... | collective-permute-start | bytes 589832 | tf_op jit(solution)/shard_map/ppermute | solution.py:74
  4.8 15.1 %collective-permute-start.1 = (bf16[64,1536]{1,0:T(8,128)(2,1)S(1)}, bf16[64,1536]{1,0:T(8,128)(2,1)}, u32[]{:S(2)}, u32[]{:S(2)}) collective-permute-start(bf16[64,1536]{1,0:T(8,128)(2,1)S(1)} %get-tuple-element.113), channel_id=1, source_target_pairs={{0,2},{2,4},{4,6},{6,0},{1,3},{3,5},{5,7},{7,1},{8,10},{10,12},{12... | collective-permute-start | bytes 589832 | tf_op jit(solution)/shard_map/ppermute | solution.py:74
  5.5 14.4 %collective-permute-start.2 = (bf16[64,1536]{1,0:T(8,128)(2,1)S(1)}, bf16[64,1536]{1,0:T(8,128)(2,1)}, u32[]{:S(2)}, u32[]{:S(2)}) collective-permute-start(bf16[64,1536]{1,0:T(8,128)(2,1)S(1)} %get-tuple-element.112), channel_id=1, source_target_pairs={{0,6},{2,0},{4,2},{6,4},{1,7},{3,1},{5,3},{7,5},{8,14},{10,8},{12,... | collective-permute-start | bytes 589832 | tf_op jit(solution)/shard_map/ppermute | solution.py:74
  10.0 10.5 %copy-start.13 = (bf16[64,1536]{1,0:T(8,128)(2,1)}, bf16[64,1536]{1,0:T(8,128)(2,1)S(1)}, u32[]{:S(2)}) copy-start(bf16[64,1536]{1,0:T(8,128)(2,1)S(1)} %collective-permute-done.3.refs_1_.refs_3_) | copy-start | bytes 589828
  10.0 10.4 %collective-permute-start.5 = (bf16[64,1536]{1,0:T(8,128)(2,1)S(1)}, bf16[64,1536]{1,0:T(8,128)(2,1)S(1)}, u32[]{:S(2)}, u32[]{:S(2)}) collective-permute-start(bf16[64,1536]{1,0:T(8,128)(2,1)S(1)} %collective-permute-done.3.refs_1_.refs_3_), channel_id=1, source_target_pairs={{0,1},{1,0},{2,3},{3,2},{4,5},{5,4},{6,7},{7,6},{8,9},{9,8},{10,11... | collective-permute-start | bytes 589832 | tf_op jit(solution)/shard_map/ppermute | solution.py:83
  13.8 8.5 %collective-permute-start.10 = (bf16[64,1536]{1,0:T(8,128)(2,1)S(1)}, bf16[64,1536]{1,0:T(8,128)(2,1)}, u32[]{:S(2)}, u32[]{:S(2)}) collective-permute-start(bf16[64,1536]{1,0:T(8,128)(2,1)S(1)} %collective-permute-done.3.refs_1_.refs_3_), channel_id=1, source_target_pairs={{0,6},{2,0},{4,2},{6,4},{1,7},{3,1},{5,3},{7,5},{8,14},{10,8},{12,... | collective-permute-start | bytes 589832 | tf_op jit(solution)/shard_map/ppermute | solution.py:74
  13.8 2.0 %copy-start.11 = (bf16[128,1536]{1,0:T(8,128)(2,1)}, bf16[128,1536]{1,0:T(8,128)(2,1)S(1)}, u32[]{:S(2)}) copy-start(bf16[128,1536]{1,0:T(8,128)(2,1)S(1)} %collective-permute-done.refs_1_) | copy-start | bytes 1179652
  13.8 8.4 %collective-permute-start.9 = (bf16[64,1536]{1,0:T(8,128)(2,1)}, bf16[64,1536]{1,0:T(8,128)(2,1)}, u32[]{:S(2)}, u32[]{:S(2)}) collective-permute-start(bf16[64,1536]{1,0:T(8,128)(2,1)} %collective-permute-done.6.refs_4_.refs_6_), channel_id=1, source_target_pairs={{0,2},{2,4},{4,6},{6,0},{1,3},{3,5},{5,7},{7,1},{8,10},{10,12},{12... | collective-permute-start | bytes 589832 | tf_op jit(solution)/shard_map/ppermute | solution.py:74
  19.8 3.0 %collective-permute-start.7 = (bf16[64,1536]{1,0:T(8,128)(2,1)}, bf16[64,1536]{1,0:T(8,128)(2,1)}, u32[]{:S(2)}, u32[]{:S(2)}) collective-permute-start(bf16[64,1536]{1,0:T(8,128)(2,1)} %collective-permute-done.6.refs_4_.refs_6_), channel_id=1, source_target_pairs={{0,1},{1,0},{2,3},{3,2},{4,5},{5,4},{6,7},{7,6},{8,9},{9,8},{10,11... | collective-permute-start | bytes 589832 | tf_op jit(solution)/shard_map/ppermute | solution.py:83
  19.9 2.9 %collective-permute-start.4 = (bf16[64,1536]{1,0:T(8,128)(2,1)}, bf16[64,1536]{1,0:T(8,128)(2,1)}, u32[]{:S(2)}, u32[]{:S(2)}) collective-permute-start(bf16[64,1536]{1,0:T(8,128)(2,1)} %collective-permute-done.2.refs_0_.refs_2_), channel_id=1, source_target_pairs={{0,1},{1,0},{2,3},{3,2},{4,5},{5,4},{6,7},{7,6},{8,9},{9,8},{10,11... | collective-permute-start | bytes 589832 | tf_op jit(solution)/shard_map/ppermute | solution.py:83
  20.4 1.9 %copy-start.14 = (bf16[64,1536]{1,0:T(8,128)(2,1)}, bf16[64,1536]{1,0:T(8,128)(2,1)S(1)}, u32[]{:S(2)}) copy-start(bf16[64,1536]{1,0:T(8,128)(2,1)S(1)} %collective-permute-done.5.refs_3_.refs_5_) | copy-start | bytes 589828
  20.4 2.4 %collective-permute-start.8 = (bf16[64,1536]{1,0:T(8,128)(2,1)}, bf16[64,1536]{1,0:T(8,128)(2,1)}, u32[]{:S(2)}, u32[]{:S(2)}) collective-permute-start(bf16[64,1536]{1,0:T(8,128)(2,1)} %collective-permute-done.1.refs_5_.refs_7_), channel_id=1, source_target_pairs={{0,1},{1,0},{2,3},{3,2},{4,5},{5,4},{6,7},{7,6},{8,9},{9,8},{10,11... | collective-permute-start | bytes 589832 | tf_op jit(solution)/shard_map/ppermute | solution.py:83
  22.3 6.0 %collective-permute-start.11 = (bf16[64,1536]{1,0:T(8,128)(2,1)}, bf16[64,1536]{1,0:T(8,128)(2,1)S(1)}, u32[]{:S(2)}, u32[]{:S(2)}) collective-permute-start(bf16[64,1536]{1,0:T(8,128)(2,1)} %collective-permute-done.9.refs_0_.refs_10_), channel_id=1, source_target_pairs={{0,1},{1,0},{2,3},{3,2},{4,5},{5,4},{6,7},{7,6},{8,9},{9,8},{10,11... | collective-permute-start | bytes 589832 | tf_op jit(solution)/shard_map/ppermute | solution.py:83
  22.3 6.0 %collective-permute-start.12 = (bf16[64,1536]{1,0:T(8,128)(2,1)}, bf16[64,1536]{1,0:T(8,128)(2,1)}, u32[]{:S(2)}, u32[]{:S(2)}) collective-permute-start(bf16[64,1536]{1,0:T(8,128)(2,1)} %collective-permute-done.10.refs_1_.refs_11_), channel_id=1, source_target_pairs={{0,1},{1,0},{2,3},{3,2},{4,5},{5,4},{6,7},{7,6},{8,9},{9,8},{10,11... | collective-permute-start | bytes 589832 | tf_op jit(solution)/shard_map/ppermute | solution.py:83
  28.3 0.7 copy-start.12
  32.9 8.9 %all-to-all-start = ((f32[8,16,128]{2,1,0:T(8,128)}), f32[8,16,128]{2,1,0:T(8,128)S(1)}, u32[]{:S(2)}, u32[]{:S(2)}) async-start(f32[8,16,128]{2,1,0:T(8,128)} %get-tuple-element.70), calls=%async_computation | async-start | bytes 131072 | tf_op jit(solution)/shard_map/all_to_all | solution.py:459
  41.8 0.6 copy-start.15
  49.6 9.5 %collective-permute-start.13 = (bf16[128,1664]{1,0:T(8,128)(2,1)}, bf16[128,1664]{1,0:T(8,128)(2,1)S(1)}, u32[]{:S(2)}, u32[]{:S(2)}) collective-permute-start(bf16[128,1664]{1,0:T(8,128)(2,1)} %get-tuple-element.78), channel_id=1, source_target_pairs={{0,8},{1,57},{8,0},{9,17},{16,24},{17,9},{24,16},{25,33},{32,40},{... | collective-permute-start | bytes 1277960 | tf_op jit(solution)/shard_map/ppermute | solution.py:63
  51.8 11.8 %collective-permute-start.15 = (bf16[128,1664]{1,0:T(8,128)(2,1)}, bf16[128,1664]{1,0:T(8,128)(2,1)}, u32[]{:S(2)}, u32[]{:S(2)}) collective-permute-start(bf16[128,1664]{1,0:T(8,128)(2,1)} %get-tuple-element.85), channel_id=1, source_target_pairs={{0,8},{1,57},{8,0},{9,17},{16,24},{17,9},{24,16},{25,33},{32,40},{... | collective-permute-start | bytes 1277960 | tf_op jit(solution)/shard_map/ppermute | solution.py:63
  51.9 9.3 %copy-start.3 = (f32[128,1536]{1,0:T(8,128)S(1)}, f32[128,1536]{1,0:T(8,128)}, u32[]{:S(2)}) copy-start(f32[128,1536]{1,0:T(8,128)} %get-tuple-element.86.keep) | copy-start | bytes 2359300
  51.9 9.3 %copy-start.7 = (f32[128,128]{1,0:T(8,128)S(1)}, f32[128,128]{1,0:T(8,128)}, u32[]{:S(2)}) copy-start(f32[128,128]{1,0:T(8,128)} %get-tuple-element.87.mass) | copy-start | bytes 196612
  51.9 15.5 %copy-start.5 = (f32[128,1536]{1,0:T(8,128)S(1)}, f32[128,1536]{1,0:T(8,128)}, u32[]{:S(2)}) copy-start(f32[128,1536]{1,0:T(8,128)} %get-tuple-element.83.keep) | copy-start | bytes 2359300
  51.9 15.5 %copy-start.9 = (f32[128,128]{1,0:T(8,128)S(1)}, f32[128,128]{1,0:T(8,128)}, u32[]{:S(2)}) copy-start(f32[128,128]{1,0:T(8,128)} %get-tuple-element.84.mass) | copy-start | bytes 196612
  59.1 13.0 %copy-start.8 = (f32[128,128]{1,0:T(8,128)S(1)}, f32[128,128]{1,0:T(8,128)}, u32[]{:S(2)}) copy-start(f32[128,128]{1,0:T(8,128)} %get-tuple-element.91.mass) | copy-start | bytes 196612
  59.1 14.9 %copy-start.1 = (bf16[1024,1536]{1,0:T(8,128)(2,1)S(1)}, bf16[1024,1536]{1,0:T(8,128)(2,1)}, u32[]{:S(2)}) copy-start(bf16[1024,1536]{1,0:T(8,128)(2,1)} %fine.1) | copy-start | bytes 9437188
  59.1 10.9 %collective-permute-start.14 = (bf16[128,1664]{1,0:T(8,128)(2,1)}, bf16[128,1664]{1,0:T(8,128)(2,1)S(1)}, u32[]{:S(2)}, u32[]{:S(2)}) collective-permute-start(bf16[128,1664]{1,0:T(8,128)(2,1)} %get-tuple-element.81), channel_id=1, source_target_pairs={{0,8},{1,57},{8,0},{9,17},{16,24},{17,9},{24,16},{25,33},{32,40},{... | collective-permute-start | bytes 1277960 | tf_op jit(solution)/shard_map/ppermute | solution.py:63
  61.1 11.0 %collective-permute-start.18 = (bf16[128,1664]{1,0:T(8,128)(2,1)}, bf16[128,1664]{1,0:T(8,128)(2,1)S(1)}, u32[]{:S(2)}, u32[]{:S(2)}) collective-permute-start(bf16[128,1664]{1,0:T(8,128)(2,1)} %get-tuple-element.92), channel_id=1, source_target_pairs={{0,8},{1,57},{8,0},{9,17},{16,24},{17,9},{24,16},{25,33},{32,40},{... | collective-permute-start | bytes 1277960 | tf_op jit(solution)/shard_map/ppermute | solution.py:63
  61.4 5.9 %collective-permute-start.16 = (bf16[64,1664]{1,0:T(8,128)(2,1)S(1)}, bf16[64,1664]{1,0:T(8,128)(2,1)S(1)}, u32[]{:S(2)}, u32[]{:S(2)}) collective-permute-start(bf16[64,1664]{1,0:T(8,128)(2,1)S(1)} %get-tuple-element.89), channel_id=1, source_target_pairs={{0,64},{64,128},{128,192},{192,0},{1,65},{65,129},{129,193},{193,1... | collective-permute-start | bytes 638984 | tf_op jit(solution)/shard_map/ppermute | solution.py:74
  62.8 7.3 %collective-permute-start.19 = (bf16[64,1664]{1,0:T(8,128)(2,1)S(1)}, bf16[64,1664]{1,0:T(8,128)(2,1)S(1)}, u32[]{:S(2)}, u32[]{:S(2)}) collective-permute-start(bf16[64,1664]{1,0:T(8,128)(2,1)S(1)} %get-tuple-element.93), channel_id=1, source_target_pairs={{0,192},{64,0},{128,64},{192,128},{1,193},{65,1},{129,65},{193,129... | collective-permute-start | bytes 638984 | tf_op jit(solution)/shard_map/ppermute | solution.py:74
  68.7 14.5 %collective-permute-start.17 = (bf16[128,1664]{1,0:T(8,128)(2,1)S(1)}, bf16[128,1664]{1,0:T(8,128)(2,1)S(1)}, u32[]{:S(2)}, u32[]{:S(2)}) collective-permute-start(bf16[128,1664]{1,0:T(8,128)(2,1)S(1)} %add_side_step.2), channel_id=1, source_target_pairs={{0,64},{64,128},{128,192},{192,0},{1,65},{65,129},{129,193},{193,1... | collective-permute-start | bytes 1277960 | tf_op jit(solution)/shard_map/ppermute | solution.py:74
  72.1 1.1 copy-start.4
  73.5 10.5 %collective-permute-start.20 = (bf16[128,1664]{1,0:T(8,128)(2,1)S(1)}, bf16[128,1664]{1,0:T(8,128)(2,1)S(1)}, u32[]{:S(2)}, u32[]{:S(2)}) collective-permute-start(bf16[128,1664]{1,0:T(8,128)(2,1)S(1)} %add_side_step.3), channel_id=1, source_target_pairs={{0,192},{64,0},{128,64},{192,128},{1,193},{65,1},{129,65},{193,129... | collective-permute-start | bytes 1277960 | tf_op jit(solution)/shard_map/ppermute | solution.py:74
  77.5 0.7 copy-start.10
  78.1 5.8 %copy-start.2 = (f32[128,1536]{1,0:T(8,128)S(1)}, f32[128,1536]{1,0:T(8,128)}, u32[]{:S(2)}) copy-start(f32[128,1536]{1,0:T(8,128)} %get-tuple-element.79.keep) | copy-start | bytes 2359300
  78.1 5.8 %copy-start.6 = (f32[128,128]{1,0:T(8,128)S(1)}, f32[128,128]{1,0:T(8,128)}, u32[]{:S(2)}) copy-start(f32[128,128]{1,0:T(8,128)} %get-tuple-element.80.mass) | copy-start | bytes 196612
  84.0 3.7 %collective-permute-start.32 = (bf16[4,144,1536]{2,1,0:T(8,128)(2,1)S(1)}, bf16[4,144,1536]{2,1,0:T(8,128)(2,1)S(1)}, u32[]{:S(2)}, u32[]{:S(2)}) collective-permute-start(bf16[4,144,1536]{2,1,0:T(8,128)(2,1)S(1)} %get-tuple-element.106), channel_id=1, source_target_pairs={{0,1},{1,0},{2,3},{3,2},{4,5},{5,4},{6,7},{7,6},{8,9},{9,8},{10,11... | collective-permute-start | bytes 5308424 | tf_op jit(solution)/shard_map/ppermute | solution.py:83
  84.4 6.2 %collective-permute-start.21 = (bf16[64,1664]{1,0:T(8,128)(2,1)S(1)}, bf16[64,1664]{1,0:T(8,128)(2,1)S(1)}, u32[]{:S(2)}, u32[]{:S(2)}) collective-permute-start(bf16[64,1664]{1,0:T(8,128)(2,1)S(1)} %get-tuple-element.102), channel_id=1, source_target_pairs={{0,56},{1,9},{8,16},{9,1},{16,8},{17,25},{24,32},{25,17},{32,24},{... | collective-permute-start | bytes 638984 | tf_op jit(solution)/shard_map/ppermute | solution.py:63
  88.9 30.1 %collective-permute-start.33 = (bf16[264,1536]{1,0:T(8,128)(2,1)S(1)}, bf16[264,1536]{1,0:T(8,128)(2,1)S(1)}, u32[]{:S(2)}, u32[]{:S(2)}) collective-permute-start(bf16[264,1536]{1,0:T(8,128)(2,1)S(1)} %pad_maximum_fusion), channel_id=1, source_target_pairs={{0,2},{1,7},{2,0},{3,5},{4,6},{5,3},{6,4},{7,1},{8,10},{9,15},{10,... | collective-permute-start | bytes 2433032 | tf_op jit(solution)/shard_map/ppermute | solution.py:67
  90.7 11.3 %collective-permute-start.22 = (bf16[64,1664]{1,0:T(8,128)(2,1)S(1)}, bf16[64,1664]{1,0:T(8,128)(2,1)S(1)}, u32[]{:S(2)}, u32[]{:S(2)}) collective-permute-start(bf16[64,1664]{1,0:T(8,128)(2,1)S(1)} %add_half_step.1.own), channel_id=1, source_target_pairs={{0,24},{1,41},{8,48},{9,33},{16,40},{17,57},{24,0},{25,49},{32,56}... | collective-permute-start | bytes 638984 | tf_op jit(solution)/shard_map/ppermute | solution.py:63
  102.2 6.3 %collective-permute-start.23 = (bf16[64,1536]{1,0:T(8,128)(2,1)S(1)}, bf16[64,1536]{1,0:T(8,128)(2,1)S(1)}, u32[]{:S(2)}, u32[]{:S(2)}) collective-permute-start(bf16[64,1536]{1,0:T(8,128)(2,1)S(1)} %add_last_step.1), channel_id=1, source_target_pairs={{0,56},{1,9},{8,16},{9,1},{16,8},{17,25},{24,32},{25,17},{32,24},{... | collective-permute-start | bytes 589832 | tf_op jit(solution)/shard_map/ppermute | solution.py:63
  108.5 17.6 %collective-permute-start.24 = (bf16[128,1536]{1,0:T(8,128)(2,1)S(1)}, bf16[128,1536]{1,0:T(8,128)(2,1)S(1)}, u32[]{:S(2)}, u32[]{:S(2)}) collective-permute-start(bf16[128,1536]{1,0:T(8,128)(2,1)S(1)} %pad_maximum_fusion.2.refs_0_), channel_id=1, source_target_pairs={{0,8},{1,57},{8,0},{9,17},{16,24},{17,9},{24,16},{25,33},{32,40},{... | collective-permute-start | bytes 1179656 | tf_op jit(solution)/shard_map/ppermute | solution.py:63
  116.5 7.8 %collective-permute-start.25 = (bf16[64,1536]{1,0:T(8,128)(2,1)S(1)}, bf16[64,1536]{1,0:T(8,128)(2,1)S(1)}, u32[]{:S(2)}, u32[]{:S(2)}) collective-permute-start(bf16[64,1536]{1,0:T(8,128)(2,1)S(1)} %collective-permute-done.23), channel_id=1, source_target_pairs={{0,64},{1,193},{64,128},{65,1},{128,192},{129,65},{192,0},{193,129... | collective-permute-start | bytes 589832 | tf_op jit(solution)/shard_map/ppermute | solution.py:79
  119.0 7.1 %collective-permute-start.26 = (bf16[64,1536]{1,0:T(8,128)(2,1)S(1)}, bf16[64,1536]{1,0:T(8,128)(2,1)S(1)}, u32[]{:S(2)}, u32[]{:S(2)}) collective-permute-start(bf16[64,1536]{1,0:T(8,128)(2,1)S(1)} %collective-permute-done.23), channel_id=1, source_target_pairs={{0,192},{1,65},{64,0},{65,129},{128,64},{129,193},{192,128},{193,1... | collective-permute-start | bytes 589832 | tf_op jit(solution)/shard_map/ppermute | solution.py:79
  119.8 26.4 %collective-permute-start.34 = (bf16[136,1536]{1,0:T(8,128)(2,1)S(1)}, bf16[136,1536]{1,0:T(8,128)(2,1)S(1)}, u32[]{:S(2)}, u32[]{:S(2)}) collective-permute-start(bf16[136,1536]{1,0:T(8,128)(2,1)S(1)} %pad_maximum_fusion.1), channel_id=1, source_target_pairs={{0,6},{1,3},{2,4},{3,1},{4,2},{5,7},{6,0},{7,5},{8,14},{9,11},{10,... | collective-permute-start | bytes 1253384 | tf_op jit(solution)/shard_map/ppermute | solution.py:67
  126.1 19.9 %collective-permute-start.27 = (bf16[128,1536]{1,0:T(8,128)(2,1)S(1)}, bf16[128,1536]{1,0:T(8,128)(2,1)S(1)}, u32[]{:S(2)}, u32[]{:S(2)}) collective-permute-start(bf16[128,1536]{1,0:T(8,128)(2,1)S(1)} %collective-permute-done.24.refs_1_), channel_id=1, source_target_pairs={{0,192},{1,65},{64,0},{65,129},{128,64},{129,193},{192,128},{193,1... | collective-permute-start | bytes 1179656 | tf_op jit(solution)/shard_map/ppermute | solution.py:79
  126.1 5.7 %collective-permute-start.28 = (bf16[64,1536]{1,0:T(8,128)(2,1)S(1)}, bf16[64,1536]{1,0:T(8,128)(2,1)S(1)}, u32[]{:S(2)}, u32[]{:S(2)}) collective-permute-start(bf16[64,1536]{1,0:T(8,128)(2,1)S(1)} %add_last_step.1), channel_id=1, source_target_pairs={{0,64},{1,193},{64,128},{65,1},{128,192},{129,65},{192,0},{193,129... | collective-permute-start | bytes 589832 | tf_op jit(solution)/shard_map/ppermute | solution.py:79
  128.1 14.1 %collective-permute-start.35 = (bf16[64,1536]{1,0:T(8,128)(2,1)S(1)}, bf16[64,1536]{1,0:T(8,128)(2,1)S(1)}, u32[]{:S(2)}, u32[]{:S(2)}) collective-permute-start(bf16[64,1536]{1,0:T(8,128)(2,1)S(1)} %add_last_step.1), channel_id=1, source_target_pairs={{0,192},{1,65},{64,0},{65,129},{128,64},{129,193},{192,128},{193,1... | collective-permute-start | bytes 589832 | tf_op jit(solution)/shard_map/ppermute | solution.py:79
  131.8 22.1 %collective-permute-start.29 = (bf16[64,1536]{1,0:T(8,128)(2,1)S(1)}, bf16[64,1536]{1,0:T(8,128)(2,1)S(1)}, u32[]{:S(2)}, u32[]{:S(2)}) collective-permute-start(bf16[64,1536]{1,0:T(8,128)(2,1)S(1)} %collective-permute-done.28.refs_4_), channel_id=1, source_target_pairs={{0,64},{1,193},{64,128},{65,1},{128,192},{129,65},{192,0},{193,129... | collective-permute-start | bytes 589832 | tf_op jit(solution)/shard_map/ppermute | solution.py:79
  133.8 20.1 %collective-permute-start.36 = (bf16[128,1536]{1,0:T(8,128)(2,1)S(1)}, bf16[128,1536]{1,0:T(8,128)(2,1)S(1)}, u32[]{:S(2)}, u32[]{:S(2)}) collective-permute-start(bf16[128,1536]{1,0:T(8,128)(2,1)S(1)} %collective-permute-done.24.refs_1_), channel_id=1, source_target_pairs={{0,64},{1,193},{64,128},{65,1},{128,192},{129,65},{192,0},{193,129... | collective-permute-start | bytes 1179656 | tf_op jit(solution)/shard_map/ppermute | solution.py:79
  142.3 11.6 %collective-permute-start.30 = (bf16[64,1536]{1,0:T(8,128)(2,1)S(1)}, bf16[64,1536]{1,0:T(8,128)(2,1)S(1)}, u32[]{:S(2)}, u32[]{:S(2)}) collective-permute-start(bf16[64,1536]{1,0:T(8,128)(2,1)S(1)} %collective-permute-done.25.refs_5_), channel_id=1, source_target_pairs={{0,64},{1,193},{64,128},{65,1},{128,192},{129,65},{192,0},{193,129... | collective-permute-start | bytes 589832 | tf_op jit(solution)/shard_map/ppermute | solution.py:79
  146.0 7.9 %collective-permute-start.31 = (bf16[128,1536]{1,0:T(8,128)(2,1)S(1)}, bf16[128,1536]{1,0:T(8,128)(2,1)S(1)}, u32[]{:S(2)}, u32[]{:S(2)}) collective-permute-start(bf16[128,1536]{1,0:T(8,128)(2,1)S(1)} %collective-permute-done.27.refs_0_), channel_id=1, source_target_pairs={{0,192},{1,65},{64,0},{65,129},{128,64},{129,193},{192,128},{193,1... | collective-permute-start | bytes 1179656 | tf_op jit(solution)/shard_map/ppermute | solution.py:79
